TPU v7x, 32 devices: a whole 2x2x4 slice. The times are simulated.
32 devices in a mesh: gx: 8 (over y, x, core), gy: 4 (over z).
Axes of the slice: x: 2, y: 2, z: 4, core: 2. Of those that a mesh axis runs over, the one named last changes fastest.
Arguments:
- gradient: bfloat16 [256, 256, 512], P(None, 'gx', 'gy'), may hold values from -6 to 6
- vertical: bfloat16 [4, 256, 256], replicated, may hold values from -0.375 to 0.375
- kernel: bfloat16 [64, 64], replicated, may hold values from -0.75 to 0.75
Outputs:
- increment: bfloat16 [256, 256, 512], P(None, 'gx', 'gy')
All inputs are finite; a program needn't handle non-finite values.
Results may differ from a plain program's by a relative error of at most 0.0085.
Values may be sent and summed in bfloat16 or wider, within the bound.
No kernel may reach another device: no remote copies, remote signals or barrier semaphores. Data moves between devices by JAX's collectives and lax.ppermute only.
A program may use at most 64 MiB of HBM per device.

v0:
```python
import jax
import jax.numpy as jnp
from jax import lax
from jax.sharding import PartitionSpec as P


def from_behind(shard, axis, by):
    count = lax.axis_size(axis)
    return lax.ppermute(shard, axis, [(i, (i + by) % count) for i in range(count)])


def shifted(block, axis, distance):
    devices = range(lax.axis_size(axis))
    route = [(i - distance, i) for i in devices if i - distance in devices]
    return lax.ppermute(block, axis, route)


def mixing(matrix, field):
    width = field.shape[0]
    flat = jnp.dot(matrix, field.reshape(width, -1), preferred_element_type=jnp.float32)
    return flat.reshape(field.shape)


def restrict_table(size):
    source = lax.broadcasted_iota(jnp.int32, (size, size // 2), 0)
    target = 2 * lax.broadcasted_iota(jnp.int32, (size, size // 2), 1)
    middle = jnp.where(source == target, 1.0, 0.0)
    sides = jnp.where((source == target + 1) | (source == target - 1), 0.5, 0.0)
    return (middle + sides).astype(jnp.float32)


def apply_table(values, table):
    width, rows, cols = values.shape
    flat = jnp.dot(
        values.reshape(width * rows, cols),
        table,
        precision=lax.Precision.HIGHEST,
        preferred_element_type=jnp.float32,
    )
    return flat.reshape(width, rows, table.shape[1])


def onehot_row(size, where):
    return jnp.where(lax.broadcasted_iota(jnp.int32, (1, 1, size), 2) == where, 1.0, 0.0).astype(
        jnp.float32
    )


def restrict_local(current):
    lower = from_behind(current[:, -1:, :], "gx", 1)
    values = current.astype(jnp.float32)
    before = jnp.concatenate([lower.astype(jnp.float32), values[:, :-1, :]], axis=1)
    half = values[:, 0::2, :] + 0.5 * (before[:, 0::2, :] + values[:, 1::2, :])
    left = shifted(half[:, :, -1:], "gy", 1)
    cols = half.shape[2]
    coarser = apply_table(half, restrict_table(cols)) + 0.5 * left * onehot_row(cols // 2, 0)
    return (coarser / 1.5).astype(jnp.bfloat16)


def prolong_local(carry):
    upper = from_behind(carry[:, :1, :], "gx", -1)
    values = carry.astype(jnp.float32)
    after = jnp.concatenate([values[:, 1:, :], upper.astype(jnp.float32)], axis=1)
    width, rows, cols = values.shape
    along = jnp.stack([values, 0.5 * (values + after)], axis=2).reshape(width, 2 * rows, cols)
    right = shifted(along[:, :, :1].astype(jnp.bfloat16), "gy", -1).astype(jnp.float32)
    spread_table = jnp.transpose(restrict_table(2 * cols))
    return apply_table(along, spread_table) + 0.5 * right * onehot_row(2 * cols, 2 * cols - 1)


def on_device(gradient, vertical, kernel):
    levels = [gradient]
    current = gradient
    for level in range(3):
        current = restrict_local(current)
        levels.append(current)
    coarse = mixing(vertical[3], levels[3]).astype(jnp.bfloat16)
    width, rows, cols = coarse.shape
    offset = lax.axis_index("gy") * cols
    own_kernel = lax.dynamic_slice_in_dim(kernel, offset, cols, 1)
    piece = lax.all_gather(coarse, "gy", axis=2, tiled=True)
    flat = jnp.dot(
        piece.reshape(width * rows, piece.shape[2]), own_kernel, preferred_element_type=jnp.float32
    )
    spread = flat.reshape(jnp.zeros((width, rows, cols), jnp.float32).shape)
    carry = (coarse.astype(jnp.float32) + spread).astype(jnp.bfloat16)
    for level in (2, 1, 0):
        finer = prolong_local(carry)
        carry = (mixing(vertical[level], levels[level]) + finer / 1.5).astype(jnp.bfloat16)
    return carry


def solution(mesh):
    in_specs = (P(None, "gx", "gy"), P(), P())
    out_specs = P(None, "gx", "gy")
    return jax.shard_map(
        on_device, mesh=mesh, in_specs=in_specs, out_specs=out_specs, check_vma=False
    )
```

profile of v0, /device:TPU:0, one launch (start us, length us, event | category | flops | bytes accessed | tf_op | source)
XLA Modules:
  0.0 89.3 jit_solution(7140568633496726595)
XLA Ops:
  0.0 0.0 copy-start
  0.0 3.0 %copy.12 = bf16[256,32,128]{0,2,1:T(8,128)(2,1)S(1)} copy(bf16[256,32,128]{2,1,0:T(8,128)(2,1)} %param.3) | data formatting | bytes 4194304 | tf_op args[0]
  3.0 0.5 collective-permute-start
  3.5 0.5 slice.128
  4.0 0.5 convert_element_type.81
  4.6 3.7 %collective-permute-done = bf16[256,1,128]{0,2,1:T(8,128)(2,1)S(1)} collective-permute-done((bf16[256,1,128]{0,2,1:T(8,128)(2,1)S(1)}, bf16[256,1,128]{0,2,1:T(8,128)(2,1)S(1)}, u32[]{:S(2)}, u32[]{:S(2)}) %collective-permute-start) | collective-permute-done | bytes 65568 | tf_op jit(solution)/shard_map/ppermute | solution.py:9
  8.4 0.4 pad_maximum_fusion
  8.8 0.5 multiply_add_fusion
  9.3 4.2 %collective-permute-start.1 = (f32[256,16,1]{0,2,1:T(1,128)S(1)}, f32[256,16,1]{0,2,1:T(1,128)S(1)}, u32[]{:S(2)}, u32[]{:S(2)}) collective-permute-start(f32[256,16,1]{0,2,1:T(1,128)S(1)} %slice.129), channel_id=1, source_target_pairs={{0,1},{1,2},{2,3},{4,5},{5,6},{6,7},{8,9},{9,10},{10,11},{12,13},{... | collective-permute-start | bytes 49160 | tf_op jit(solution)/shard_map/ppermute | solution.py:15
  13.6 1.4 %collective-permute-done.1 = f32[256,16,1]{0,2,1:T(1,128)S(1)} collective-permute-done((f32[256,16,1]{0,2,1:T(1,128)S(1)}, f32[256,16,1]{0,2,1:T(1,128)S(1)}, u32[]{:S(2)}, u32[]{:S(2)}) %collective-permute-start.1) | collective-permute-done | bytes 16416 | tf_op jit(solution)/shard_map/ppermute | solution.py:15
  15.0 1.4 %fusion.108 = (f32[256,16,64]{0,2,1:T(8,128)S(1)}, bf16[256,16,64]{0,2,1:T(8,128)(2,1)S(1)}) fusion(f32[64]{0:T(128)S(1)} %compare_select_fusion.5, f32[256,16]{0,1:T(8,128)S(1)} %bitcast.125, f32[256,16,128]{0,2,1:T(8,128)S(1)} %multiply_add_fusion, s32[64]{0:T(128)S(1)} %get-tuple-element.10, s32[64]{0:T(128)S(1)} %broadcast_add_fusion.5, ...), kind=kOutput, calls=%fused_computation.160 | convolution fusion | flops 404021248 | bytes 3687424 | tf_op jit(solution)/shard_map/dot_general | solution.py:34
  16.4 0.1 collective-permute-start.2
  16.5 0.1 slice.131
  16.6 4.1 %collective-permute-done.2 = bf16[256,1,64]{0,2,1:T(8,128)(2,1)S(1)} collective-permute-done((bf16[256,1,64]{0,2,1:T(8,128)(2,1)S(1)}, bf16[256,1,64]{0,2,1:T(8,128)(2,1)S(1)}, u32[]{:S(2)}, u32[]{:S(2)}) %collective-permute-start.2) | collective-permute-done | bytes 32800 | tf_op jit(solution)/shard_map/ppermute | solution.py:9
  20.7 0.1 pad_maximum_fusion.2
  20.8 0.0 copy-start.1
  20.9 0.1 multiply_add_fusion.1
  21.0 4.3 %collective-permute-start.3 = (f32[256,8,1]{0,2,1:T(1,128)S(1)}, f32[256,8,1]{0,2,1:T(1,128)S(1)}, u32[]{:S(2)}, u32[]{:S(2)}) collective-permute-start(f32[256,8,1]{0,2,1:T(1,128)S(1)} %slice.132), channel_id=1, source_target_pairs={{0,1},{1,2},{2,3},{4,5},{5,6},{6,7},{8,9},{9,10},{10,11},{12,13},{... | collective-permute-start | bytes 24584 | tf_op jit(solution)/shard_map/ppermute | solution.py:15
  25.3 1.3 %collective-permute-done.3 = f32[256,8,1]{0,2,1:T(1,128)S(1)} collective-permute-done((f32[256,8,1]{0,2,1:T(1,128)S(1)}, f32[256,8,1]{0,2,1:T(1,128)S(1)}, u32[]{:S(2)}, u32[]{:S(2)}) %collective-permute-start.3) | collective-permute-done | bytes 8224 | tf_op jit(solution)/shard_map/ppermute | solution.py:15
  26.7 0.4 fusion.109
  27.1 0.1 collective-permute-start.4
  27.2 4.0 %collective-permute-done.4 = bf16[256,1,32]{0,2,1:T(8,128)(2,1)S(1)} collective-permute-done((bf16[256,1,32]{0,2,1:T(8,128)(2,1)S(1)}, bf16[256,1,32]{0,2,1:T(8,128)(2,1)S(1)}, u32[]{:S(2)}, u32[]{:S(2)}) %collective-permute-start.4) | collective-permute-done | bytes 16416 | tf_op jit(solution)/shard_map/ppermute | solution.py:9
  31.3 4.2 %collective-permute-start.5 = (f32[256,4,1]{0,2,1:T(1,128)S(1)}, f32[256,4,1]{0,2,1:T(1,128)S(1)}, u32[]{:S(2)}, u32[]{:S(2)}) collective-permute-start(f32[256,4,1]{0,2,1:T(1,128)S(1)} %slice.135), channel_id=1, source_target_pairs={{0,1},{1,2},{2,3},{4,5},{5,6},{6,7},{8,9},{9,10},{10,11},{12,13},{... | collective-permute-start | bytes 12296 | tf_op jit(solution)/shard_map/ppermute | solution.py:15
  35.6 0.0 copy-done.1
  35.6 2.3 %copy.36 = bf16[32,8,32,128]{3,1,2,0:T(8,128)(2,1)} copy(bf16[32,8,32,128]{3,2,1,0:T(8,128)(2,1)S(1)} %bitcast.110) | data formatting | bytes 4194304
  37.9 0.0 copy-start.2
  37.9 3.3 %copy.11 = bf16[4096,256]{1,0:T(8,128)(2,1)S(1)} copy(bf16[4096,256]{0,1:T(8,128)(2,1)} %bitcast.111) | data formatting | bytes 4194304 | tf_op jit(solution)/shard_map/dot_general | solution.py:20
  41.2 0.0 collective-permute-done.5
  41.2 0.3 multiply_convert_fusion.2
  41.5 0.0 copy-done.2
  41.5 0.2 convolution_convert_fusion
  41.7 13.6 %all_gather.3 = bf16[256,4,64]{0,2,1:T(8,128)(2,1)S(1)} all-gather(bf16[256,4,16]{0,2,1:T(8,128)(2,1)S(1)} %bitcast.121), channel_id=1, replica_groups=mesh['gx'=8,'gy'=4] {'gy'}, dimensions={2}, use_global_device_ids=true | all-gather | bytes 163840 | tf_op jit(solution)/shard_map/all_gather | solution.py:81
  55.3 0.0 copy-done
  55.3 0.2 fusion.6
  55.5 0.1 collective-permute-start.6
  55.6 1.3 %collective-permute-done.6 = bf16[256,1,16]{0,2,1:T(8,128)(2,1)S(1)} collective-permute-done((bf16[256,1,16]{0,2,1:T(8,128)(2,1)S(1)}, bf16[256,1,16]{0,2,1:T(8,128)(2,1)S(1)}, u32[]{:S(2)}, u32[]{:S(2)}) %collective-permute-start.6) | collective-permute-done | bytes 8224 | tf_op jit(solution)/shard_map/ppermute | solution.py:9
  57.0 1.3 %collective-permute-start.7 = (bf16[256,8,1]{0,2,1:T(2,128)(2,1)S(1)}, bf16[256,8,1]{0,2,1:T(2,128)(2,1)S(1)}, u32[]{:S(2)}, u32[]{:S(2)}) collective-permute-start(bf16[256,8,1]{0,2,1:T(2,128)(2,1)S(1)} %slice.175), channel_id=1, source_target_pairs={{1,0},{2,1},{3,2},{5,4},{6,5},{7,6},{9,8},{10,9},{11,10},{13,12},{... | collective-permute-start | bytes 12296 | tf_op jit(solution)/shard_map/ppermute | solution.py:15
  58.3 0.2 fusion.12
  58.5 4.0 %collective-permute-done.7 = bf16[256,8,1]{0,2,1:T(2,128)(2,1)S(1)} collective-permute-done((bf16[256,8,1]{0,2,1:T(2,128)(2,1)S(1)}, bf16[256,8,1]{0,2,1:T(2,128)(2,1)S(1)}, u32[]{:S(2)}, u32[]{:S(2)}) %collective-permute-start.7) | collective-permute-done | bytes 4128 | tf_op jit(solution)/shard_map/ppermute | solution.py:15
  62.6 0.5 fusion.5
  63.1 1.5 %collective-permute-start.8 = (bf16[256,1,32]{0,2,1:T(8,128)(2,1)S(1)}, bf16[256,1,32]{0,2,1:T(8,128)(2,1)S(1)}, u32[]{:S(2)}, u32[]{:S(2)}) collective-permute-start(bf16[256,1,32]{0,2,1:T(8,128)(2,1)S(1)} %slice.140), channel_id=1, source_target_pairs={{0,28},{4,0},{8,4},{12,8},{16,12},{20,16},{24,20},{28,24},{1,29},{... | collective-permute-start | bytes 49160 | tf_op jit(solution)/shard_map/ppermute | solution.py:9
  64.7 1.4 %collective-permute-done.8 = bf16[256,1,32]{0,2,1:T(8,128)(2,1)S(1)} collective-permute-done((bf16[256,1,32]{0,2,1:T(8,128)(2,1)S(1)}, bf16[256,1,32]{0,2,1:T(8,128)(2,1)S(1)}, u32[]{:S(2)}, u32[]{:S(2)}) %collective-permute-start.8) | collective-permute-done | bytes 16416 | tf_op jit(solution)/shard_map/ppermute | solution.py:9
  66.2 1.3 %collective-permute-start.9 = (bf16[256,16,1]{0,2,1:T(2,128)(2,1)S(1)}, bf16[256,16,1]{0,2,1:T(2,128)(2,1)S(1)}, u32[]{:S(2)}, u32[]{:S(2)}) collective-permute-start(bf16[256,16,1]{0,2,1:T(2,128)(2,1)S(1)} %slice.174), channel_id=1, source_target_pairs={{1,0},{2,1},{3,2},{5,4},{6,5},{7,6},{9,8},{10,9},{11,10},{13,12},{... | collective-permute-start | bytes 24584 | tf_op jit(solution)/shard_map/ppermute | solution.py:15
  67.5 0.3 fusion.14
  67.8 4.0 %collective-permute-done.9 = bf16[256,16,1]{0,2,1:T(2,128)(2,1)S(1)} collective-permute-done((bf16[256,16,1]{0,2,1:T(2,128)(2,1)S(1)}, bf16[256,16,1]{0,2,1:T(2,128)(2,1)S(1)}, u32[]{:S(2)}, u32[]{:S(2)}) %collective-permute-start.9) | collective-permute-done | bytes 8224 | tf_op jit(solution)/shard_map/ppermute | solution.py:15
  71.9 1.2 %fusion.2 = bf16[256,16,64]{0,2,1:T(8,128)(2,1)S(1)} fusion(f32[256,16,64]{0,2,1:T(8,128)S(1)} %bitcast.114, f32[256,16,32]{0,2,1:T(8,128)S(1)} %bitcast.116, f32[64]{0:T(128)S(1)} %compare_select_fusion.1, f32[256,16]{0,1:T(8,128)S(1)} %bitcast.124, s32[32]{0:T(128)S(1)} %get-tuple-element.12, s32[32]{0:T(128)S(1)} %broadcast_add_fusion.3, ...), kind=kOutput, calls=%fused_computation.8 | convolution fusion | flops 101988352 | bytes 2114176 | tf_op jit(solution)/shard_map/dot_general | solution.py:34
  73.1 1.5 %collective-permute-start.10 = (bf16[256,1,64]{0,2,1:T(8,128)(2,1)S(1)}, bf16[256,1,64]{0,2,1:T(8,128)(2,1)S(1)}, u32[]{:S(2)}, u32[]{:S(2)}) collective-permute-start(bf16[256,1,64]{0,2,1:T(8,128)(2,1)S(1)} %slice.143), channel_id=1, source_target_pairs={{0,28},{4,0},{8,4},{12,8},{16,12},{20,16},{24,20},{28,24},{1,29},{... | collective-permute-start | bytes 98312 | tf_op jit(solution)/shard_map/ppermute | solution.py:9
  74.6 0.1 convert_bitcast_fusion
  74.7 0.1 slice.142
  74.8 1.4 %collective-permute-done.10 = bf16[256,1,64]{0,2,1:T(8,128)(2,1)S(1)} collective-permute-done((bf16[256,1,64]{0,2,1:T(8,128)(2,1)S(1)}, bf16[256,1,64]{0,2,1:T(8,128)(2,1)S(1)}, u32[]{:S(2)}, u32[]{:S(2)}) %collective-permute-start.10) | collective-permute-done | bytes 32800 | tf_op jit(solution)/shard_map/ppermute | solution.py:9
  76.2 0.1 fusion.8
  76.3 0.2 pad_maximum_fusion.1
  76.5 0.2 copy.18
  76.8 1.5 %collective-permute-start.11 = (bf16[256,32,1]{0,2,1:T(2,128)(2,1)S(1)}, bf16[256,32,1]{0,2,1:T(2,128)(2,1)S(1)}, u32[]{:S(2)}, u32[]{:S(2)}) collective-permute-start(bf16[256,32,1]{0,2,1:T(2,128)(2,1)S(1)} %slice.173), channel_id=1, source_target_pairs={{1,0},{2,1},{3,2},{5,4},{6,5},{7,6},{9,8},{10,9},{11,10},{13,12},{... | collective-permute-start | bytes 49160 | tf_op jit(solution)/shard_map/ppermute | solution.py:15
  78.3 6.8 %fusion.26 = f32[256,32,128]{2,0,1:T(8,128)S(1)} fusion(f32[256,32,64]{0,2,1:T(8,128)S(1)} %bitcast.109, s32[64]{0:T(128)S(1)} %get-tuple-element.10, s32[64]{0:T(128)S(1)} %broadcast_add_fusion.5, s32[64]{0:T(128)S(1)} %get-tuple-element.9), kind=kOutput, calls=%fused_computation.52 | convolution fusion | flops 805363712 | bytes 6292224 | tf_op jit(solution)/shard_map/dot_general | solution.py:34
  85.1 0.0 collective-permute-done.11
  85.2 1.4 %add_convert_fusion = bf16[256,32,128]{2,0,1:T(8,128)(2,1)S(1)} fusion(f32[256,32,128]{2,0,1:T(8,128)S(1)} %fusion.26, f32[128]{0:T(128)S(1)} %compare_select_fusion, f32[256,32]{0,1:T(8,128)S(1)} %bitcast.123, bf16[32,128,256]{2,1,0:T(8,128)(2,1)S(1)} %bitcast.112, bf16[4,256,256]{2,1,0:T(8,128)(2,1)S(1)} %copy-done.2), kind=kOutput, calls=%fused_computation.1 | convolution fusion | flops 542113792 | bytes 8552960 | tf_op jit(solution)/shard_map/dot_general | solution.py:20
  86.6 2.7 %copy.19 = bf16[256,32,128]{2,1,0:T(8,128)(2,1)} copy(bf16[256,32,128]{2,0,1:T(8,128)(2,1)S(1)} %add_convert_fusion) | data formatting | bytes 4194304 | tf_op jit(solution)/shard_map/convert_element_type | solution.py:89
  (55 shorter events, 0.6 us)
Async XLA Ops:
  0.0 55.3 %copy-start = (bf16[64,64]{1,0:T(8,128)(2,1)S(1)}, bf16[64,64]{1,0:T(8,128)(2,1)}, u32[]{:S(2)}) copy-start(bf16[64,64]{1,0:T(8,128)(2,1)} %param.5) | copy-start | bytes 24580
  3.0 5.3 %collective-permute-start = (bf16[256,1,128]{0,2,1:T(8,128)(2,1)S(1)}, bf16[256,1,128]{0,2,1:T(8,128)(2,1)S(1)}, u32[]{:S(2)}, u32[]{:S(2)}) collective-permute-start(bf16[256,1,128]{0,2,1:T(8,128)(2,1)S(1)} %slice.127), channel_id=1, source_target_pairs={{0,4},{4,8},{8,12},{12,16},{16,20},{20,24},{24,28},{28,0},{1,5},{5... | collective-permute-start | bytes 196616 | tf_op jit(solution)/shard_map/ppermute | solution.py:9
  9.3 5.7 %collective-permute-start.1 = (f32[256,16,1]{0,2,1:T(1,128)S(1)}, f32[256,16,1]{0,2,1:T(1,128)S(1)}, u32[]{:S(2)}, u32[]{:S(2)}) collective-permute-start(f32[256,16,1]{0,2,1:T(1,128)S(1)} %slice.129), channel_id=1, source_target_pairs={{0,1},{1,2},{2,3},{4,5},{5,6},{6,7},{8,9},{9,10},{10,11},{12,13},{... | collective-permute-start | bytes 49160 | tf_op jit(solution)/shard_map/ppermute | solution.py:15
  16.4 4.3 %collective-permute-start.2 = (bf16[256,1,64]{0,2,1:T(8,128)(2,1)S(1)}, bf16[256,1,64]{0,2,1:T(8,128)(2,1)S(1)}, u32[]{:S(2)}, u32[]{:S(2)}) collective-permute-start(bf16[256,1,64]{0,2,1:T(8,128)(2,1)S(1)} %slice.130), channel_id=1, source_target_pairs={{0,4},{4,8},{8,12},{12,16},{16,20},{20,24},{24,28},{28,0},{1,5},{5... | collective-permute-start | bytes 98312 | tf_op jit(solution)/shard_map/ppermute | solution.py:9
  20.8 14.7 %copy-start.1 = (bf16[256,32,128]{2,1,0:T(8,128)(2,1)S(1)}, bf16[256,32,128]{2,1,0:T(8,128)(2,1)}, u32[]{:S(2)}) copy-start(bf16[256,32,128]{2,1,0:T(8,128)(2,1)} %param.3) | copy-start | bytes 6291460
  21.0 5.7 %collective-permute-start.3 = (f32[256,8,1]{0,2,1:T(1,128)S(1)}, f32[256,8,1]{0,2,1:T(1,128)S(1)}, u32[]{:S(2)}, u32[]{:S(2)}) collective-permute-start(f32[256,8,1]{0,2,1:T(1,128)S(1)} %slice.132), channel_id=1, source_target_pairs={{0,1},{1,2},{2,3},{4,5},{5,6},{6,7},{8,9},{9,10},{10,11},{12,13},{... | collective-permute-start | bytes 24584 | tf_op jit(solution)/shard_map/ppermute | solution.py:15
  27.1 4.1 %collective-permute-start.4 = (bf16[256,1,32]{0,2,1:T(8,128)(2,1)S(1)}, bf16[256,1,32]{0,2,1:T(8,128)(2,1)S(1)}, u32[]{:S(2)}, u32[]{:S(2)}) collective-permute-start(bf16[256,1,32]{0,2,1:T(8,128)(2,1)S(1)} %slice.133), channel_id=1, source_target_pairs={{0,4},{4,8},{8,12},{12,16},{16,20},{20,24},{24,28},{28,0},{1,5},{5... | collective-permute-start | bytes 49160 | tf_op jit(solution)/shard_map/ppermute | solution.py:9
  31.3 9.9 %collective-permute-start.5 = (f32[256,4,1]{0,2,1:T(1,128)S(1)}, f32[256,4,1]{0,2,1:T(1,128)S(1)}, u32[]{:S(2)}, u32[]{:S(2)}) collective-permute-start(f32[256,4,1]{0,2,1:T(1,128)S(1)} %slice.135), channel_id=1, source_target_pairs={{0,1},{1,2},{2,3},{4,5},{5,6},{6,7},{8,9},{9,10},{10,11},{12,13},{... | collective-permute-start | bytes 12296 | tf_op jit(solution)/shard_map/ppermute | solution.py:15
  37.9 3.6 %copy-start.2 = (bf16[4,256,256]{2,1,0:T(8,128)(2,1)S(1)}, bf16[4,256,256]{2,1,0:T(8,128)(2,1)}, u32[]{:S(2)}) copy-start(bf16[4,256,256]{2,1,0:T(8,128)(2,1)} %param.4) | copy-start | bytes 1572868
  55.5 1.4 %collective-permute-start.6 = (bf16[256,1,16]{0,2,1:T(8,128)(2,1)S(1)}, bf16[256,1,16]{0,2,1:T(8,128)(2,1)S(1)}, u32[]{:S(2)}, u32[]{:S(2)}) collective-permute-start(bf16[256,1,16]{0,2,1:T(8,128)(2,1)S(1)} %slice.137), channel_id=1, source_target_pairs={{0,28},{4,0},{8,4},{12,8},{16,12},{20,16},{24,20},{28,24},{1,29},{... | collective-permute-start | bytes 24584 | tf_op jit(solution)/shard_map/ppermute | solution.py:9
  57.0 5.5 %collective-permute-start.7 = (bf16[256,8,1]{0,2,1:T(2,128)(2,1)S(1)}, bf16[256,8,1]{0,2,1:T(2,128)(2,1)S(1)}, u32[]{:S(2)}, u32[]{:S(2)}) collective-permute-start(bf16[256,8,1]{0,2,1:T(2,128)(2,1)S(1)} %slice.175), channel_id=1, source_target_pairs={{1,0},{2,1},{3,2},{5,4},{6,5},{7,6},{9,8},{10,9},{11,10},{13,12},{... | collective-permute-start | bytes 12296 | tf_op jit(solution)/shard_map/ppermute | solution.py:15
  63.1 3.0 %collective-permute-start.8 = (bf16[256,1,32]{0,2,1:T(8,128)(2,1)S(1)}, bf16[256,1,32]{0,2,1:T(8,128)(2,1)S(1)}, u32[]{:S(2)}, u32[]{:S(2)}) collective-permute-start(bf16[256,1,32]{0,2,1:T(8,128)(2,1)S(1)} %slice.140), channel_id=1, source_target_pairs={{0,28},{4,0},{8,4},{12,8},{16,12},{20,16},{24,20},{28,24},{1,29},{... | collective-permute-start | bytes 49160 | tf_op jit(solution)/shard_map/ppermute | solution.py:9
  66.2 5.6 %collective-permute-start.9 = (bf16[256,16,1]{0,2,1:T(2,128)(2,1)S(1)}, bf16[256,16,1]{0,2,1:T(2,128)(2,1)S(1)}, u32[]{:S(2)}, u32[]{:S(2)}) collective-permute-start(bf16[256,16,1]{0,2,1:T(2,128)(2,1)S(1)} %slice.174), channel_id=1, source_target_pairs={{1,0},{2,1},{3,2},{5,4},{6,5},{7,6},{9,8},{10,9},{11,10},{13,12},{... | collective-permute-start | bytes 24584 | tf_op jit(solution)/shard_map/ppermute | solution.py:15
  73.1 3.1 %collective-permute-start.10 = (bf16[256,1,64]{0,2,1:T(8,128)(2,1)S(1)}, bf16[256,1,64]{0,2,1:T(8,128)(2,1)S(1)}, u32[]{:S(2)}, u32[]{:S(2)}) collective-permute-start(bf16[256,1,64]{0,2,1:T(8,128)(2,1)S(1)} %slice.143), channel_id=1, source_target_pairs={{0,28},{4,0},{8,4},{12,8},{16,12},{20,16},{24,20},{28,24},{1,29},{... | collective-permute-start | bytes 98312 | tf_op jit(solution)/shard_map/ppermute | solution.py:9
  76.8 8.3 %collective-permute-start.11 = (bf16[256,32,1]{0,2,1:T(2,128)(2,1)S(1)}, bf16[256,32,1]{0,2,1:T(2,128)(2,1)S(1)}, u32[]{:S(2)}, u32[]{:S(2)}) collective-permute-start(bf16[256,32,1]{0,2,1:T(2,128)(2,1)S(1)} %slice.173), channel_id=1, source_target_pairs={{1,0},{2,1},{3,2},{5,4},{6,5},{7,6},{9,8},{10,9},{11,10},{13,12},{... | collective-permute-start | bytes 49160 | tf_op jit(solution)/shard_map/ppermute | solution.py:15
where the time goes:
time: 90.8 us; the launch traced here: 89.3 us
  waiting for transfers between devices  26.7 us (29%)
  starting transfers between devices  20.5 us (23%)
  blocking collectives  13.6 us (15%)
  matrix products  13 us (14%)
  local copies, waits for them, and re-layouts  12.4 us (14%)
  other arithmetic  2.43 us (3%)
    ppermute x6, starting transfers between devices, shifted(): return lax.ppermute(block, axis, route)  16.8 us
    ppermute x6, waiting for transfers between devices, from_behind(): lax.ppermute(shard, axis, [(i, (i + by) % count) for i in range(count)])  16 us
    all_gather x1, blocking collectives, on_device(): piece = lax.all_gather(coarse, 'gy', axis=2, tiled=True)  13.6 us
    ppermute x6, waiting for transfers between devices, shifted(): return lax.ppermute(block, axis, route)  10.8 us
    dot_general x6, matrix products, apply_table(): jnp.dot(values.reshape(width * rows, cols), table, precision=lax.Precisio...  10.6 us
    unnamed x14, local copies, waits for them, and re-layouts  5.34 us
    ppermute x6, starting transfers between devices, from_behind(): lax.ppermute(shard, axis, [(i, (i + by) % count) for i in range(count)])  3.71 us
    dot_general x1, local copies, waits for them, and re-layouts, mixing(): jnp.dot(matrix, field.reshape(width, -1), preferred_element_type=jnp.floa...  3.32 us
  transfers between devices with their start and end apart: 12, of which 10 were waited for; matrix products, arithmetic and copies ran while one was open for 16% of the time, Pallas kernels for 0%

commit v1 on v0

v1 whole, which is shorter than its diff:
```python
import jax
import jax.numpy as jnp
import ml_dtypes
import numpy as np
from jax import lax
from jax.experimental import pallas as pl
from jax.experimental.pallas import tpu as pltpu
from jax.sharding import PartitionSpec as P

BF16 = jnp.bfloat16
F32 = jnp.float32
HALF = 16
VMEM = pltpu.VMEM


def hat(level, fine, cell):
    size = 2**level
    return np.maximum(0.0, 1.0 - np.abs(fine - size * cell) / size)


def weights(level, xs, ys, cell_x, cell_y):
    wx = hat(level, np.asarray(xs)[:, None], np.asarray(cell_x)[None, :])
    wy = hat(level, np.asarray(ys)[:, None], np.asarray(cell_y)[None, :])
    return (wx[:, None, :] * wy[None, :, :]).reshape(len(xs) * len(ys), len(cell_x))


def up16(n):
    return -(-n // 16) * 16


class Plan:
    def __init__(self, rows, cols):
        self.rows, self.cols = rows, cols
        ys = range(cols)
        counts = [(rows >> k, cols >> k) for k in range(4)]
        self.counts = counts
        row_cells = [(k, c) for k in (1, 2, 3) for c in range(counts[k][1] + 1)]
        self.row_cells = row_cells
        self.row_size = up16(len(row_cells))
        assert self.row_size == 128
        n3, m3 = counts[3][0] + 1, counts[3][1] + 1
        self.block = up16(n3 * m3)
        self.edge = (n3 * m3) // 16 * 16
        self.spare = n3 * m3 - self.edge
        level3 = [(3, r, c) for r in range(n3) for c in range(m3)]
        edge = [(k, r) for k in (1, 2) for r in range(counts[k][0] + 1)]
        right = level3 + [(k, r, counts[k][1]) for k, r in edge]
        left = level3 + [(k, r, 0) for k, r in edge]
        self.message = up16(len(right))
        self.edge_size = self.message - self.edge
        cells = []
        for part in (right, left):
            cells += part + [None] * (self.message - len(part))
        self.column_cells = cells

        def table(cells, xs):
            out = np.zeros((len(cells), len(xs) * cols))
            for k in (1, 2, 3):
                where = [i for i, cell in enumerate(cells) if cell is not None and cell[0] == k]
                at = [cells[i] for i in where]
                out[where] = weights(k, xs, ys, [c[1] for c in at], [c[2] for c in at]).T
            return out

        pad = [None] * (self.row_size - len(row_cells))
        lower = [(k, 0, c) for k, c in row_cells] + pad
        upper = [(k, counts[k][0], c) for k, c in row_cells] + pad
        self.send_lower = table(lower, range(0, 8))
        self.send_upper = table(upper, range(rows - 8, rows))
        self.send_column = table(cells, range(rows))
        merge = np.zeros((len(cells), 2 * self.row_size))
        for i, cell in enumerate(cells):
            if cell is None:
                continue
            k, r, c = cell
            if r == 0:
                merge[i, row_cells.index((k, c))] = 1
            if r == counts[k][0]:
                merge[i, self.row_size + row_cells.index((k, c))] = 1
        self.merge = merge
        c1, c2 = counts[1][1], counts[2][1]
        grid = lambda n, m: (np.repeat(np.arange(n), m), np.tile(np.arange(m), n))
        self.to_level1 = weights(1, range(-1, 8), ys, *grid(4, c1))
        self.to_level2 = weights(1, range(counts[1][0]), range(c1), *grid(counts[2][0], c2))
        self.even = weights(1, range(0, 2), ys, *grid(2, c1)).T
        self.odd = weights(1, range(2, 4), ys, *grid(4, c1)).T
        def from_row(xs, ends):
            out = np.zeros((2 * self.row_size, 4 * cols))
            for i, (k, c) in enumerate(row_cells):
                if k < 3 and c < counts[k][1]:
                    out[(k - 1) * self.row_size + i] = weights(k, xs, ys, [ends[k]], [c])[:, 0]
            return out

        self.from_first = from_row(range(0, 4), (0, 0, 0))
        self.from_last = from_row(range(rows - 4, rows), [n for n, _ in counts])
        final = [c for c in level3] + [None] * (self.block - len(level3))
        for k in (1, 2):
            for side in (0, 1):
                part = [None] * self.spare
                for level, r in edge:
                    part.append((k, r, side * counts[k][1]) if level == k else None)
                final += part + [None] * (self.edge_size - len(part))
        self.final_size = len(final)
        self.final = table(final, range(rows))


def const(table):
    return jnp.asarray(np.asarray(table).astype(ml_dtypes.bfloat16))


def in_vmem(x):
    return pltpu.with_memory_space_constraint(x, VMEM)


def dot(a, b):
    return jnp.dot(a, b, preferred_element_type=F32)


def dot_nt(a, b):
    return lax.dot_general(a, b, (((1,), (1,)), ((), ())), preferred_element_type=F32)


def first_kernel(plan, x_ref, lower_ref, upper_ref, flat_ref, a_ref, b_ref, buf, nat, sem):
    rows, cols = plan.rows, plan.cols
    width = x_ref.shape[0]
    parts = rows // HALF
    copies = [
        pltpu.make_async_copy(x_ref.at[:, pl.ds(h * HALF, HALF), :], buf.at[h], sem.at[h])
        for h in range(parts)
    ]
    for copy in copies:
        copy.start()
    even = lax.rem(lax.axis_index("gx"), 2) == 0

    def message(table_ref, start):
        total = None
        for j in range(4):
            lanes = pl.ds((start + 2 * j) * cols, 2 * cols)
            term = dot_nt(table_ref[:, pl.ds(2 * j * cols, 2 * cols)], flat_ref[:, lanes])
            total = term if total is None else total + term
        return total.astype(BF16)

    low = None
    for h in range(parts):
        copies[h].wait()
        nat[h] = buf[h].astype(F32).reshape(width * HALF, cols)
        for x in range(HALF):
            row = nat[h, pl.ds(x, width, stride=HALF), :]
            flat_ref[:, pl.ds((h * HALF + x) * cols, cols)] = row.astype(BF16)
        if h == 0:
            low = message(lower_ref, 0)
    up = message(upper_ref, rows - 8)
    a_ref[...] = jnp.where(even, up, low)
    b_ref[...] = jnp.where(even, low, up)


def column_kernel(plan, flat_ref, table_ref, out_ref):
    total = None
    for j in range(plan.rows // 2):
        lanes = pl.ds(2 * j * plan.cols, 2 * plan.cols)
        term = dot_nt(table_ref[:, lanes], flat_ref[:, lanes])
        total = term if total is None else total + term
    out_ref[...] = total


def merge_kernel(plan, own_ref, a_ref, b_ref, merge_ref, right_ref, left_ref, block_ref):
    even = lax.rem(lax.axis_index("gx"), 2) == 0
    size = plan.row_size
    a, b = a_ref[...], b_ref[...]
    before, after = jnp.where(even, b, a), jnp.where(even, a, b)
    total = own_ref[...] + dot(merge_ref[:, :size], before) + dot(merge_ref[:, size:], after)
    total = total.astype(BF16)
    right_ref[...] = total[: plan.message]
    left_ref[...] = total[plan.message :]
    block_ref[...] = total[: plan.block]


def local_kernel(
    plan, count, flat_ref, v_ref, k_ref, sa_ref, sb_ref, ra_ref, rb_ref, t1_ref, t2_ref, u2_ref, even_ref, odd_ref,
    first_ref, last_ref, base_ref, spread_ref, keep_ref, level1, carry1,
):
    rows, cols = plan.rows, plan.cols
    c1 = plan.counts[1][1]
    n1 = plan.counts[1][0]
    for k in range(rows // 8):
        total = None
        for j in range(4):
            lanes = pl.ds((8 * k + 2 * j) * cols, 2 * cols)
            term = dot(flat_ref[:, lanes], t1_ref[pl.ds((2 * j + 1) * cols, 2 * cols), :])
            total = term if total is None else total + term
        if k > 0:
            total = total + dot(flat_ref[:, pl.ds((8 * k - 1) * cols, cols)], t1_ref[pl.ds(0, cols), :])
        level1[:, pl.ds(4 * k * c1, 4 * c1)] = (total * (1 / 1.5)).astype(BF16)
    level2 = (dot(level1[...], t2_ref[...]) * (1 / 1.5)).astype(BF16)
    mixed2 = (dot(v_ref[2], level2) * (1 / 1.5)).astype(BF16)
    step = 4 * c1
    for k in range(n1 * c1 // step):
        lanes = pl.ds(k * step, step)
        mixed1 = dot(v_ref[1], level1[:, lanes]) + dot(mixed2, u2_ref[:, lanes])
        carry1[:, lanes] = (mixed1 * (1 / 1.5)).astype(BF16)

    even = lax.rem(lax.axis_index("gx"), 2) == 0
    a, b = ra_ref[...], rb_ref[...]
    before, after = jnp.where(even, b, a), jnp.where(even, a, b)
    own = jnp.where(even, sa_ref[...], sb_ref[...])
    after = (after.astype(F32) + own.astype(F32)).astype(BF16)

    def mixed_rows(message):
        one = dot_nt(v_ref[1], message) * (1 / 1.5**2)
        two = dot_nt(v_ref[2], message) * (1 / 1.5**4)
        return jnp.concatenate([one, two], axis=1).astype(BF16)

    first, last = mixed_rows(before), mixed_rows(after)
    pairs = rows // 2
    for i in range(pairs):
        lanes = pl.ds(2 * i * cols, 2 * cols)
        total = dot(v_ref[0], flat_ref[:, lanes])
        if i % 2 == 0:
            total = total + dot(carry1[:, pl.ds(i * c1, 2 * c1)], even_ref[...])
        elif i < pairs - 1:
            total = total + dot(carry1[:, pl.ds((i - 1) * c1, 4 * c1)], odd_ref[...])
        else:
            total = total + dot(carry1[:, pl.ds((i - 1) * c1, 2 * c1)], odd_ref[pl.ds(0, 2 * c1), :])
        if i < 2:
            total = total + dot(first, first_ref[:, pl.ds(2 * i * cols, 2 * cols)])
        if i >= pairs - 2:
            total = total + dot(last, last_ref[:, pl.ds(2 * (i - pairs + 2) * cols, 2 * cols)])
        base_ref[:, lanes] = total

    n3, m3 = plan.counts[3][0] + 1, plan.counts[3][1] + 1
    size = k_ref.shape[0]
    block = plan.block
    z = lax.axis_index("gy")

    def parts(shape, dim):
        index = lax.broadcasted_iota(jnp.int32, shape, dim)
        row = jnp.zeros(shape, jnp.int32)
        for r in range(1, n3 + 1):
            row = row + jnp.where(index >= r * m3, 1, 0)
        return row, index - row * m3

    def one(mask):
        return jnp.where(mask, 1.0, 0.0).astype(BF16)

    row, col = parts((block, size), 0)
    place = lax.broadcasted_iota(jnp.int32, (block, size), 1)
    pick = one((place == z * (m3 - 1) + col) & (row < n3))
    picked = dot_nt(pick, k_ref[...]).astype(BF16)
    target_row, target_col = parts((block, block), 0)
    source_row, source_col = parts((block, block), 1)
    same = (target_row == source_row) & (target_row < n3)
    target = z * (m3 - 1) + target_col
    _, col = parts((size, block), 1)
    place = lax.broadcasted_iota(jnp.int32, (size, block), 0)
    for d in range(count):
        start = lax.rem(z - d + count, count) * (m3 - 1)
        spread = dot(picked, one(place == start + col))
        lanes = pl.ds(d * block, block)
        spread_ref[d] = jnp.where(same, spread, 0.0).astype(BF16)
        keep_ref[d] = one(same & (target == start + source_col) & (target < size))


def last_kernel(plan, count, *refs):
    own_ref, *in_refs = refs[: count]
    v_ref, spread_ref, keep_ref, final_ref, base_ref, out_ref, nat, buf, sem = refs[count:]
    rows, cols = plan.rows, plan.cols
    width = v_ref.shape[1]
    block = plan.block
    z = lax.axis_index("gy")
    carry = None
    for d in range(count):
        level3 = own_ref[:block] if d == 0 else in_refs[d - 1][:block]
        mixed = (dot_nt(level3, v_ref[3]) * (1 / 1.5**3)).astype(BF16)
        term = dot(spread_ref[d], mixed) + dot(keep_ref[d], mixed)
        carry = term if carry is None else carry + term
    carry = carry.astype(BF16).astype(F32) * (1 / 1.5**3)
    left = in_refs[0][plan.edge :]
    right = (in_refs[-1][plan.edge :].astype(F32) + own_ref[plan.edge :].astype(F32)).astype(BF16)
    left = jnp.where(z > 0, left, jnp.zeros_like(left))
    right = jnp.where(z < count - 1, right, jnp.zeros_like(right))
    edges = jnp.concatenate([left, right], axis=0)
    one = dot_nt(edges, v_ref[1]) * (1 / 1.5**2)
    two = dot_nt(edges, v_ref[2]) * (1 / 1.5**4)
    parts = jnp.concatenate([carry, one, two], axis=0).T.astype(BF16)
    copies = []
    for h in range(rows // HALF):
        for x in range(0, HALF, 2):
            lanes = pl.ds((h * HALF + x) * cols, 2 * cols)
            total = base_ref[:, lanes] + dot(parts, final_ref[:, lanes])
            nat[h, pl.ds(x, width, stride=HALF), :] = total[:, :cols]
            nat[h, pl.ds(x + 1, width, stride=HALF), :] = total[:, cols:]
        buf[h] = nat[h].reshape(width, HALF, cols).astype(BF16)
        copy = pltpu.make_async_copy(buf.at[h], out_ref.at[:, pl.ds(h * HALF, HALF), :], sem.at[h])
        copy.start()
        copies.append(copy)
    for copy in copies:
        copy.wait()


LIMIT = 48 * 1024 * 1024


def call(kernel, ins, outs, scratch=(), any_in=(), any_out=(), name=None, cost=None):
    specs = [pl.BlockSpec(memory_space=pl.ANY if i in any_in else VMEM) for i in range(len(ins))]
    out_specs = [pl.BlockSpec(memory_space=pl.ANY if i in any_out else VMEM) for i in range(len(outs))]
    out_shape = [
        jax.ShapeDtypeStruct(s, t) if i in any_out else VMEM(s, t) for i, (s, t) in enumerate(outs)
    ]
    ins = [x if i in any_in else in_vmem(x) for i, x in enumerate(ins)]
    return pl.pallas_call(
        kernel,
        in_specs=specs,
        out_specs=out_specs,
        out_shape=out_shape,
        scratch_shapes=list(scratch),
        compiler_params=pltpu.CompilerParams(vmem_limit_bytes=LIMIT),
        cost_estimate=cost,
        name=name,
    )(*ins)


def solution(mesh):
    across, along = mesh.shape["gx"], mesh.shape["gy"]

    def swap(x, first):
        def partner(i):
            return i ^ 1 if first else (i + 1 if i % 2 else i - 1) % across

        return lax.ppermute(x, "gx", [(i, partner(i)) for i in range(across)])

    def on_device(gradient, vertical, kernel):
        width, rows, cols = gradient.shape
        plan = Plan(rows, cols)
        parts = rows // HALF
        size = rows * cols
        flat, send_a, send_b = call(
            lambda *refs: first_kernel(plan, *refs),
            [gradient, const(plan.send_lower), const(plan.send_upper)],
            [((width, size), BF16), ((plan.row_size, width), BF16), ((plan.row_size, width), BF16)],
            [
                VMEM((parts, width, HALF, cols), BF16),
                VMEM((parts, width * HALF, cols), F32),
                pltpu.SemaphoreType.DMA((parts,)),
            ],
            any_in=(0,),
            name="first",
        )
        recv_a, recv_b = swap(send_a, True), swap(send_b, False)
        cells = 2 * plan.message
        (own,) = call(
            lambda *refs: column_kernel(plan, *refs),
            [flat, const(plan.send_column)],
            [((cells, width), F32)],
            name="columns",
            cost=pl.CostEstimate(flops=2 * cells * width * size, bytes_accessed=4 * 1024 * 1024, transcendentals=0),
        )
        right, left, block = call(
            lambda *refs: merge_kernel(plan, *refs),
            [own, recv_a, recv_b, const(plan.merge)],
            [((plan.message, width), BF16), ((plan.message, width), BF16), ((plan.block, width), BF16)],
            name="merge",
        )
        messages = [block] * (along + 1)
        messages[1], messages[along - 1] = right, left
        arrived = [
            lax.ppermute(messages[d], "gy", [(i, (i + d) % along) for i in range(along)]) for d in range(1, along)
        ]
        base, spread, keep = call(
            lambda *refs: local_kernel(plan, along, *refs),
            [
                flat, vertical, kernel, send_a, send_b, recv_a, recv_b, const(plan.to_level1), const(plan.to_level2),
                const(plan.to_level2.T), const(plan.even), const(plan.odd), const(plan.from_first),
                const(plan.from_last),
            ],
            [
                ((width, size), F32),
                ((along, plan.block, plan.block), BF16),
                ((along, plan.block, plan.block), BF16),
            ],
            [VMEM((width, size // 4), BF16), VMEM((width, size // 4), BF16)],
            name="local",
            cost=pl.CostEstimate(flops=6 * width * width * size, bytes_accessed=8 * 1024 * 1024, transcendentals=0),
        )
        (out,) = call(
            lambda *refs: last_kernel(plan, along, *refs),
            [right, *arrived, vertical, spread, keep, const(plan.final), base],
            [((width, rows, cols), BF16)],
            [
                VMEM((parts, width * HALF, cols), F32),
                VMEM((parts, width, HALF, cols), BF16),
                pltpu.SemaphoreType.DMA((parts,)),
            ],
            any_out=(0,),
            name="last",
        )
        return out

    spec = P(None, "gx", "gy")
    return jax.shard_map(on_device, mesh=mesh, in_specs=(spec, P(), P()), out_specs=spec, check_vma=False)
```

time: 90.8 us -> 25.1 us (0.28); the launches traced: 89.3 us -> 24.9 us
  waiting for transfers between devices: 26.7 us -> 2.35 us
  blocking collectives: 13.6 us -> 0 us
  matrix products: 13 us -> 0 us
  starting transfers between devices: 20.5 us -> 8.97 us
  Pallas kernels: 0 us -> 9.87 us
  local copies, waits for them, and re-layouts: 12.4 us -> 3.56 us
  other arithmetic: 2.43 us -> 0 us
    ppermute x12 -> x5, waiting for transfers between devices: 26.7 us -> 2.35 us  [the longest x3 1.28 us: on_device(): lax.ppermute(messages[d], 'gy', [(i, (i + d) % along) for i in range(alon...]
    all_gather x1 -> x0, blocking collectives: 13.6 us -> none  [on_device(): piece = lax.all_gather(coarse, 'gy', axis=2, tiled=True)]
    dot_general x11 -> x0, matrix products: 13 us -> none  [the longest x6 10.6 us: apply_table(): jnp.dot(values.reshape(width * rows, cols), table, precision=lax.Precisio...]
    ppermute x12 -> x5, starting transfers between devices: 20.5 us -> 8.97 us  [the longest x3 4.9 us: on_device(): lax.ppermute(messages[d], 'gy', [(i, (i + d) % along) for i in range(alon...]
    pallas_call x0 -> x5, Pallas kernels: none -> 9.87 us  [call(): pl.pallas_call(kernel, in_specs=specs, out_specs=out_specs, out_shape=out...]
    dot_general x1 -> x0, local copies, waits for them, and re-layouts: 3.32 us -> none  [mixing(): jnp.dot(matrix, field.reshape(width, -1), preferred_element_type=jnp.floa...]
    convert_element_type x1 -> x0, local copies, waits for them, and re-layouts: 2.67 us -> none  [on_device(): (mixing(vertical[level], levels[level]) + finer / 1.5).astype(jnp.bfloat16)]
    unnamed x14 -> x30, local copies, waits for them, and re-layouts: 5.34 us -> 3.56 us
  transfers between devices with their start and end apart: 12 -> 5, of which waited for: 10 -> 2; matrix products, arithmetic and copies ran while one was open for 16% -> 0% of each run, Pallas kernels for 0% -> 16%
where the time goes in v1:
time: 25.1 us; the launch traced here: 24.9 us
  Pallas kernels  9.87 us (39%)
  starting transfers between devices  8.97 us (36%)
  local copies, waits for them, and re-layouts  3.56 us (14%)
  waiting for transfers between devices  2.35 us (9%)
    pallas_call x5, Pallas kernels, call(): pl.pallas_call(kernel, in_specs=specs, out_specs=out_specs, out_shape=out...  9.87 us
    ppermute x3, starting transfers between devices, on_device(): lax.ppermute(messages[d], 'gy', [(i, (i + d) % along) for i in range(alon...  4.9 us
    ppermute x2, starting transfers between devices, swap(): return lax.ppermute(x, 'gx', [(i, partner(i)) for i in range(across)])  4.07 us
    unnamed x30, local copies, waits for them, and re-layouts  3.56 us
    ppermute x3, waiting for transfers between devices, on_device(): lax.ppermute(messages[d], 'gy', [(i, (i + d) % along) for i in range(alon...  1.28 us
    ppermute x2, waiting for transfers between devices, swap(): return lax.ppermute(x, 'gx', [(i, partner(i)) for i in range(across)])  1.06 us
  transfers between devices with their start and end apart: 5, of which 2 were waited for; matrix products, arithmetic and copies ran while one was open for 0% of the time, Pallas kernels for 16%

profile of v1, /device:TPU:0, one launch (start us, length us, event | category | flops | bytes accessed | tf_op | source)
XLA Modules:
  0.0 24.9 jit_solution(7911880985501866677)
XLA Ops:
  0.0 0.0 copy-start
  0.0 1.6 %copy-done = bf16[256,32,128]{2,1,0:T(8,128)(2,1)S(1)} copy-done((bf16[256,32,128]{2,1,0:T(8,128)(2,1)S(1)}, bf16[256,32,128]{2,1,0:T(8,128)(2,1)}, u32[]{:S(2)}) %copy-start) | copy-done | bytes 2097176
  1.6 0.0 copy-start.4
  1.6 0.9 %copy-done.4 = bf16[128,1024]{1,0:T(8,128)(2,1)S(1)} copy-done((bf16[128,1024]{1,0:T(8,128)(2,1)S(1)}, bf16[128,1024]{1,0:T(8,128)(2,1)}, u32[]{:S(2)}) %copy-start.4) | copy-done | bytes 262168
  2.5 0.0 copy-start.5
  2.5 0.9 %copy-done.5 = bf16[128,1024]{1,0:T(8,128)(2,1)S(1)} copy-done((bf16[128,1024]{1,0:T(8,128)(2,1)S(1)}, bf16[128,1024]{1,0:T(8,128)(2,1)}, u32[]{:S(2)}) %copy-start.5) | copy-done | bytes 262168
  3.5 0.0 copy-start.2
  3.5 2.2 %first.1 = (bf16[256,4096]{1,0:T(8,128)(2,1)S(1)}, bf16[128,256]{1,0:T(8,128)(2,1)S(1)}, bf16[128,256]{1,0:T(8,128)(2,1)S(1)}) custom-call(bf16[256,32,128]{2,1,0:T(8,128)(2,1)S(1)} %copy-done, bf16[128,1024]{1,0:T(8,128)(2,1)S(1)} %copy-done.4, bf16[128,1024]{1,0:T(8,128)(2,1)S(1)} %copy-done.5), custom_call_target="tpu_custom_call" | custom-call | tf_op jit(solution)/shard_map/first/pallas_call | solution.py:309
  5.7 0.0 copy-start.6
  5.7 0.5 %collective-permute-start = (bf16[128,256]{1,0:T(8,128)(2,1)S(1)}, bf16[128,256]{1,0:T(8,128)(2,1)S(1)}, u32[]{:S(2)}, u32[]{:S(2)}) collective-permute-start(bf16[128,256]{1,0:T(8,128)(2,1)S(1)} %get-tuple-element.15.refs_3_), channel_id=1, source_target_pairs={{0,4},{4,0},{8,12},{12,8},{16,20},{20,16},{24,28},{28,24},{1,5},{5... | collective-permute-start | bytes 196616 | tf_op jit(solution)/shard_map/ppermute | solution.py:328
  6.3 3.6 %collective-permute-start.1 = (bf16[128,256]{1,0:T(8,128)(2,1)S(1)}, bf16[128,256]{1,0:T(8,128)(2,1)S(1)}, u32[]{:S(2)}, u32[]{:S(2)}) collective-permute-start(bf16[128,256]{1,0:T(8,128)(2,1)S(1)} %get-tuple-element.16.refs_4_), channel_id=1, source_target_pairs={{0,28},{4,8},{8,4},{12,16},{16,12},{20,24},{24,20},{28,0},{1,29},{... | collective-permute-start | bytes 196616 | tf_op jit(solution)/shard_map/ppermute | solution.py:328
  9.8 0.0 copy-done.2
  9.8 0.0 copy-start.3
  9.8 0.0 copy-start.7
  9.8 0.0 copy-start.8
  9.8 0.0 copy-start.9
  9.8 0.0 copy-start.10
  9.8 0.0 copy-start.11
  9.9 0.0 copy-start.12
  9.9 0.0 copy-start.13
  9.9 0.0 copy-start.14
  9.9 0.8 %columns.1.refs_0_ = f32[224,256]{1,0:T(8,128)S(1)} custom-call(bf16[256,4096]{1,0:T(8,128)(2,1)S(1)} %get-tuple-element.14.refs_0_, bf16[224,4096]{1,0:T(8,128)(2,1)S(1)} %copy-done.2), custom_call_target="tpu_custom_call" | custom-call | flops 469762048 | bytes 4194304 | tf_op jit(solution)/shard_map/columns/pallas_call | solution.py:309
  10.7 0.0 collective-permute-done.refs_1_.refs_5_
  10.7 1.1 %collective-permute-done.1.refs_2_.refs_6_ = bf16[128,256]{1,0:T(8,128)(2,1)S(1)} collective-permute-done((bf16[128,256]{1,0:T(8,128)(2,1)S(1)}, bf16[128,256]{1,0:T(8,128)(2,1)S(1)}, u32[]{:S(2)}, u32[]{:S(2)}) %collective-permute-start.1) | collective-permute-done | bytes 65568 | tf_op jit(solution)/shard_map/ppermute | solution.py:328
  11.8 0.0 copy-done.6
  11.8 0.2 merge.1
  12.0 1.9 %collective-permute-start.2 = (bf16[112,256]{1,0:T(8,128)(2,1)S(1)}, bf16[112,256]{1,0:T(8,128)(2,1)S(1)}, u32[]{:S(2)}, u32[]{:S(2)}) collective-permute-start(bf16[112,256]{1,0:T(8,128)(2,1)S(1)} %get-tuple-element.17.refs_0_), channel_id=1, source_target_pairs={{0,1},{1,2},{2,3},{3,0},{4,5},{5,6},{6,7},{7,4},{8,9},{9,10},{10,1... | collective-permute-start | bytes 172040 | tf_op jit(solution)/shard_map/ppermute | solution.py:365
  13.8 2.1 %collective-permute-start.4 = (bf16[112,256]{1,0:T(8,128)(2,1)S(1)}, bf16[112,256]{1,0:T(8,128)(2,1)S(1)}, u32[]{:S(2)}, u32[]{:S(2)}) collective-permute-start(bf16[112,256]{1,0:T(8,128)(2,1)S(1)} %get-tuple-element.19), channel_id=1, source_target_pairs={{0,3},{1,0},{2,1},{3,2},{4,7},{5,4},{6,5},{7,6},{8,11},{9,8},{10,9... | collective-permute-start | bytes 172040 | tf_op jit(solution)/shard_map/ppermute | solution.py:365
  15.9 0.0 copy-start.1
  15.9 0.9 %collective-permute-start.3 = (bf16[96,256]{1,0:T(8,128)(2,1)S(1)}, bf16[96,256]{1,0:T(8,128)(2,1)S(1)}, u32[]{:S(2)}, u32[]{:S(2)}) collective-permute-start(bf16[96,256]{1,0:T(8,128)(2,1)S(1)} %get-tuple-element.18), channel_id=1, source_target_pairs={{0,2},{1,3},{2,0},{3,1},{4,6},{5,7},{6,4},{7,5},{8,10},{9,11},{10,... | collective-permute-start | bytes 147464 | tf_op jit(solution)/shard_map/ppermute | solution.py:365
  16.9 0.0 copy-done.3
  16.9 0.0 copy-done.7
  16.9 0.0 copy-done.8
  16.9 0.0 copy-done.9
  16.9 0.0 copy-done.10
  16.9 0.0 copy-done.11
  16.9 0.0 copy-done.12
  16.9 0.0 copy-done.13
  16.9 0.0 copy-done.14
  16.9 3.2 %local.1 = (f32[256,4096]{1,0:T(8,128)S(1)}, bf16[4,96,96]{2,1,0:T(8,128)(2,1)S(1)}, bf16[4,96,96]{2,1,0:T(8,128)(2,1)S(1)}) custom-call(bf16[256,4096]{1,0:T(8,128)(2,1)S(1)} %get-tuple-element.14.refs_0_, bf16[4,256,256]{2,1,0:T(8,128)(2,1)S(1)} %copy-done.3, bf16[64,64]{1,0:T(8,128)(2,1)S(1)} %copy-done.7, ...), custom_call_target="tpu_custom_call" | custom-call | flops 1610612736 | bytes 8388608 | tf_op jit(solution)/shard_map/local/pallas_call | solution.py:309
  20.1 1.3 %collective-permute-done.3.refs_2_ = bf16[96,256]{1,0:T(8,128)(2,1)S(1)} collective-permute-done((bf16[96,256]{1,0:T(8,128)(2,1)S(1)}, bf16[96,256]{1,0:T(8,128)(2,1)S(1)}, u32[]{:S(2)}, u32[]{:S(2)}) %collective-permute-start.3) | collective-permute-done | bytes 49184 | tf_op jit(solution)/shard_map/ppermute | solution.py:365
  21.4 0.0 collective-permute-done.2.refs_1_
  21.4 0.0 collective-permute-done.4.refs_3_
  21.4 0.0 copy-done.1
  21.4 3.5 %last.1 = bf16[256,32,128]{2,1,0:T(8,128)(2,1)} custom-call(bf16[112,256]{1,0:T(8,128)(2,1)S(1)} %get-tuple-element.17.refs_0_, bf16[112,256]{1,0:T(8,128)(2,1)S(1)} %collective-permute-done.2.refs_1_, bf16[96,256]{1,0:T(8,128)(2,1)S(1)} %collective-permute-done.3.refs_2_, bf16[112,256]{1,0:T(8,128)(2,1)S(1)} %collective-permute-done.4.refs_3_, ...), custom_call_target="tpu_custom_call" | custom-call | tf_op jit(solution)/shard_map/last/pallas_call | solution.py:309
Async XLA Ops:
  0.0 1.6 %copy-start = (bf16[256,32,128]{2,1,0:T(8,128)(2,1)S(1)}, bf16[256,32,128]{2,1,0:T(8,128)(2,1)}, u32[]{:S(2)}) copy-start(bf16[256,32,128]{2,1,0:T(8,128)(2,1)} %refs_0_.1) | copy-start | bytes 6291460
  1.6 0.9 %copy-start.4 = (bf16[128,1024]{1,0:T(8,128)(2,1)S(1)}, bf16[128,1024]{1,0:T(8,128)(2,1)}, u32[]{:S(2)}) copy-start(bf16[128,1024]{1,0:T(8,128)(2,1)} %constant.24.clone.refs_1_) | copy-start | bytes 786436
  2.5 0.9 %copy-start.5 = (bf16[128,1024]{1,0:T(8,128)(2,1)S(1)}, bf16[128,1024]{1,0:T(8,128)(2,1)}, u32[]{:S(2)}) copy-start(bf16[128,1024]{1,0:T(8,128)(2,1)} %constant.25.clone.refs_2_) | copy-start | bytes 786436
  3.5 6.3 %copy-start.2 = (bf16[224,4096]{1,0:T(8,128)(2,1)S(1)}, bf16[224,4096]{1,0:T(8,128)(2,1)}, u32[]{:S(2)}) copy-start(bf16[224,4096]{1,0:T(8,128)(2,1)} %constant.26.clone.refs_1_) | copy-start | bytes 5505028
  5.7 6.0 %copy-start.6 = (bf16[224,256]{1,0:T(8,128)(2,1)S(1)}, bf16[224,256]{1,0:T(8,128)(2,1)}, u32[]{:S(2)}) copy-start(bf16[224,256]{1,0:T(8,128)(2,1)} %constant.27.clone.refs_3_) | copy-start | bytes 344068
  5.7 5.0 %collective-permute-start = (bf16[128,256]{1,0:T(8,128)(2,1)S(1)}, bf16[128,256]{1,0:T(8,128)(2,1)S(1)}, u32[]{:S(2)}, u32[]{:S(2)}) collective-permute-start(bf16[128,256]{1,0:T(8,128)(2,1)S(1)} %get-tuple-element.15.refs_3_), channel_id=1, source_target_pairs={{0,4},{4,0},{8,12},{12,8},{16,20},{20,16},{24,28},{28,24},{1,5},{5... | collective-permute-start | bytes 196616 | tf_op jit(solution)/shard_map/ppermute | solution.py:328
  6.3 5.5 %collective-permute-start.1 = (bf16[128,256]{1,0:T(8,128)(2,1)S(1)}, bf16[128,256]{1,0:T(8,128)(2,1)S(1)}, u32[]{:S(2)}, u32[]{:S(2)}) collective-permute-start(bf16[128,256]{1,0:T(8,128)(2,1)S(1)} %get-tuple-element.16.refs_4_), channel_id=1, source_target_pairs={{0,28},{4,8},{8,4},{12,16},{16,12},{20,24},{24,20},{28,0},{1,29},{... | collective-permute-start | bytes 196616 | tf_op jit(solution)/shard_map/ppermute | solution.py:328
  9.8 7.1 %copy-start.3 = (bf16[4,256,256]{2,1,0:T(8,128)(2,1)S(1)}, bf16[4,256,256]{2,1,0:T(8,128)(2,1)}, u32[]{:S(2)}) copy-start(bf16[4,256,256]{2,1,0:T(8,128)(2,1)} %refs_4_.1) | copy-start | bytes 1572868
  9.8 7.1 %copy-start.7 = (bf16[64,64]{1,0:T(8,128)(2,1)S(1)}, bf16[64,64]{1,0:T(8,128)(2,1)}, u32[]{:S(2)}) copy-start(bf16[64,64]{1,0:T(8,128)(2,1)} %refs_2_.2) | copy-start | bytes 24580
  9.8 7.1 %copy-start.8 = (bf16[1152,256]{1,0:T(8,128)(2,1)S(1)}, bf16[1152,256]{1,0:T(8,128)(2,1)}, u32[]{:S(2)}) copy-start(bf16[1152,256]{1,0:T(8,128)(2,1)} %constant.28.clone.refs_7_) | copy-start | bytes 1769476
  9.8 7.1 %copy-start.9 = (bf16[1024,256]{1,0:T(8,128)(2,1)S(1)}, bf16[1024,256]{1,0:T(8,128)(2,1)}, u32[]{:S(2)}) copy-start(bf16[1024,256]{1,0:T(8,128)(2,1)} %constant.29.clone.refs_8_) | copy-start | bytes 1572868
  9.8 7.1 %copy-start.10 = (bf16[256,1024]{1,0:T(8,128)(2,1)S(1)}, bf16[256,1024]{1,0:T(8,128)(2,1)}, u32[]{:S(2)}) copy-start(bf16[256,1024]{1,0:T(8,128)(2,1)} %constant.30.clone.refs_9_) | copy-start | bytes 1572868
  9.8 7.1 %copy-start.11 = (bf16[256,512]{1,0:T(8,128)(2,1)S(1)}, bf16[256,512]{1,0:T(8,128)(2,1)}, u32[]{:S(2)}) copy-start(bf16[256,512]{1,0:T(8,128)(2,1)} %constant.33.clone.refs_12_) | copy-start | bytes 786436
  9.9 7.1 %copy-start.12 = (bf16[256,512]{1,0:T(8,128)(2,1)S(1)}, bf16[256,512]{1,0:T(8,128)(2,1)}, u32[]{:S(2)}) copy-start(bf16[256,512]{1,0:T(8,128)(2,1)} %constant.34.clone.refs_13_) | copy-start | bytes 786436
  9.9 7.1 %copy-start.13 = (bf16[256,256]{1,0:T(8,128)(2,1)S(1)}, bf16[256,256]{1,0:T(8,128)(2,1)}, u32[]{:S(2)}) copy-start(bf16[256,256]{1,0:T(8,128)(2,1)} %constant.32.clone.refs_11_) | copy-start | bytes 393220
  9.9 7.1 %copy-start.14 = (bf16[128,256]{1,0:T(8,128)(2,1)S(1)}, bf16[128,256]{1,0:T(8,128)(2,1)}, u32[]{:S(2)}) copy-start(bf16[128,256]{1,0:T(8,128)(2,1)} %constant.31.clone.refs_10_) | copy-start | bytes 196612
  12.0 9.4 %collective-permute-start.2 = (bf16[112,256]{1,0:T(8,128)(2,1)S(1)}, bf16[112,256]{1,0:T(8,128)(2,1)S(1)}, u32[]{:S(2)}, u32[]{:S(2)}) collective-permute-start(bf16[112,256]{1,0:T(8,128)(2,1)S(1)} %get-tuple-element.17.refs_0_), channel_id=1, source_target_pairs={{0,1},{1,2},{2,3},{3,0},{4,5},{5,6},{6,7},{7,4},{8,9},{9,10},{10,1... | collective-permute-start | bytes 172040 | tf_op jit(solution)/shard_map/ppermute | solution.py:365
  13.8 7.6 %collective-permute-start.4 = (bf16[112,256]{1,0:T(8,128)(2,1)S(1)}, bf16[112,256]{1,0:T(8,128)(2,1)S(1)}, u32[]{:S(2)}, u32[]{:S(2)}) collective-permute-start(bf16[112,256]{1,0:T(8,128)(2,1)S(1)} %get-tuple-element.19), channel_id=1, source_target_pairs={{0,3},{1,0},{2,1},{3,2},{4,7},{5,4},{6,5},{7,6},{8,11},{9,8},{10,9... | collective-permute-start | bytes 172040 | tf_op jit(solution)/shard_map/ppermute | solution.py:365
  15.9 5.5 %copy-start.1 = (bf16[224,4096]{1,0:T(8,128)(2,1)S(1)}, bf16[224,4096]{1,0:T(8,128)(2,1)}, u32[]{:S(2)}) copy-start(bf16[224,4096]{1,0:T(8,128)(2,1)} %constant.35.clone.refs_7_) | copy-start | bytes 5505028
  15.9 5.4 %collective-permute-start.3 = (bf16[96,256]{1,0:T(8,128)(2,1)S(1)}, bf16[96,256]{1,0:T(8,128)(2,1)S(1)}, u32[]{:S(2)}, u32[]{:S(2)}) collective-permute-start(bf16[96,256]{1,0:T(8,128)(2,1)S(1)} %get-tuple-element.18), channel_id=1, source_target_pairs={{0,2},{1,3},{2,0},{3,1},{4,6},{5,7},{6,4},{7,5},{8,10},{9,11},{10,... | collective-permute-start | bytes 147464 | tf_op jit(solution)/shard_map/ppermute | solution.py:365

commit v2 on v1

v2 whole, which is shorter than its diff:
```python
import jax
import jax.numpy as jnp
import ml_dtypes
import numpy as np
from jax import lax
from jax.experimental import pallas as pl
from jax.experimental.pallas import tpu as pltpu
from jax.sharding import PartitionSpec as P

BF16 = jnp.bfloat16
F32 = jnp.float32
HALF = 16
CHUNKS = 2
VMEM = pltpu.VMEM


def hat(level, fine, cell):
    size = 2**level
    return np.maximum(0.0, 1.0 - np.abs(fine - size * cell) / size)


def weights(level, xs, ys, cell_x, cell_y):
    wx = hat(level, np.asarray(xs)[:, None], np.asarray(cell_x)[None, :])
    wy = hat(level, np.asarray(ys)[:, None], np.asarray(cell_y)[None, :])
    return (wx[:, None, :] * wy[None, :, :]).reshape(len(xs) * len(ys), len(cell_x))


def up16(n):
    return -(-n // 16) * 16


class Plan:
    def __init__(self, rows, cols):
        self.rows, self.cols = rows, cols
        ys = range(cols)
        counts = [(rows >> k, cols >> k) for k in range(4)]
        self.counts = counts
        row_cells = [(k, c) for k in (1, 2, 3) for c in range(counts[k][1] + 1)]
        self.row_cells = row_cells
        self.row_size = up16(len(row_cells))
        assert self.row_size == 128
        n3, m3 = counts[3][0] + 1, counts[3][1] + 1
        self.cells3 = up16(n3 * m3)
        self.block = -(-n3 * m3 // 128) * 128
        self.edge = (n3 * m3) // 16 * 16
        self.spare = n3 * m3 - self.edge
        level3 = [(3, r, c) for r in range(n3) for c in range(m3)]
        edge = [(k, r) for k in (1, 2) for r in range(counts[k][0] + 1)]
        self.message = up16(len(level3) + len(edge))
        self.edge_size = self.message - self.edge
        cells = []
        for side in (1, 0):
            part = [(k, r, side * counts[k][1]) for k, r in edge]
            part = (level3[self.edge :] if side else [None] * self.spare) + part
            cells += (level3[: self.edge] if side else []) + part + [None] * (self.edge_size - len(part))
        cells += [None] * (-len(cells) % 16)
        self.cells = len(cells)

        def table(cells, xs):
            out = np.zeros((len(cells), len(xs) * cols))
            for k in (1, 2, 3):
                where = [i for i, cell in enumerate(cells) if cell is not None and cell[0] == k]
                at = [cells[i] for i in where]
                out[where] = weights(k, xs, ys, [c[1] for c in at], [c[2] for c in at]).T
            return out

        self.send_column = table(cells, range(rows))
        merge = np.zeros((len(cells), 2 * self.row_size))
        for i, cell in enumerate(cells):
            if cell is None:
                continue
            k, r, c = cell
            if r == 0:
                merge[i, row_cells.index((k, c))] = 1
            if r == counts[k][0]:
                merge[i, self.row_size + row_cells.index((k, c))] = 1
        self.merge = merge
        c1, c2 = counts[1][1], counts[2][1]
        grid = lambda n, m: (np.repeat(np.arange(n), m), np.tile(np.arange(m), n))
        self.to_level1 = weights(1, range(-1, 8), ys, *grid(4, c1))
        self.to_level2 = weights(1, range(counts[1][0]), range(c1), *grid(counts[2][0], c2))
        self.even = weights(1, range(0, 2), ys, *grid(2, c1)).T
        self.odd = weights(1, range(2, 4), ys, *grid(4, c1)).T
        def from_row(xs, ends):
            out = np.zeros((2 * self.row_size, 4 * cols))
            for i, (k, c) in enumerate(row_cells):
                if k < 3 and c < counts[k][1]:
                    out[(k - 1) * self.row_size + i] = weights(k, xs, ys, [ends[k]], [c])[:, 0]
            return out

        self.from_first = from_row(range(0, 4), (0, 0, 0))
        self.from_last = from_row(range(rows - 4, rows), [n for n, _ in counts])
        final = [c for c in level3] + [None] * (self.block - len(level3))
        for k in (1, 2):
            for side in (0, 1):
                part = [None] * self.spare
                for level, r in edge:
                    part.append((k, r, side * counts[k][1]) if level == k else None)
                final += part + [None] * (self.edge_size - len(part))
        self.final_size = len(final)
        self.final = table(final, range(rows))


def const(table):
    return jnp.asarray(np.asarray(table).astype(ml_dtypes.bfloat16))


def dot(a, b):
    return jnp.dot(a, b, preferred_element_type=F32)


def dot_nt(a, b):
    return lax.dot_general(a, b, (((1,), (1,)), ((), ())), preferred_element_type=F32)


def row_table(plan, x, end):
    shape = (plan.row_size, plan.cols)
    cell = lax.broadcasted_iota(jnp.int32, shape, 0)
    y = lax.broadcasted_iota(jnp.int32, shape, 1)
    start, scale, inverse, used = cell * 0, cell * 0, jnp.zeros(shape, F32), 0
    for k in (1, 2, 3):
        stop = used + plan.counts[k][1] + 1
        mine = (cell >= used) & (cell < stop)
        start = jnp.where(mine, used, start)
        scale = jnp.where(mine, 2**k, scale)
        inverse = jnp.where(mine, 0.5**k, inverse)
        used = stop
    along = jnp.maximum(0, scale - jnp.abs(y - scale * (cell - start))).astype(F32)
    across = jnp.maximum(0, scale - abs(x - end)).astype(F32)
    return (along * across * (inverse * inverse)).astype(BF16)


def first_kernel(plan, x_ref, *refs):
    count = (len(refs) - 6) // 2
    fetched = refs[:count]
    raw_ref, flat_ref, a_ref, b_ref = refs[count : count + 4]
    nat, sem = refs[-2:]
    rows, cols = plan.rows, plan.cols
    width = x_ref.shape[0]
    chunk = width // CHUNKS
    last = rows // HALF - 1
    copies = {}
    for h in range(last + 1):
        for c in range(CHUNKS):
            fields = pl.ds(c * chunk, chunk)
            copies[h, c] = pltpu.make_async_copy(
                x_ref.at[fields, pl.ds(h * HALF, HALF), :], raw_ref.at[h, fields], sem.at[h, c]
            )
            copies[h, c].start()
    fetches = [
        pltpu.make_async_copy(src, dst, sem.at[last + 1, i])
        for i, (src, dst) in enumerate(zip(fetched, refs[count + 4 : -2]))
    ]
    for fetch in fetches:
        fetch.start()
    even = lax.rem(lax.axis_index("gx"), 2) == 0

    def message(h, start, end):
        for c in range(CHUNKS):
            copies[h, c].wait()
            fields = pl.ds(c * chunk, chunk)
            nat[c] = raw_ref[h, fields].astype(F32)[:, start : start + 8, :].reshape(chunk * 8, cols)
            for x in range(8):
                lanes = pl.ds(((8 if start else 0) + x) * cols, cols)
                flat_ref[fields, lanes] = nat[c, pl.ds(x, chunk, stride=8), :].astype(BF16)
        total = None
        for x in range(0, 8, 2):
            table = jnp.concatenate([row_table(plan, x, end), row_table(plan, x + 1, end)], axis=1)
            term = dot_nt(table, flat_ref[:, pl.ds(((8 if start else 0) + x) * cols, 2 * cols)])
            total = term if total is None else total + term
        return total.astype(BF16)

    low = message(0, 0, 0)
    up = message(last, HALF - 8, 8)
    a_ref[...] = jnp.where(even, up, low)
    b_ref[...] = jnp.where(even, low, up)
    for h in range(1, last):
        for c in range(CHUNKS):
            copies[h, c].wait()
    for fetch in fetches:
        fetch.wait()


class Rows:
    def __init__(self, plan, ends_ref, inner_ref):
        self.plan, self.ends, self.inner = plan, ends_ref, inner_ref

    def __call__(self, x, count):
        rows, cols = self.plan.rows, self.plan.cols
        if x < 8:
            return self.ends[:, pl.ds(x * cols, count * cols)]
        if x >= rows - 8:
            return self.ends[:, pl.ds((x - rows + 16) * cols, count * cols)]
        return self.inner[:, pl.ds((x - 8) * cols, count * cols)]


def inner_kernel(
    plan, raw_ref, ends_ref, v_ref, column_ref, t1_ref, t2_ref, inner_ref, own_ref, carry1_ref, nat, level1
):
    rows, cols = plan.rows, plan.cols
    width = ends_ref.shape[0]
    for h in range(rows // HALF):
        nat[h] = raw_ref[h].astype(F32).reshape(width * HALF, cols)
        for x in range(HALF):
            at = h * HALF + x
            if 8 <= at < rows - 8:
                row = nat[h, pl.ds(x, width, stride=HALF), :]
                inner_ref[:, pl.ds((at - 8) * cols, cols)] = row.astype(BF16)
    fine = Rows(plan, ends_ref, inner_ref)
    total = None
    for x in range(0, rows, 2):
        term = dot_nt(column_ref[:, pl.ds(x * cols, 2 * cols)], fine(x, 2))
        total = term if total is None else total + term
    own_ref[...] = total
    n1, c1 = plan.counts[1]
    for k in range(rows // 8):
        total = None
        for j in range(4):
            term = dot(fine(8 * k + 2 * j, 2), t1_ref[pl.ds((2 * j + 1) * cols, 2 * cols), :])
            total = term if total is None else total + term
        if k > 0:
            total = total + dot(fine(8 * k - 1, 1), t1_ref[pl.ds(0, cols), :])
        level1[:, pl.ds(4 * k * c1, 4 * c1)] = (total * (1 / 1.5)).astype(BF16)
    level2 = (dot(level1[...], t2_ref[...]) * (1 / 1.5)).astype(BF16)
    mixed2 = (dot(v_ref[2], level2) * (1 / 1.5)).astype(BF16)
    step = 4 * c1
    for k in range(n1 * c1 // step):
        lanes = pl.ds(k * step, step)
        mixed1 = dot(v_ref[1], level1[:, lanes]) + dot_nt(mixed2, t2_ref[lanes, :])
        carry1_ref[:, lanes] = (mixed1 * (1 / 1.5)).astype(BF16)


def merge_kernel(plan, own_ref, a_ref, b_ref, merge_ref, right_ref, left_ref, block_ref):
    even = lax.rem(lax.axis_index("gx"), 2) == 0
    size = plan.row_size
    a, b = a_ref[...], b_ref[...]
    before, after = jnp.where(even, b, a), jnp.where(even, a, b)
    total32 = own_ref[...] + dot(merge_ref[:, :size], before) + dot(merge_ref[:, size:], after)
    total = total32.astype(BF16)
    right_ref[...] = total[: plan.message]
    left_ref[: plan.edge] = total[: plan.edge]
    row = lax.broadcasted_iota(jnp.int32, (plan.edge_size, total.shape[1]), 0)
    tile = jnp.where(row < plan.spare, total32[plan.edge : plan.message], total32[plan.message :])
    left_ref[plan.edge :] = tile.astype(BF16)
    block_ref[...] = total[: plan.cells3]


def local_kernel(
    plan, count, ends_ref, inner_ref, carry1, v_ref, k_ref, sa_ref, sb_ref, ra_ref, rb_ref, even_ref, odd_ref,
    first_ref, last_ref, base_ref, spread_ref,
):
    rows, cols = plan.rows, plan.cols
    n1, c1 = plan.counts[1]
    fine = Rows(plan, ends_ref, inner_ref)

    even = lax.rem(lax.axis_index("gx"), 2) == 0
    a, b = ra_ref[...], rb_ref[...]
    before, after = jnp.where(even, b, a), jnp.where(even, a, b)
    own = jnp.where(even, sa_ref[...], sb_ref[...])
    after = (after.astype(F32) + own.astype(F32)).astype(BF16)

    def mixed_rows(message):
        one = dot_nt(v_ref[1], message) * (1 / 1.5**2)
        two = dot_nt(v_ref[2], message) * (1 / 1.5**4)
        return jnp.concatenate([one, two], axis=1).astype(BF16)

    first, last = mixed_rows(before), mixed_rows(after)
    pairs = rows // 2
    for i in range(pairs):
        lanes = pl.ds(2 * i * cols, 2 * cols)
        total = dot(v_ref[0], fine(2 * i, 2))
        if i % 2 == 0:
            total = total + dot(carry1[:, pl.ds(i * c1, 2 * c1)], even_ref[...])
        elif i < pairs - 1:
            total = total + dot(carry1[:, pl.ds((i - 1) * c1, 4 * c1)], odd_ref[...])
        else:
            total = total + dot(carry1[:, pl.ds((i - 1) * c1, 2 * c1)], odd_ref[pl.ds(0, 2 * c1), :])
        if i < 2:
            total = total + dot(first, first_ref[:, pl.ds(2 * i * cols, 2 * cols)])
        if i >= pairs - 2:
            total = total + dot(last, last_ref[:, pl.ds(2 * (i - pairs + 2) * cols, 2 * cols)])
        base_ref[:, lanes] = total

    n3, m3 = plan.counts[3][0] + 1, plan.counts[3][1] + 1
    size = k_ref.shape[0]
    block, cells3 = plan.block, plan.cells3
    z = lax.axis_index("gy")

    def parts(shape, dim):
        index = lax.broadcasted_iota(jnp.int32, shape, dim)
        row = jnp.zeros(shape, jnp.int32)
        for r in range(1, n3 + 1):
            row = row + jnp.where(index >= r * m3, 1, 0)
        return row, index - row * m3

    def one(mask):
        return jnp.where(mask, 1.0, 0.0).astype(BF16)

    row, col = parts((size, block), 1)
    place = lax.broadcasted_iota(jnp.int32, (size, block), 0)
    picked = dot(k_ref[...], one((place == z * (m3 - 1) + col) & (row < n3))).astype(BF16)
    source_row, source_col = parts((cells3, block), 0)
    target_row, target_col = parts((cells3, block), 1)
    same = (target_row == source_row) & (target_row < n3)
    target = z * (m3 - 1) + target_col
    _, col = parts((cells3, size), 0)
    place = lax.broadcasted_iota(jnp.int32, (cells3, size), 1)
    for d in range(count):
        start = lax.rem(z - d + count, count) * (m3 - 1)
        spread = jnp.where(same, dot(one(place == start + col), picked), 0.0).astype(BF16)
        keep = one(same & (target == start + source_col) & (target < size))
        spread_ref[pl.ds(d * cells3, cells3), :block] = spread
        spread_ref[pl.ds(d * cells3, cells3), block:] = keep


def last_kernel(plan, count, *refs):
    own_ref, *in_refs = refs[:count]
    v_ref, spread_ref, final_ref, base_ref, out_ref, nat, buf, sem = refs[count:]
    rows, cols = plan.rows, plan.cols
    width = v_ref.shape[1]
    block = plan.block
    z = lax.axis_index("gy")
    level3 = jnp.concatenate([own_ref[: plan.cells3]] + [ref[: plan.cells3] for ref in in_refs], axis=0)
    mixed = (dot_nt(v_ref[3], level3) * (1 / 1.5**3)).astype(BF16)
    carry = dot(mixed, spread_ref[...])
    carry = (carry[:, :block] + carry[:, block:]) * (1 / 1.5**3)
    left = in_refs[0][plan.edge :]
    right = (in_refs[-1][plan.edge :].astype(F32) + own_ref[plan.edge :].astype(F32)).astype(BF16)
    left = jnp.where(z > 0, left, jnp.zeros_like(left))
    right = jnp.where(z < count - 1, right, jnp.zeros_like(right))
    edges = jnp.concatenate([left, right], axis=0)
    one = dot_nt(v_ref[1], edges) * (1 / 1.5**2)
    two = dot_nt(v_ref[2], edges) * (1 / 1.5**4)
    parts = jnp.concatenate([carry, one, two], axis=1).astype(BF16)
    copies = []
    for h in range(rows // HALF):
        for x in range(0, HALF, 2):
            lanes = pl.ds((h * HALF + x) * cols, 2 * cols)
            total = base_ref[:, lanes] + dot(parts, final_ref[:, lanes])
            nat[h, pl.ds(x, width, stride=HALF), :] = total[:, :cols]
            nat[h, pl.ds(x + 1, width, stride=HALF), :] = total[:, cols:]
        buf[h] = nat[h].reshape(width, HALF, cols).astype(BF16)
        copy = pltpu.make_async_copy(buf.at[h], out_ref.at[:, pl.ds(h * HALF, HALF), :], sem.at[h])
        copy.start()
        copies.append(copy)
    for copy in copies:
        copy.wait()


LIMIT = 14 * 1024 * 1024


def call(kernel, ins, outs, scratch=(), hbm=(), any_out=(), name=None, cost=None):
    specs = [pl.BlockSpec(memory_space=pl.ANY if i in hbm else VMEM) for i in range(len(ins))]
    out_specs = [pl.BlockSpec(memory_space=pl.ANY if i in any_out else VMEM) for i in range(len(outs))]
    out_shape = [
        jax.ShapeDtypeStruct(s, t) if i in any_out else VMEM(s, t) for i, (s, t) in enumerate(outs)
    ]
    ins = [pltpu.with_memory_space_constraint(x, pltpu.HBM if i in hbm else VMEM) for i, x in enumerate(ins)]
    return pl.pallas_call(
        kernel,
        in_specs=specs,
        out_specs=out_specs,
        out_shape=out_shape,
        scratch_shapes=list(scratch),
        compiler_params=pltpu.CompilerParams(vmem_limit_bytes=LIMIT),
        cost_estimate=cost,
        name=name,
    )(*ins)


def solution(mesh):
    across, along = mesh.shape["gx"], mesh.shape["gy"]

    def swap(x, first):
        def partner(i):
            return i ^ 1 if first else (i + 1 if i % 2 else i - 1) % across

        return lax.ppermute(x, "gx", [(i, partner(i)) for i in range(across)])

    def on_device(gradient, vertical, kernel):
        width, rows, cols = gradient.shape
        plan = Plan(rows, cols)
        parts = rows // HALF
        size = rows * cols
        row_message = ((plan.row_size, width), BF16)
        fetched = [vertical, const(plan.send_column), const(plan.to_level1), const(plan.to_level2)]
        raw, ends, send_a, send_b, vertical, column, to_level1, to_level2 = call(
            lambda *refs: first_kernel(plan, *refs),
            [gradient, *fetched],
            [((parts, width, HALF, cols), BF16), ((width, 16 * cols), BF16), row_message, row_message]
            + [(x.shape, x.dtype) for x in fetched],
            [VMEM((CHUNKS, width // CHUNKS * 8, cols), F32), pltpu.SemaphoreType.DMA((parts + 1, max(CHUNKS, 4)))],
            hbm=range(5),
            name="first",
        )
        recv_a, recv_b = swap(send_a, True), swap(send_b, False)
        cells = plan.cells
        inner, own, carry1 = call(
            lambda *refs: inner_kernel(plan, *refs),
            [
                raw, ends, vertical, column, to_level1, to_level2,
            ],
            [((width, size - 16 * cols), BF16), ((cells, width), F32), ((width, size // 4), BF16)],
            [VMEM((parts, width * HALF, cols), F32), VMEM((width, size // 4), BF16)],
            name="inner",
            cost=pl.CostEstimate(flops=3 * cells * width * size, bytes_accessed=4 * 1024 * 1024, transcendentals=0),
        )
        right, left, block = call(
            lambda *refs: merge_kernel(plan, *refs),
            [own, recv_a, recv_b, const(plan.merge)],
            [((plan.message, width), BF16), ((plan.message, width), BF16), ((plan.cells3, width), BF16)],
            name="merge",
        )
        messages = [block] * (along + 1)
        messages[1], messages[along - 1] = right, left
        arrived = [
            lax.ppermute(messages[d], "gy", [(i, (i + d) % along) for i in range(along)]) for d in range(1, along)
        ]
        base, spread = call(
            lambda *refs: local_kernel(plan, along, *refs),
            [
                ends, inner, carry1, vertical, kernel, send_a, send_b, recv_a, recv_b, const(plan.even),
                const(plan.odd), const(plan.from_first), const(plan.from_last),
            ],
            [((width, size), F32), ((along * plan.cells3, 2 * plan.block), BF16)],
            name="local",
            cost=pl.CostEstimate(flops=4 * width * width * size, bytes_accessed=8 * 1024 * 1024, transcendentals=0),
        )
        (out,) = call(
            lambda *refs: last_kernel(plan, along, *refs),
            [right, *arrived, vertical, spread, const(plan.final), base],
            [((width, rows, cols), BF16)],
            [
                VMEM((parts, width * HALF, cols), F32),
                VMEM((parts, width, HALF, cols), BF16),
                pltpu.SemaphoreType.DMA((parts,)),
            ],
            any_out=(0,),
            name="last",
        )
        return out

    spec = P(None, "gx", "gy")
    return jax.shard_map(on_device, mesh=mesh, in_specs=(spec, P(), P()), out_specs=spec, check_vma=False)
```

time: 25.1 us -> 21.9 us (0.87)
  local copies, waits for them, and re-layouts: 3.56 us -> 0.03 us
  waiting for transfers between devices: 2.35 us -> 2.69 us
    unnamed x30 -> x14, local copies, waits for them, and re-layouts: 3.56 us -> 0.03 us
    ppermute x3, waiting for transfers between devices: 1.28 us -> 2.69 us  [on_device(): lax.ppermute(messages[d], 'gy', [(i, (i + d) % along) for i in range(alon...]
    ppermute x2, waiting for transfers between devices: 1.06 us -> 0.01 us  [swap(): return lax.ppermute(x, 'gx', [(i, partner(i)) for i in range(across)])]
    pallas_call x5, Pallas kernels: 9.87 us -> 10.1 us  [call(): pl.pallas_call(kernel, in_specs=specs, out_specs=out_specs, out_shape=out...]
  transfers between devices with their start and end apart: 5 -> 5, of which waited for: 2 -> 1; matrix products, arithmetic and copies ran while one was open for 0% -> 0% of each run, Pallas kernels for 16% -> 20%
where the time goes in v2:
time: 21.9 us; the launch traced here: 21.7 us
  Pallas kernels  10.1 us (46%)
  starting transfers between devices  8.74 us (40%)
  waiting for transfers between devices  2.69 us (12%)
    pallas_call x5, Pallas kernels, call(): pl.pallas_call(kernel, in_specs=specs, out_specs=out_specs, out_shape=out...  10.1 us
    ppermute x3, starting transfers between devices, on_device(): lax.ppermute(messages[d], 'gy', [(i, (i + d) % along) for i in range(alon...  4.66 us
    ppermute x2, starting transfers between devices, swap(): return lax.ppermute(x, 'gx', [(i, partner(i)) for i in range(across)])  4.07 us
    ppermute x3, waiting for transfers between devices, on_device(): lax.ppermute(messages[d], 'gy', [(i, (i + d) % along) for i in range(alon...  2.69 us
  transfers between devices with their start and end apart: 5, of which 1 were waited for; matrix products, arithmetic and copies ran while one was open for 0% of the time, Pallas kernels for 20%

profile of v2, /device:TPU:0, one launch (start us, length us, event | category | flops | bytes accessed | tf_op | source)
XLA Modules:
  0.0 21.7 jit_solution(14562908269872287455)
XLA Ops:
  0.0 2.5 %first.1 = (bf16[2,256,16,128]{3,2,1,0:T(8,128)(2,1)S(1)}, bf16[256,2048]{1,0:T(8,128)(2,1)S(1)}, bf16[128,256]{1,0:T(8,128)(2,1)S(1)}, bf16[128,256]{1,0:T(8,12...) custom-call(bf16[256,32,128]{2,1,0:T(8,128)(2,1)} %refs_0_.1, ...), custom_call_target="tpu_custom_call" | custom-call | tf_op jit(solution)/shard_map/first/pallas_call | solution.py:360
  2.5 0.5 %collective-permute-start = (bf16[128,256]{1,0:T(8,128)(2,1)S(1)}, bf16[128,256]{1,0:T(8,128)(2,1)S(1)}, u32[]{:S(2)}, u32[]{:S(2)}) collective-permute-start(bf16[128,256]{1,0:T(8,128)(2,1)S(1)} %get-tuple-element.28.refs_5_), channel_id=1, source_target_pairs={{0,4},{4,0},{8,12},{12,8},{16,20},{20,16},{24,28},{28,24},{1,5},{5... | collective-permute-start | bytes 196616 | tf_op jit(solution)/shard_map/ppermute | solution.py:379
  3.0 3.6 %collective-permute-start.1 = (bf16[128,256]{1,0:T(8,128)(2,1)S(1)}, bf16[128,256]{1,0:T(8,128)(2,1)S(1)}, u32[]{:S(2)}, u32[]{:S(2)}) collective-permute-start(bf16[128,256]{1,0:T(8,128)(2,1)S(1)} %get-tuple-element.29.refs_6_), channel_id=1, source_target_pairs={{0,28},{4,8},{8,4},{12,16},{16,12},{20,24},{24,20},{28,0},{1,29},{... | collective-permute-start | bytes 196616 | tf_op jit(solution)/shard_map/ppermute | solution.py:379
  6.6 0.0 copy-start.4
  6.6 0.0 copy-start.1
  6.6 0.0 copy-start.2
  6.6 0.0 copy-start.3
  6.6 0.0 copy-start.5
  6.6 0.0 copy-start.6
  6.6 2.6 %inner.1 = (bf16[256,2048]{1,0:T(8,128)(2,1)S(1)}, f32[144,256]{1,0:T(8,128)S(1)}, bf16[256,1024]{1,0:T(8,128)(2,1)S(1)}) custom-call(bf16[2,256,16,128]{3,2,1,0:T(8,128)(2,1)S(1)} %get-tuple-element.21.refs_0_, bf16[256,2048]{1,0:T(8,128)(2,1)S(1)} %get-tuple-element.22.refs_1_.refs_0_, bf16[4,256,256]{2,1,0:T(8,128)(2,1)S(1)} %get-tuple-element.23.refs_2_.refs_3_.refs_4_, ...), custom_call_target="tpu_custom_call" | custom-call | flops 452984832 | bytes 4194304 | tf_op jit(solution)/shard_map/inner/pallas_call | solution.py:360
  9.2 0.0 collective-permute-done.refs_1_.refs_7_
  9.2 0.0 collective-permute-done.1.refs_2_.refs_8_
  9.3 0.0 copy-done.4
  9.3 0.2 merge.1
  9.5 0.0 copy-start
  9.5 1.6 %collective-permute-start.2 = (bf16[112,256]{1,0:T(8,128)(2,1)S(1)}, bf16[112,256]{1,0:T(8,128)(2,1)S(1)}, u32[]{:S(2)}, u32[]{:S(2)}) collective-permute-start(bf16[112,256]{1,0:T(8,128)(2,1)S(1)} %get-tuple-element.30.refs_0_), channel_id=1, source_target_pairs={{0,1},{1,2},{2,3},{3,0},{4,5},{5,6},{6,7},{7,4},{8,9},{9,10},{10,1... | collective-permute-start | bytes 172040 | tf_op jit(solution)/shard_map/ppermute | solution.py:418
  11.1 2.2 %collective-permute-start.4 = (bf16[112,256]{1,0:T(8,128)(2,1)S(1)}, bf16[112,256]{1,0:T(8,128)(2,1)S(1)}, u32[]{:S(2)}, u32[]{:S(2)}) collective-permute-start(bf16[112,256]{1,0:T(8,128)(2,1)S(1)} %get-tuple-element.32), channel_id=1, source_target_pairs={{0,3},{1,0},{2,1},{3,2},{4,7},{5,4},{6,5},{7,6},{8,11},{9,8},{10,9... | collective-permute-start | bytes 172040 | tf_op jit(solution)/shard_map/ppermute | solution.py:418
  13.4 0.8 %collective-permute-start.3 = (bf16[96,256]{1,0:T(8,128)(2,1)S(1)}, bf16[96,256]{1,0:T(8,128)(2,1)S(1)}, u32[]{:S(2)}, u32[]{:S(2)}) collective-permute-start(bf16[96,256]{1,0:T(8,128)(2,1)S(1)} %get-tuple-element.31), channel_id=1, source_target_pairs={{0,2},{1,3},{2,0},{3,1},{4,6},{5,7},{6,4},{7,5},{8,10},{9,11},{10,... | collective-permute-start | bytes 147464 | tf_op jit(solution)/shard_map/ppermute | solution.py:418
  14.1 0.0 copy-done.1
  14.1 0.0 copy-done.2
  14.1 0.0 copy-done.3
  14.2 0.0 copy-done.5
  14.2 0.0 copy-done.6
  14.2 1.7 %local.1 = (f32[256,4096]{1,0:T(8,128)S(1)}, bf16[384,256]{1,0:T(8,128)(2,1)S(1)}) custom-call(bf16[256,2048]{1,0:T(8,128)(2,1)S(1)} %get-tuple-element.22.refs_1_.refs_0_, bf16[256,2048]{1,0:T(8,128)(2,1)S(1)} %get-tuple-element.33.refs_1_, bf16[256,1024]{1,0:T(8,128)(2,1)S(1)} %get-tuple-element.34.refs_2_, ...), custom_call_target="tpu_custom_call" | custom-call | flops 1073741824 | bytes 8388608 | tf_op jit(solution)/shard_map/local/pallas_call | solution.py:360
  15.9 2.7 %collective-permute-done.3.refs_2_ = bf16[96,256]{1,0:T(8,128)(2,1)S(1)} collective-permute-done((bf16[96,256]{1,0:T(8,128)(2,1)S(1)}, bf16[96,256]{1,0:T(8,128)(2,1)S(1)}, u32[]{:S(2)}, u32[]{:S(2)}) %collective-permute-start.3) | collective-permute-done | bytes 49184 | tf_op jit(solution)/shard_map/ppermute | solution.py:418
  18.6 0.0 collective-permute-done.2.refs_1_
  18.6 0.0 collective-permute-done.4.refs_3_
  18.6 0.0 copy-done
  18.6 3.1 %last.1 = bf16[256,32,128]{2,1,0:T(8,128)(2,1)} custom-call(bf16[112,256]{1,0:T(8,128)(2,1)S(1)} %get-tuple-element.30.refs_0_, bf16[112,256]{1,0:T(8,128)(2,1)S(1)} %collective-permute-done.2.refs_1_, bf16[96,256]{1,0:T(8,128)(2,1)S(1)} %collective-permute-done.3.refs_2_, bf16[112,256]{1,0:T(8,128)(2,1)S(1)} %collective-permute-done.4.refs_3_, ...), custom_call_target="tpu_custom_call" | custom-call | tf_op jit(solution)/shard_map/last/pallas_call | solution.py:360
Async XLA Ops:
  2.5 6.8 %collective-permute-start = (bf16[128,256]{1,0:T(8,128)(2,1)S(1)}, bf16[128,256]{1,0:T(8,128)(2,1)S(1)}, u32[]{:S(2)}, u32[]{:S(2)}) collective-permute-start(bf16[128,256]{1,0:T(8,128)(2,1)S(1)} %get-tuple-element.28.refs_5_), channel_id=1, source_target_pairs={{0,4},{4,0},{8,12},{12,8},{16,20},{20,16},{24,28},{28,24},{1,5},{5... | collective-permute-start | bytes 196616 | tf_op jit(solution)/shard_map/ppermute | solution.py:379
  3.0 6.3 %collective-permute-start.1 = (bf16[128,256]{1,0:T(8,128)(2,1)S(1)}, bf16[128,256]{1,0:T(8,128)(2,1)S(1)}, u32[]{:S(2)}, u32[]{:S(2)}) collective-permute-start(bf16[128,256]{1,0:T(8,128)(2,1)S(1)} %get-tuple-element.29.refs_6_), channel_id=1, source_target_pairs={{0,28},{4,8},{8,4},{12,16},{16,12},{20,24},{24,20},{28,0},{1,29},{... | collective-permute-start | bytes 196616 | tf_op jit(solution)/shard_map/ppermute | solution.py:379
  6.6 2.7 %copy-start.4 = (bf16[144,256]{1,0:T(8,128)(2,1)S(1)}, bf16[144,256]{1,0:T(8,128)(2,1)}, u32[]{:S(2)}) copy-start(bf16[144,256]{1,0:T(8,128)(2,1)} %constant.21.clone.refs_3_) | copy-start | bytes 221188
  6.6 7.6 %copy-start.1 = (bf16[256,512]{1,0:T(8,128)(2,1)S(1)}, bf16[256,512]{1,0:T(8,128)(2,1)}, u32[]{:S(2)}) copy-start(bf16[256,512]{1,0:T(8,128)(2,1)} %constant.24.clone.refs_11_) | copy-start | bytes 786436
  6.6 7.6 %copy-start.2 = (bf16[256,512]{1,0:T(8,128)(2,1)S(1)}, bf16[256,512]{1,0:T(8,128)(2,1)}, u32[]{:S(2)}) copy-start(bf16[256,512]{1,0:T(8,128)(2,1)} %constant.25.clone.refs_12_) | copy-start | bytes 786436
  6.6 7.6 %copy-start.3 = (bf16[256,256]{1,0:T(8,128)(2,1)S(1)}, bf16[256,256]{1,0:T(8,128)(2,1)}, u32[]{:S(2)}) copy-start(bf16[256,256]{1,0:T(8,128)(2,1)} %constant.23.clone.refs_10_) | copy-start | bytes 393220
  6.6 7.6 %copy-start.5 = (bf16[128,256]{1,0:T(8,128)(2,1)S(1)}, bf16[128,256]{1,0:T(8,128)(2,1)}, u32[]{:S(2)}) copy-start(bf16[128,256]{1,0:T(8,128)(2,1)} %constant.22.clone.refs_9_) | copy-start | bytes 196612
  6.6 7.6 %copy-start.6 = (bf16[64,64]{1,0:T(8,128)(2,1)S(1)}, bf16[64,64]{1,0:T(8,128)(2,1)}, u32[]{:S(2)}) copy-start(bf16[64,64]{1,0:T(8,128)(2,1)} %refs_4_.2) | copy-start | bytes 24580
  9.5 9.1 %copy-start = (bf16[256,4096]{1,0:T(8,128)(2,1)S(1)}, bf16[256,4096]{1,0:T(8,128)(2,1)}, u32[]{:S(2)}) copy-start(bf16[256,4096]{1,0:T(8,128)(2,1)} %constant.26.clone.refs_6_) | copy-start | bytes 6291460
  9.5 9.1 %collective-permute-start.2 = (bf16[112,256]{1,0:T(8,128)(2,1)S(1)}, bf16[112,256]{1,0:T(8,128)(2,1)S(1)}, u32[]{:S(2)}, u32[]{:S(2)}) collective-permute-start(bf16[112,256]{1,0:T(8,128)(2,1)S(1)} %get-tuple-element.30.refs_0_), channel_id=1, source_target_pairs={{0,1},{1,2},{2,3},{3,0},{4,5},{5,6},{6,7},{7,4},{8,9},{9,10},{10,1... | collective-permute-start | bytes 172040 | tf_op jit(solution)/shard_map/ppermute | solution.py:418
  11.1 7.5 %collective-permute-start.4 = (bf16[112,256]{1,0:T(8,128)(2,1)S(1)}, bf16[112,256]{1,0:T(8,128)(2,1)S(1)}, u32[]{:S(2)}, u32[]{:S(2)}) collective-permute-start(bf16[112,256]{1,0:T(8,128)(2,1)S(1)} %get-tuple-element.32), channel_id=1, source_target_pairs={{0,3},{1,0},{2,1},{3,2},{4,7},{5,4},{6,5},{7,6},{8,11},{9,8},{10,9... | collective-permute-start | bytes 172040 | tf_op jit(solution)/shard_map/ppermute | solution.py:418
  13.4 5.2 %collective-permute-start.3 = (bf16[96,256]{1,0:T(8,128)(2,1)S(1)}, bf16[96,256]{1,0:T(8,128)(2,1)S(1)}, u32[]{:S(2)}, u32[]{:S(2)}) collective-permute-start(bf16[96,256]{1,0:T(8,128)(2,1)S(1)} %get-tuple-element.31), channel_id=1, source_target_pairs={{0,2},{1,3},{2,0},{3,1},{4,6},{5,7},{6,4},{7,5},{8,10},{9,11},{10,... | collective-permute-start | bytes 147464 | tf_op jit(solution)/shard_map/ppermute | solution.py:418

commit v3 on v2

--- a/solution.py
+++ b/solution.py
@@ -9,8 +9,7 @@
 
 BF16 = jnp.bfloat16
 F32 = jnp.float32
-HALF = 16
-CHUNKS = 2
+PART = 8
 VMEM = pltpu.VMEM
 
 
@@ -64,7 +63,7 @@
                 out[where] = weights(k, xs, ys, [c[1] for c in at], [c[2] for c in at]).T
             return out
 
-        self.send_column = table(cells, range(rows))
+        self.cell_list = cells
         merge = np.zeros((len(cells), 2 * self.row_size))
         for i, cell in enumerate(cells):
             if cell is None:
@@ -75,10 +74,8 @@
             if r == counts[k][0]:
                 merge[i, self.row_size + row_cells.index((k, c))] = 1
         self.merge = merge
-        c1, c2 = counts[1][1], counts[2][1]
+        c1 = counts[1][1]
         grid = lambda n, m: (np.repeat(np.arange(n), m), np.tile(np.arange(m), n))
-        self.to_level1 = weights(1, range(-1, 8), ys, *grid(4, c1))
-        self.to_level2 = weights(1, range(counts[1][0]), range(c1), *grid(counts[2][0], c2))
         self.even = weights(1, range(0, 2), ys, *grid(2, c1)).T
         self.odd = weights(1, range(2, 4), ys, *grid(4, c1)).T
         def from_row(xs, ends):
@@ -113,72 +110,105 @@
     return lax.dot_general(a, b, (((1,), (1,)), ((), ())), preferred_element_type=F32)
 
 
-def row_table(plan, x, end):
-    shape = (plan.row_size, plan.cols)
-    cell = lax.broadcasted_iota(jnp.int32, shape, 0)
-    y = lax.broadcasted_iota(jnp.int32, shape, 1)
-    start, scale, inverse, used = cell * 0, cell * 0, jnp.zeros(shape, F32), 0
-    for k in (1, 2, 3):
-        stop = used + plan.counts[k][1] + 1
-        mine = (cell >= used) & (cell < stop)
-        start = jnp.where(mine, used, start)
-        scale = jnp.where(mine, 2**k, scale)
-        inverse = jnp.where(mine, 0.5**k, inverse)
-        used = stop
-    along = jnp.maximum(0, scale - jnp.abs(y - scale * (cell - start))).astype(F32)
-    across = jnp.maximum(0, scale - abs(x - end)).astype(F32)
-    return (along * across * (inverse * inverse)).astype(BF16)
-
-
-def first_kernel(plan, x_ref, *refs):
-    count = (len(refs) - 6) // 2
-    fetched = refs[:count]
-    raw_ref, flat_ref, a_ref, b_ref = refs[count : count + 4]
-    nat, sem = refs[-2:]
+def ramp(size, offset):
+    return jnp.maximum(0, size - jnp.abs(offset))
+
+
+def cell_tables(cells, shape):
+    index = lax.broadcasted_iota(jnp.int32, shape, 0)
+    width, first, second = index * 0, index * 0, index * 0
+    at = 0
+    while at < len(cells):
+        if cells[at] is None:
+            at += 1
+            continue
+        k, r, c = cells[at]
+        stop = at + 1
+        step = None
+        while stop < len(cells) and cells[stop] is not None and cells[stop][0] == k:
+            move = (cells[stop][1] - cells[stop - 1][1], cells[stop][2] - cells[stop - 1][2])
+            if step is None and move in ((0, 1), (1, 0)):
+                step = move
+            if move != step:
+                break
+            stop += 1
+        step = step or (0, 0)
+        mine = (index >= at) & (index < stop)
+        width = jnp.where(mine, 2**k, width)
+        first = jnp.where(mine, r + step[0] * (index - at), first)
+        second = jnp.where(mine, c + step[1] * (index - at), second)
+        at = stop
+    return width, first, second
+
+
+def split(index, size, count):
+    high = index * 0
+    for i in range(1, count):
+        high = high + jnp.where(index >= i * size, 1, 0)
+    return high, index - high * size
+
+
+def first_kernel(plan, x_ref, v_in_ref, raw_ref, ends_ref, a_ref, b_ref, v_ref, column_ref, t1_ref, t2_ref, nat, sem):
     rows, cols = plan.rows, plan.cols
     width = x_ref.shape[0]
-    chunk = width // CHUNKS
-    last = rows // HALF - 1
-    copies = {}
-    for h in range(last + 1):
-        for c in range(CHUNKS):
-            fields = pl.ds(c * chunk, chunk)
-            copies[h, c] = pltpu.make_async_copy(
-                x_ref.at[fields, pl.ds(h * HALF, HALF), :], raw_ref.at[h, fields], sem.at[h, c]
-            )
-            copies[h, c].start()
-    fetches = [
-        pltpu.make_async_copy(src, dst, sem.at[last + 1, i])
-        for i, (src, dst) in enumerate(zip(fetched, refs[count + 4 : -2]))
+    last = rows // PART - 1
+    copies = [
+        pltpu.make_async_copy(x_ref.at[:, pl.ds(h * PART, PART), :], raw_ref.at[h], sem.at[h]) for h in range(last + 1)
     ]
-    for fetch in fetches:
-        fetch.start()
+    order = [copies[0], copies[last], *copies[1:last], pltpu.make_async_copy(v_in_ref, v_ref, sem.at[last + 1])]
+    for copy in order:
+        copy.start()
     even = lax.rem(lax.axis_index("gx"), 2) == 0
 
-    def message(h, start, end):
-        for c in range(CHUNKS):
-            copies[h, c].wait()
-            fields = pl.ds(c * chunk, chunk)
-            nat[c] = raw_ref[h, fields].astype(F32)[:, start : start + 8, :].reshape(chunk * 8, cols)
-            for x in range(8):
-                lanes = pl.ds(((8 if start else 0) + x) * cols, cols)
-                flat_ref[fields, lanes] = nat[c, pl.ds(x, chunk, stride=8), :].astype(BF16)
+    shape = (plan.cells, cols)
+    size, first, second = cell_tables(plan.cell_list, shape)
+    y = lax.broadcasted_iota(jnp.int32, shape, 1)
+    inverse = jnp.where(size == 2, 0.25, jnp.where(size == 4, 0.0625, 0.015625))
+    along = ramp(size, y - size * second).astype(F32) * inverse
+    size, start = size.astype(F32), (size * first).astype(F32)
+    for x in range(rows):
+        column_ref[:, pl.ds(x * cols, cols)] = (ramp(size, start - x) * along).astype(BF16)
+    n1, c1 = plan.counts[1]
+    n2, c2 = plan.counts[2]
+    shape = (cols, 4 * c1)
+    i, c = split(lax.broadcasted_iota(jnp.int32, shape, 1), c1, 4)
+    along = ramp(2, lax.broadcasted_iota(jnp.int32, shape, 0) - 2 * c).astype(F32) * 0.25
+    i = 2 * i[:1]
+    for x in range(9):
+        t1_ref[pl.ds(x * cols, cols), :] = (ramp(2, i - (x - 1)).astype(F32) * along).astype(BF16)
+    shape = (c1, n2 * c2)
+    i, c = split(lax.broadcasted_iota(jnp.int32, shape, 1), c2, n2)
+    along = ramp(2, lax.broadcasted_iota(jnp.int32, shape, 0) - 2 * c).astype(F32) * 0.25
+    i = 2 * i[:1]
+    for x in range(n1):
+        t2_ref[pl.ds(x * c1, c1), :] = (ramp(2, i - x).astype(F32) * along).astype(BF16)
+    shape = (plan.row_size, cols)
+    cells = [(k, 0, c) for k, c in plan.row_cells]
+    size, _, second = cell_tables(cells, shape)
+    y = lax.broadcasted_iota(jnp.int32, shape, 1)
+    inverse = jnp.where(size == 2, 0.25, jnp.where(size == 4, 0.0625, 0.015625))
+    along = ramp(size, y - size * second).astype(F32) * inverse
+    size = size.astype(F32)
+
+    def message(h, place, end):
+        copies[h].wait()
+        nat[place] = raw_ref[h].astype(F32).reshape(width * PART, cols)
+        for x in range(PART):
+            row = nat[place, pl.ds(x, width, stride=PART), :]
+            ends_ref[:, pl.ds((place * PART + x) * cols, cols)] = row.astype(BF16)
         total = None
-        for x in range(0, 8, 2):
-            table = jnp.concatenate([row_table(plan, x, end), row_table(plan, x + 1, end)], axis=1)
-            term = dot_nt(table, flat_ref[:, pl.ds(((8 if start else 0) + x) * cols, 2 * cols)])
+        for x in range(0, PART, 2):
+            table = [(ramp(size, size * 0 + (end - x - i)) * along).astype(BF16) for i in range(2)]
+            term = dot_nt(jnp.concatenate(table, axis=1), ends_ref[:, pl.ds((place * PART + x) * cols, 2 * cols)])
             total = term if total is None else total + term
         return total.astype(BF16)
 
     low = message(0, 0, 0)
-    up = message(last, HALF - 8, 8)
+    up = message(last, 1, PART)
     a_ref[...] = jnp.where(even, up, low)
     b_ref[...] = jnp.where(even, low, up)
-    for h in range(1, last):
-        for c in range(CHUNKS):
-            copies[h, c].wait()
-    for fetch in fetches:
-        fetch.wait()
+    for copy in order[2:]:
+        copy.wait()
 
 
 class Rows:
@@ -199,13 +229,11 @@
 ):
     rows, cols = plan.rows, plan.cols
     width = ends_ref.shape[0]
-    for h in range(rows // HALF):
-        nat[h] = raw_ref[h].astype(F32).reshape(width * HALF, cols)
-        for x in range(HALF):
-            at = h * HALF + x
-            if 8 <= at < rows - 8:
-                row = nat[h, pl.ds(x, width, stride=HALF), :]
-                inner_ref[:, pl.ds((at - 8) * cols, cols)] = row.astype(BF16)
+    for h in range(1, rows // PART - 1):
+        nat[h - 1] = raw_ref[h].astype(F32).reshape(width * PART, cols)
+        for x in range(PART):
+            row = nat[h - 1, pl.ds(x, width, stride=PART), :]
+            inner_ref[:, pl.ds(((h - 1) * PART + x) * cols, cols)] = row.astype(BF16)
     fine = Rows(plan, ends_ref, inner_ref)
     total = None
     for x in range(0, rows, 2):
@@ -333,14 +361,14 @@
     two = dot_nt(v_ref[2], edges) * (1 / 1.5**4)
     parts = jnp.concatenate([carry, one, two], axis=1).astype(BF16)
     copies = []
-    for h in range(rows // HALF):
-        for x in range(0, HALF, 2):
-            lanes = pl.ds((h * HALF + x) * cols, 2 * cols)
+    for h in range(rows // PART):
+        for x in range(0, PART, 2):
+            lanes = pl.ds((h * PART + x) * cols, 2 * cols)
             total = base_ref[:, lanes] + dot(parts, final_ref[:, lanes])
-            nat[h, pl.ds(x, width, stride=HALF), :] = total[:, :cols]
-            nat[h, pl.ds(x + 1, width, stride=HALF), :] = total[:, cols:]
-        buf[h] = nat[h].reshape(width, HALF, cols).astype(BF16)
-        copy = pltpu.make_async_copy(buf.at[h], out_ref.at[:, pl.ds(h * HALF, HALF), :], sem.at[h])
+            nat[h, pl.ds(x, width, stride=PART), :] = total[:, :cols]
+            nat[h, pl.ds(x + 1, width, stride=PART), :] = total[:, cols:]
+        buf[h] = nat[h].reshape(width, PART, cols).astype(BF16)
+        copy = pltpu.make_async_copy(buf.at[h], out_ref.at[:, pl.ds(h * PART, PART), :], sem.at[h])
         copy.start()
         copies.append(copy)
     for copy in copies:
@@ -381,28 +409,32 @@
     def on_device(gradient, vertical, kernel):
         width, rows, cols = gradient.shape
         plan = Plan(rows, cols)
-        parts = rows // HALF
+        parts = rows // PART
+        n1, c1 = plan.counts[1]
+        n2, c2 = plan.counts[2]
         size = rows * cols
         row_message = ((plan.row_size, width), BF16)
-        fetched = [vertical, const(plan.send_column), const(plan.to_level1), const(plan.to_level2)]
+        cells = plan.cells
         raw, ends, send_a, send_b, vertical, column, to_level1, to_level2 = call(
             lambda *refs: first_kernel(plan, *refs),
-            [gradient, *fetched],
-            [((parts, width, HALF, cols), BF16), ((width, 16 * cols), BF16), row_message, row_message]
-            + [(x.shape, x.dtype) for x in fetched],
-            [VMEM((CHUNKS, width // CHUNKS * 8, cols), F32), pltpu.SemaphoreType.DMA((parts + 1, max(CHUNKS, 4)))],
-            hbm=range(5),
+            [gradient, vertical],
+            [
+                ((parts, width, PART, cols), BF16), ((width, 2 * PART * cols), BF16), row_message, row_message,
+                (vertical.shape, BF16), ((cells, size), BF16), ((9 * cols, 4 * c1), BF16), ((n1 * c1, n2 * c2), BF16),
+            ],
+            [VMEM((2, width * PART, cols), F32), pltpu.SemaphoreType.DMA((parts + 1,))],
+            hbm=(0, 1),
             name="first",
         )
-        recv_a, recv_b = swap(send_a, True), swap(send_b, False)
-        cells = plan.cells
+        recv_b = swap(send_b, False)
+        recv_a = swap(send_a, True)
         inner, own, carry1 = call(
             lambda *refs: inner_kernel(plan, *refs),
             [
                 raw, ends, vertical, column, to_level1, to_level2,
             ],
             [((width, size - 16 * cols), BF16), ((cells, width), F32), ((width, size // 4), BF16)],
-            [VMEM((parts, width * HALF, cols), F32), VMEM((width, size // 4), BF16)],
+            [VMEM((parts - 2, width * PART, cols), F32), VMEM((width, size // 4), BF16)],
             name="inner",
             cost=pl.CostEstimate(flops=3 * cells * width * size, bytes_accessed=4 * 1024 * 1024, transcendentals=0),
         )
@@ -432,8 +464,8 @@
             [right, *arrived, vertical, spread, const(plan.final), base],
             [((width, rows, cols), BF16)],
             [
-                VMEM((parts, width * HALF, cols), F32),
-                VMEM((parts, width, HALF, cols), BF16),
+                VMEM((parts, width * PART, cols), F32),
+                VMEM((parts, width, PART, cols), BF16),
                 pltpu.SemaphoreType.DMA((parts,)),
             ],
             any_out=(0,),

time: 21.9 us -> 20.4 us (0.932)
  Pallas kernels: 10.1 us -> 8.76 us
    pallas_call x5, Pallas kernels: 10.1 us -> 8.76 us  [call(): pl.pallas_call(kernel, in_specs=specs, out_specs=out_specs, out_shape=out...]
where the time goes in v3:
time: 20.4 us; the launch traced here: 20.3 us
  Pallas kernels  8.76 us (43%)
  starting transfers between devices  8.74 us (43%)
  waiting for transfers between devices  2.64 us (13%)
    pallas_call x5, Pallas kernels, call(): pl.pallas_call(kernel, in_specs=specs, out_specs=out_specs, out_shape=out...  8.76 us
    ppermute x3, starting transfers between devices, on_device(): lax.ppermute(messages[d], 'gy', [(i, (i + d) % along) for i in range(alon...  4.67 us
    ppermute x2, starting transfers between devices, swap(): return lax.ppermute(x, 'gx', [(i, partner(i)) for i in range(across)])  4.07 us
    ppermute x3, waiting for transfers between devices, on_device(): lax.ppermute(messages[d], 'gy', [(i, (i + d) % along) for i in range(alon...  2.63 us
  transfers between devices with their start and end apart: 5, of which 1 were waited for; matrix products, arithmetic and copies ran while one was open for 0% of the time, Pallas kernels for 20%

profile of v3, /device:TPU:0, one launch (start us, length us, event | category | flops | bytes accessed | tf_op | source)
XLA Modules:
  0.0 20.3 jit_solution(12638946758204680979)
XLA Ops:
  0.0 2.1 %first.1 = (bf16[4,256,8,128]{3,2,1,0:T(8,128)(2,1)S(1)}, bf16[256,2048]{1,0:T(8,128)(2,1)S(1)}, bf16[128,256]{1,0:T(8,128)(2,1)S(1)}, bf16[128,256]{1,0:T(8,128...) custom-call(bf16[256,32,128]{2,1,0:T(8,128)(2,1)} %refs_0_.1, ...), custom_call_target="tpu_custom_call" | custom-call | tf_op jit(solution)/shard_map/first/pallas_call | solution.py:388
  2.1 0.5 %collective-permute-start = (bf16[128,256]{1,0:T(8,128)(2,1)S(1)}, bf16[128,256]{1,0:T(8,128)(2,1)S(1)}, u32[]{:S(2)}, u32[]{:S(2)}) collective-permute-start(bf16[128,256]{1,0:T(8,128)(2,1)S(1)} %get-tuple-element.28.refs_5_), channel_id=1, source_target_pairs={{0,4},{4,0},{8,12},{12,8},{16,20},{20,16},{24,28},{28,24},{1,5},{5... | collective-permute-start | bytes 196616 | tf_op jit(solution)/shard_map/ppermute | solution.py:407
  2.7 3.6 %collective-permute-start.1 = (bf16[128,256]{1,0:T(8,128)(2,1)S(1)}, bf16[128,256]{1,0:T(8,128)(2,1)S(1)}, u32[]{:S(2)}, u32[]{:S(2)}) collective-permute-start(bf16[128,256]{1,0:T(8,128)(2,1)S(1)} %get-tuple-element.29.refs_6_), channel_id=1, source_target_pairs={{0,28},{4,8},{8,4},{12,16},{16,12},{20,24},{24,20},{28,0},{1,29},{... | collective-permute-start | bytes 196616 | tf_op jit(solution)/shard_map/ppermute | solution.py:407
  6.2 0.0 copy-start.4
  6.2 0.0 copy-start.1
  6.2 0.0 copy-start.2
  6.2 0.0 copy-start.3
  6.2 0.0 copy-start.5
  6.2 0.0 copy-start.6
  6.3 2.3 %inner.1 = (bf16[256,2048]{1,0:T(8,128)(2,1)S(1)}, f32[144,256]{1,0:T(8,128)S(1)}, bf16[256,1024]{1,0:T(8,128)(2,1)S(1)}) custom-call(bf16[4,256,8,128]{3,2,1,0:T(8,128)(2,1)S(1)} %get-tuple-element.21.refs_0_, bf16[256,2048]{1,0:T(8,128)(2,1)S(1)} %get-tuple-element.22.refs_1_.refs_0_, bf16[4,256,256]{2,1,0:T(8,128)(2,1)S(1)} %get-tuple-element.23.refs_2_.refs_3_.refs_4_, ...), custom_call_target="tpu_custom_call" | custom-call | flops 452984832 | bytes 4194304 | tf_op jit(solution)/shard_map/inner/pallas_call | solution.py:388
  8.5 0.0 collective-permute-done.refs_1_.refs_7_
  8.5 0.0 collective-permute-done.1.refs_2_.refs_8_
  8.5 0.0 copy-done.4
  8.5 0.2 merge.1
  8.7 0.0 copy-start
  8.8 1.6 %collective-permute-start.2 = (bf16[112,256]{1,0:T(8,128)(2,1)S(1)}, bf16[112,256]{1,0:T(8,128)(2,1)S(1)}, u32[]{:S(2)}, u32[]{:S(2)}) collective-permute-start(bf16[112,256]{1,0:T(8,128)(2,1)S(1)} %get-tuple-element.30.refs_0_), channel_id=1, source_target_pairs={{0,1},{1,2},{2,3},{3,0},{4,5},{5,6},{6,7},{7,4},{8,9},{9,10},{10,1... | collective-permute-start | bytes 172040 | tf_op jit(solution)/shard_map/ppermute | solution.py:450
  10.4 2.2 %collective-permute-start.4 = (bf16[112,256]{1,0:T(8,128)(2,1)S(1)}, bf16[112,256]{1,0:T(8,128)(2,1)S(1)}, u32[]{:S(2)}, u32[]{:S(2)}) collective-permute-start(bf16[112,256]{1,0:T(8,128)(2,1)S(1)} %get-tuple-element.32), channel_id=1, source_target_pairs={{0,3},{1,0},{2,1},{3,2},{4,7},{5,4},{6,5},{7,6},{8,11},{9,8},{10,9... | collective-permute-start | bytes 172040 | tf_op jit(solution)/shard_map/ppermute | solution.py:450
  12.6 0.8 %collective-permute-start.3 = (bf16[96,256]{1,0:T(8,128)(2,1)S(1)}, bf16[96,256]{1,0:T(8,128)(2,1)S(1)}, u32[]{:S(2)}, u32[]{:S(2)}) collective-permute-start(bf16[96,256]{1,0:T(8,128)(2,1)S(1)} %get-tuple-element.31), channel_id=1, source_target_pairs={{0,2},{1,3},{2,0},{3,1},{4,6},{5,7},{6,4},{7,5},{8,10},{9,11},{10,... | collective-permute-start | bytes 147464 | tf_op jit(solution)/shard_map/ppermute | solution.py:450
  13.4 0.0 copy-done.1
  13.4 0.0 copy-done.2
  13.4 0.0 copy-done.3
  13.4 0.0 copy-done.5
  13.4 0.0 copy-done.6
  13.4 1.7 %local.1 = (f32[256,4096]{1,0:T(8,128)S(1)}, bf16[384,256]{1,0:T(8,128)(2,1)S(1)}) custom-call(bf16[256,2048]{1,0:T(8,128)(2,1)S(1)} %get-tuple-element.22.refs_1_.refs_0_, bf16[256,2048]{1,0:T(8,128)(2,1)S(1)} %get-tuple-element.33.refs_1_, bf16[256,1024]{1,0:T(8,128)(2,1)S(1)} %get-tuple-element.34.refs_2_, ...), custom_call_target="tpu_custom_call" | custom-call | flops 1073741824 | bytes 8388608 | tf_op jit(solution)/shard_map/local/pallas_call | solution.py:388
  15.2 2.6 %collective-permute-done.3.refs_2_ = bf16[96,256]{1,0:T(8,128)(2,1)S(1)} collective-permute-done((bf16[96,256]{1,0:T(8,128)(2,1)S(1)}, bf16[96,256]{1,0:T(8,128)(2,1)S(1)}, u32[]{:S(2)}, u32[]{:S(2)}) %collective-permute-start.3) | collective-permute-done | bytes 49184 | tf_op jit(solution)/shard_map/ppermute | solution.py:450
  17.8 0.0 collective-permute-done.2.refs_1_
  17.8 0.0 collective-permute-done.4.refs_3_
  17.8 0.0 copy-done
  17.8 2.5 %last.1 = bf16[256,32,128]{2,1,0:T(8,128)(2,1)} custom-call(bf16[112,256]{1,0:T(8,128)(2,1)S(1)} %get-tuple-element.30.refs_0_, bf16[112,256]{1,0:T(8,128)(2,1)S(1)} %collective-permute-done.2.refs_1_, bf16[96,256]{1,0:T(8,128)(2,1)S(1)} %collective-permute-done.3.refs_2_, bf16[112,256]{1,0:T(8,128)(2,1)S(1)} %collective-permute-done.4.refs_3_, ...), custom_call_target="tpu_custom_call" | custom-call | tf_op jit(solution)/shard_map/last/pallas_call | solution.py:388
Async XLA Ops:
  2.1 6.4 %collective-permute-start = (bf16[128,256]{1,0:T(8,128)(2,1)S(1)}, bf16[128,256]{1,0:T(8,128)(2,1)S(1)}, u32[]{:S(2)}, u32[]{:S(2)}) collective-permute-start(bf16[128,256]{1,0:T(8,128)(2,1)S(1)} %get-tuple-element.28.refs_5_), channel_id=1, source_target_pairs={{0,4},{4,0},{8,12},{12,8},{16,20},{20,16},{24,28},{28,24},{1,5},{5... | collective-permute-start | bytes 196616 | tf_op jit(solution)/shard_map/ppermute | solution.py:407
  2.7 5.9 %collective-permute-start.1 = (bf16[128,256]{1,0:T(8,128)(2,1)S(1)}, bf16[128,256]{1,0:T(8,128)(2,1)S(1)}, u32[]{:S(2)}, u32[]{:S(2)}) collective-permute-start(bf16[128,256]{1,0:T(8,128)(2,1)S(1)} %get-tuple-element.29.refs_6_), channel_id=1, source_target_pairs={{0,28},{4,8},{8,4},{12,16},{16,12},{20,24},{24,20},{28,0},{1,29},{... | collective-permute-start | bytes 196616 | tf_op jit(solution)/shard_map/ppermute | solution.py:407
  6.2 2.3 %copy-start.4 = (bf16[144,256]{1,0:T(8,128)(2,1)S(1)}, bf16[144,256]{1,0:T(8,128)(2,1)}, u32[]{:S(2)}) copy-start(bf16[144,256]{1,0:T(8,128)(2,1)} %constant.12.clone.refs_3_) | copy-start | bytes 221188
  6.2 7.2 %copy-start.1 = (bf16[256,512]{1,0:T(8,128)(2,1)S(1)}, bf16[256,512]{1,0:T(8,128)(2,1)}, u32[]{:S(2)}) copy-start(bf16[256,512]{1,0:T(8,128)(2,1)} %constant.15.clone.refs_11_) | copy-start | bytes 786436
  6.2 7.2 %copy-start.2 = (bf16[256,512]{1,0:T(8,128)(2,1)S(1)}, bf16[256,512]{1,0:T(8,128)(2,1)}, u32[]{:S(2)}) copy-start(bf16[256,512]{1,0:T(8,128)(2,1)} %constant.16.clone.refs_12_) | copy-start | bytes 786436
  6.2 7.2 %copy-start.3 = (bf16[256,256]{1,0:T(8,128)(2,1)S(1)}, bf16[256,256]{1,0:T(8,128)(2,1)}, u32[]{:S(2)}) copy-start(bf16[256,256]{1,0:T(8,128)(2,1)} %constant.14.clone.refs_10_) | copy-start | bytes 393220
  6.2 7.2 %copy-start.5 = (bf16[128,256]{1,0:T(8,128)(2,1)S(1)}, bf16[128,256]{1,0:T(8,128)(2,1)}, u32[]{:S(2)}) copy-start(bf16[128,256]{1,0:T(8,128)(2,1)} %constant.13.clone.refs_9_) | copy-start | bytes 196612
  6.2 7.2 %copy-start.6 = (bf16[64,64]{1,0:T(8,128)(2,1)S(1)}, bf16[64,64]{1,0:T(8,128)(2,1)}, u32[]{:S(2)}) copy-start(bf16[64,64]{1,0:T(8,128)(2,1)} %refs_4_.1) | copy-start | bytes 24580
  8.7 9.1 %copy-start = (bf16[256,4096]{1,0:T(8,128)(2,1)S(1)}, bf16[256,4096]{1,0:T(8,128)(2,1)}, u32[]{:S(2)}) copy-start(bf16[256,4096]{1,0:T(8,128)(2,1)} %constant.17.clone.refs_6_) | copy-start | bytes 6291460
  8.8 9.0 %collective-permute-start.2 = (bf16[112,256]{1,0:T(8,128)(2,1)S(1)}, bf16[112,256]{1,0:T(8,128)(2,1)S(1)}, u32[]{:S(2)}, u32[]{:S(2)}) collective-permute-start(bf16[112,256]{1,0:T(8,128)(2,1)S(1)} %get-tuple-element.30.refs_0_), channel_id=1, source_target_pairs={{0,1},{1,2},{2,3},{3,0},{4,5},{5,6},{6,7},{7,4},{8,9},{9,10},{10,1... | collective-permute-start | bytes 172040 | tf_op jit(solution)/shard_map/ppermute | solution.py:450
  10.4 7.4 %collective-permute-start.4 = (bf16[112,256]{1,0:T(8,128)(2,1)S(1)}, bf16[112,256]{1,0:T(8,128)(2,1)S(1)}, u32[]{:S(2)}, u32[]{:S(2)}) collective-permute-start(bf16[112,256]{1,0:T(8,128)(2,1)S(1)} %get-tuple-element.32), channel_id=1, source_target_pairs={{0,3},{1,0},{2,1},{3,2},{4,7},{5,4},{6,5},{7,6},{8,11},{9,8},{10,9... | collective-permute-start | bytes 172040 | tf_op jit(solution)/shard_map/ppermute | solution.py:450
  12.6 5.2 %collective-permute-start.3 = (bf16[96,256]{1,0:T(8,128)(2,1)S(1)}, bf16[96,256]{1,0:T(8,128)(2,1)S(1)}, u32[]{:S(2)}, u32[]{:S(2)}) collective-permute-start(bf16[96,256]{1,0:T(8,128)(2,1)S(1)} %get-tuple-element.31), channel_id=1, source_target_pairs={{0,2},{1,3},{2,0},{3,1},{4,6},{5,7},{6,4},{7,5},{8,10},{9,11},{10,... | collective-permute-start | bytes 147464 | tf_op jit(solution)/shard_map/ppermute | solution.py:450

commit v4 on v3

--- a/solution.py
+++ b/solution.py
@@ -10,6 +10,7 @@
 BF16 = jnp.bfloat16
 F32 = jnp.float32
 PART = 8
+CHUNKS = 2
 VMEM = pltpu.VMEM
 
 
@@ -22,6 +23,25 @@
     wx = hat(level, np.asarray(xs)[:, None], np.asarray(cell_x)[None, :])
     wy = hat(level, np.asarray(ys)[:, None], np.asarray(cell_y)[None, :])
     return (wx[:, None, :] * wy[None, :, :]).reshape(len(xs) * len(ys), len(cell_x))
+
+
+def routes(count):
+    if count == 4:
+        return [(1, 3, 0, 2), (3, 2, 1, 0), (2, 0, 3, 1)]
+    return [[(i + d) % count for i in range(count)] for d in range(1, count)]
+
+
+def arrivals(count):
+    return [
+        [(k, step.index(z)) for k, step in enumerate(routes(count)) if step[z] != z] for z in range(count)
+    ]
+
+
+def chosen(index, values):
+    result = index * 0
+    for i, value in enumerate(values):
+        result = result + jnp.where(index == i, value, 0)
+    return result
 
 
 def up16(n):
@@ -148,16 +168,23 @@
     return high, index - high * size
 
 
-def first_kernel(plan, x_ref, v_in_ref, raw_ref, ends_ref, a_ref, b_ref, v_ref, column_ref, t1_ref, t2_ref, nat, sem):
+def first_kernel(plan, x_ref, raw_ref, ends_ref, a_ref, b_ref, column_ref, t1_ref, t2_ref, nat, sem):
     rows, cols = plan.rows, plan.cols
     width = x_ref.shape[0]
     last = rows // PART - 1
+    chunk = width // CHUNKS
+
+    def fetch(h, start, count, i):
+        fields = pl.ds(start, count)
+        return pltpu.make_async_copy(x_ref.at[fields, pl.ds(h * PART, PART), :], raw_ref.at[h, fields], sem.at[i])
+
     copies = [
-        pltpu.make_async_copy(x_ref.at[:, pl.ds(h * PART, PART), :], raw_ref.at[h], sem.at[h]) for h in range(last + 1)
+        [fetch(h, c * chunk, chunk, 2 * c + place) for place, h in enumerate((0, last))] for c in range(CHUNKS)
     ]
-    order = [copies[0], copies[last], *copies[1:last], pltpu.make_async_copy(v_in_ref, v_ref, sem.at[last + 1])]
-    for copy in order:
-        copy.start()
+    copies.append([fetch(h, 0, width, 2 * CHUNKS + h - 1) for h in range(1, last)])
+    for group in copies:
+        for copy in group:
+            copy.start()
     even = lax.rem(lax.axis_index("gx"), 2) == 0
 
     shape = (plan.cells, cols)
@@ -190,12 +217,7 @@
     along = ramp(size, y - size * second).astype(F32) * inverse
     size = size.astype(F32)
 
-    def message(h, place, end):
-        copies[h].wait()
-        nat[place] = raw_ref[h].astype(F32).reshape(width * PART, cols)
-        for x in range(PART):
-            row = nat[place, pl.ds(x, width, stride=PART), :]
-            ends_ref[:, pl.ds((place * PART + x) * cols, cols)] = row.astype(BF16)
+    def message(place, end):
         total = None
         for x in range(0, PART, 2):
             table = [(ramp(size, size * 0 + (end - x - i)) * along).astype(BF16) for i in range(2)]
@@ -203,11 +225,18 @@
             total = term if total is None else total + term
         return total.astype(BF16)
 
-    low = message(0, 0, 0)
-    up = message(last, 1, PART)
+    for c in range(CHUNKS):
+        fields = pl.ds(c * chunk, chunk)
+        for place, h in enumerate((0, last)):
+            copies[c][place].wait()
+            nat[c, place] = raw_ref[h, fields].astype(F32).reshape(chunk * PART, cols)
+            for x in range(PART):
+                row = nat[c, place, pl.ds(x, chunk, stride=PART), :]
+                ends_ref[fields, pl.ds((place * PART + x) * cols, cols)] = row.astype(BF16)
+    low, up = message(0, 0), message(1, PART)
     a_ref[...] = jnp.where(even, up, low)
     b_ref[...] = jnp.where(even, low, up)
-    for copy in order[2:]:
+    for copy in copies[-1]:
         copy.wait()
 
 
@@ -225,7 +254,7 @@
 
 
 def inner_kernel(
-    plan, raw_ref, ends_ref, v_ref, column_ref, t1_ref, t2_ref, inner_ref, own_ref, carry1_ref, nat, level1
+    plan, raw_ref, ends_ref, column_ref, t1_ref, t2_ref, inner_ref, own_ref, level1, level2, nat
 ):
     rows, cols = plan.rows, plan.cols
     width = ends_ref.shape[0]
@@ -249,16 +278,10 @@
         if k > 0:
             total = total + dot(fine(8 * k - 1, 1), t1_ref[pl.ds(0, cols), :])
         level1[:, pl.ds(4 * k * c1, 4 * c1)] = (total * (1 / 1.5)).astype(BF16)
-    level2 = (dot(level1[...], t2_ref[...]) * (1 / 1.5)).astype(BF16)
-    mixed2 = (dot(v_ref[2], level2) * (1 / 1.5)).astype(BF16)
-    step = 4 * c1
-    for k in range(n1 * c1 // step):
-        lanes = pl.ds(k * step, step)
-        mixed1 = dot(v_ref[1], level1[:, lanes]) + dot_nt(mixed2, t2_ref[lanes, :])
-        carry1_ref[:, lanes] = (mixed1 * (1 / 1.5)).astype(BF16)
-
-
-def merge_kernel(plan, own_ref, a_ref, b_ref, merge_ref, right_ref, left_ref, block_ref):
+    level2[...] = (dot(level1[...], t2_ref[...]) * (1 / 1.5)).astype(BF16)
+
+
+def merge_kernel(plan, count, own_ref, b_ref, a_ref, merge_ref, right_ref, *out_refs):
     even = lax.rem(lax.axis_index("gx"), 2) == 0
     size = plan.row_size
     a, b = a_ref[...], b_ref[...]
@@ -266,20 +289,33 @@
     total32 = own_ref[...] + dot(merge_ref[:, :size], before) + dot(merge_ref[:, size:], after)
     total = total32.astype(BF16)
     right_ref[...] = total[: plan.message]
-    left_ref[: plan.edge] = total[: plan.edge]
     row = lax.broadcasted_iota(jnp.int32, (plan.edge_size, total.shape[1]), 0)
     tile = jnp.where(row < plan.spare, total32[plan.edge : plan.message], total32[plan.message :])
-    left_ref[plan.edge :] = tile.astype(BF16)
-    block_ref[...] = total[: plan.cells3]
+    right, left = total[plan.edge : plan.message], tile.astype(BF16)
+    z = lax.axis_index("gy")
+    for step, ref in zip(routes(count), out_refs):
+        to_left = chosen(z, [int(step[i] == i - 1) for i in range(count)]) == 1
+        ref[: plan.edge] = total[: plan.edge]
+        ref[plan.edge :] = jnp.where(to_left, left, right)
+
+
+def source_of(z, count, d):
+    return z if d == 0 else chosen(z, [got[d - 1][1] for got in arrivals(count)])
 
 
 def local_kernel(
-    plan, count, ends_ref, inner_ref, carry1, v_ref, k_ref, sa_ref, sb_ref, ra_ref, rb_ref, even_ref, odd_ref,
-    first_ref, last_ref, base_ref, spread_ref,
+    plan, count, ends_ref, inner_ref, level1, level2, t2_ref, v_ref, k_ref, sa_ref, sb_ref, ra_ref, rb_ref, even_ref, odd_ref,
+    first_ref, last_ref, base_ref, spread_ref, carry1,
 ):
     rows, cols = plan.rows, plan.cols
     n1, c1 = plan.counts[1]
     fine = Rows(plan, ends_ref, inner_ref)
+    mixed2 = (dot(v_ref[2], level2[...]) * (1 / 1.5)).astype(BF16)
+    step = 4 * c1
+    for k in range(n1 * c1 // step):
+        lanes = pl.ds(k * step, step)
+        mixed1 = dot(v_ref[1], level1[:, lanes]) + dot_nt(mixed2, t2_ref[lanes, :])
+        carry1[:, lanes] = (mixed1 * (1 / 1.5)).astype(BF16)
 
     even = lax.rem(lax.axis_index("gx"), 2) == 0
     a, b = ra_ref[...], rb_ref[...]
@@ -334,7 +370,7 @@
     _, col = parts((cells3, size), 0)
     place = lax.broadcasted_iota(jnp.int32, (cells3, size), 1)
     for d in range(count):
-        start = lax.rem(z - d + count, count) * (m3 - 1)
+        start = source_of(z, count, d) * (m3 - 1)
         spread = jnp.where(same, dot(one(place == start + col), picked), 0.0).astype(BF16)
         keep = one(same & (target == start + source_col) & (target < size))
         spread_ref[pl.ds(d * cells3, cells3), :block] = spread
@@ -342,20 +378,34 @@
 
 
 def last_kernel(plan, count, *refs):
-    own_ref, *in_refs = refs[:count]
-    v_ref, spread_ref, final_ref, base_ref, out_ref, nat, buf, sem = refs[count:]
+    steps = routes(count)
+    own_ref, *in_refs = refs[: 1 + len(steps)]
+    v_ref, spread_ref, final_ref, base_ref, out_ref, nat, buf, sem = refs[1 + len(steps) :]
     rows, cols = plan.rows, plan.cols
     width = v_ref.shape[1]
     block = plan.block
     z = lax.axis_index("gy")
-    level3 = jnp.concatenate([own_ref[: plan.cells3]] + [ref[: plan.cells3] for ref in in_refs], axis=0)
+    messages = [own_ref[...]]
+    for d in range(1, count):
+        step_of = [got[d - 1][0] for got in arrivals(count)]
+        message = None
+        for step in sorted(set(step_of)):
+            value = in_refs[step][...]
+            mine = chosen(z, [int(s == step) for s in step_of]) == 1
+            message = value if message is None else jnp.where(mine, value, message)
+        messages.append(message)
+    level3 = jnp.concatenate([message[: plan.cells3] for message in messages], axis=0)
     mixed = (dot_nt(v_ref[3], level3) * (1 / 1.5**3)).astype(BF16)
     carry = dot(mixed, spread_ref[...])
     carry = (carry[:, :block] + carry[:, block:]) * (1 / 1.5**3)
-    left = in_refs[0][plan.edge :]
-    right = (in_refs[-1][plan.edge :].astype(F32) + own_ref[plan.edge :].astype(F32)).astype(BF16)
-    left = jnp.where(z > 0, left, jnp.zeros_like(left))
-    right = jnp.where(z < count - 1, right, jnp.zeros_like(right))
+    left = jnp.zeros((plan.edge_size, width), F32)
+    right = own_ref[plan.edge :].astype(F32)
+    for d in range(1, count):
+        source, edge = source_of(z, count, d), messages[d][plan.edge :].astype(F32)
+        left = left + jnp.where((source == z - 1) & (z > 0), edge, 0.0)
+        right = right + jnp.where((source == z + 1) & (z < count - 1), edge, 0.0)
+    left = left.astype(BF16)
+    right = jnp.where(z < count - 1, right, 0.0).astype(BF16)
     edges = jnp.concatenate([left, right], axis=0)
     one = dot_nt(v_ref[1], edges) * (1 / 1.5**2)
     two = dot_nt(v_ref[2], edges) * (1 / 1.5**4)
@@ -415,47 +465,50 @@
         size = rows * cols
         row_message = ((plan.row_size, width), BF16)
         cells = plan.cells
-        raw, ends, send_a, send_b, vertical, column, to_level1, to_level2 = call(
+        raw, ends, send_a, send_b, column, to_level1, to_level2 = call(
             lambda *refs: first_kernel(plan, *refs),
-            [gradient, vertical],
+            [gradient],
             [
                 ((parts, width, PART, cols), BF16), ((width, 2 * PART * cols), BF16), row_message, row_message,
-                (vertical.shape, BF16), ((cells, size), BF16), ((9 * cols, 4 * c1), BF16), ((n1 * c1, n2 * c2), BF16),
+                ((cells, size), BF16), ((9 * cols, 4 * c1), BF16), ((n1 * c1, n2 * c2), BF16),
             ],
-            [VMEM((2, width * PART, cols), F32), pltpu.SemaphoreType.DMA((parts + 1,))],
-            hbm=(0, 1),
+            [
+                VMEM((CHUNKS, 2, width // CHUNKS * PART, cols), F32),
+                pltpu.SemaphoreType.DMA((2 * CHUNKS + parts - 2,)),
+            ],
+            hbm=(0,),
             name="first",
         )
         recv_b = swap(send_b, False)
         recv_a = swap(send_a, True)
-        inner, own, carry1 = call(
+        inner, own, level1, level2 = call(
             lambda *refs: inner_kernel(plan, *refs),
+            [raw, ends, column, to_level1, to_level2],
             [
-                raw, ends, vertical, column, to_level1, to_level2,
+                ((width, size - 2 * PART * cols), BF16), ((cells, width), F32), ((width, n1 * c1), BF16),
+                ((width, n2 * c2), BF16),
             ],
-            [((width, size - 16 * cols), BF16), ((cells, width), F32), ((width, size // 4), BF16)],
-            [VMEM((parts - 2, width * PART, cols), F32), VMEM((width, size // 4), BF16)],
+            [VMEM((parts - 2, width * PART, cols), F32)],
             name="inner",
             cost=pl.CostEstimate(flops=3 * cells * width * size, bytes_accessed=4 * 1024 * 1024, transcendentals=0),
         )
-        right, left, block = call(
-            lambda *refs: merge_kernel(plan, *refs),
-            [own, recv_a, recv_b, const(plan.merge)],
-            [((plan.message, width), BF16), ((plan.message, width), BF16), ((plan.cells3, width), BF16)],
+        steps = routes(along)
+        message = ((plan.message, width), BF16)
+        right, *messages = call(
+            lambda *refs: merge_kernel(plan, along, *refs),
+            [own, recv_b, recv_a, const(plan.merge)],
+            [message] * (1 + len(steps)),
             name="merge",
         )
-        messages = [block] * (along + 1)
-        messages[1], messages[along - 1] = right, left
-        arrived = [
-            lax.ppermute(messages[d], "gy", [(i, (i + d) % along) for i in range(along)]) for d in range(1, along)
-        ]
+        arrived = [lax.ppermute(x, "gy", list(enumerate(step))) for x, step in zip(messages, steps)]
         base, spread = call(
             lambda *refs: local_kernel(plan, along, *refs),
             [
-                ends, inner, carry1, vertical, kernel, send_a, send_b, recv_a, recv_b, const(plan.even),
+                ends, inner, level1, level2, to_level2, vertical, kernel, send_a, send_b, recv_a, recv_b, const(plan.even),
                 const(plan.odd), const(plan.from_first), const(plan.from_last),
             ],
             [((width, size), F32), ((along * plan.cells3, 2 * plan.block), BF16)],
+            [VMEM((width, n1 * c1), BF16)],
             name="local",
             cost=pl.CostEstimate(flops=4 * width * width * size, bytes_accessed=8 * 1024 * 1024, transcendentals=0),
         )

time: 20.4 us -> 19.7 us (0.966)
  waiting for transfers between devices: 2.64 us -> 0.6 us
  starting transfers between devices: 8.74 us -> 10.4 us
  Pallas kernels: 8.76 us -> 8.34 us
    ppermute x3, starting transfers between devices: 4.67 us -> 7.03 us  [on_device(): lax.ppermute(x, 'gy', list(enumerate(step)))]
    ppermute x3, waiting for transfers between devices: 2.63 us -> 0.43 us  [on_device(): lax.ppermute(x, 'gy', list(enumerate(step)))]
    ppermute x2, starting transfers between devices: 4.07 us -> 3.4 us  [swap(): return lax.ppermute(x, 'gx', [(i, partner(i)) for i in range(across)])]
    pallas_call x5, Pallas kernels: 8.76 us -> 8.34 us  [call(): pl.pallas_call(kernel, in_specs=specs, out_specs=out_specs, out_shape=out...]
  transfers between devices with their start and end apart: 5 -> 5, of which waited for: 1 -> 2; matrix products, arithmetic and copies ran while one was open for 0% -> 0% of each run, Pallas kernels for 20% -> 20%
where the time goes in v4:
time: 19.7 us; the launch traced here: 19.5 us
  starting transfers between devices  10.4 us (53%)
  Pallas kernels  8.34 us (42%)
  waiting for transfers between devices  0.6 us (3%)
    pallas_call x5, Pallas kernels, call(): pl.pallas_call(kernel, in_specs=specs, out_specs=out_specs, out_shape=out...  8.34 us
    ppermute x3, starting transfers between devices, on_device(): lax.ppermute(x, 'gy', list(enumerate(step)))  7.03 us
    ppermute x2, starting transfers between devices, swap(): return lax.ppermute(x, 'gx', [(i, partner(i)) for i in range(across)])  3.4 us
    ppermute x3, waiting for transfers between devices, on_device(): lax.ppermute(x, 'gy', list(enumerate(step)))  0.43 us
  transfers between devices with their start and end apart: 5, of which 2 were waited for; matrix products, arithmetic and copies ran while one was open for 0% of the time, Pallas kernels for 20%

profile of v4, /device:TPU:0, one launch (start us, length us, event | category | flops | bytes accessed | tf_op | source)
XLA Modules:
  0.0 19.5 jit_solution(15136072825507812505)
XLA Ops:
  0.0 1.9 %first.1 = (bf16[4,256,8,128]{3,2,1,0:T(8,128)(2,1)S(1)}, bf16[256,2048]{1,0:T(8,128)(2,1)S(1)}, bf16[128,256]{1,0:T(8,128)(2,1)S(1)}, bf16[128,256]{1,0:T(8,128...) custom-call(bf16[256,32,128]{2,1,0:T(8,128)(2,1)} %refs_0_.1), custom_call_target="tpu_custom_call" | custom-call | tf_op jit(solution)/shard_map/first/pallas_call | solution.py:438
  1.9 3.4 %collective-permute-start = (bf16[128,256]{1,0:T(8,128)(2,1)S(1)}, bf16[128,256]{1,0:T(8,128)(2,1)S(1)}, u32[]{:S(2)}, u32[]{:S(2)}) collective-permute-start(bf16[128,256]{1,0:T(8,128)(2,1)S(1)} %get-tuple-element.28.refs_8_), channel_id=1, source_target_pairs={{0,28},{4,8},{8,4},{12,16},{16,12},{20,24},{24,20},{28,0},{1,29},{... | collective-permute-start | bytes 196616 | tf_op jit(solution)/shard_map/ppermute | solution.py:457
  5.3 0.0 collective-permute-start.1
  5.3 0.0 copy-start.5
  5.3 0.0 copy-start
  5.3 0.0 copy-start.2
  5.4 0.0 copy-start.3
  5.4 0.0 copy-start.4
  5.4 0.0 copy-start.6
  5.4 0.0 copy-start.7
  5.4 1.7 %inner.1 = (bf16[256,2048]{1,0:T(8,128)(2,1)S(1)}, f32[144,256]{1,0:T(8,128)S(1)}, bf16[256,1024]{1,0:T(8,128)(2,1)S(1)}, bf16[256,256]{1,0:T(8,128)(2,1)S(1)}) custom-call(bf16[4,256,8,128]{3,2,1,0:T(8,128)(2,1)S(1)} %get-tuple-element.22.refs_0_, bf16[256,2048]{1,0:T(8,128)(2,1)S(1)} %get-tuple-element.23.refs_1_.refs_0_, ...), custom_call_target="tpu_custom_call" | custom-call | flops 452984832 | bytes 4194304 | tf_op jit(solution)/shard_map/inner/pallas_call | solution.py:438
  7.1 0.2 collective-permute-done.refs_1_.refs_10_
  7.3 0.0 collective-permute-done.1.refs_2_.refs_9_
  7.3 0.0 copy-done.5
  7.3 0.2 merge.1
  7.5 3.0 %collective-permute-start.2 = (bf16[112,256]{1,0:T(8,128)(2,1)S(1)}, bf16[112,256]{1,0:T(8,128)(2,1)S(1)}, u32[]{:S(2)}, u32[]{:S(2)}) collective-permute-start(bf16[112,256]{1,0:T(8,128)(2,1)S(1)} %get-tuple-element.31), channel_id=1, source_target_pairs={{0,1},{1,3},{2,0},{3,2},{4,5},{5,7},{6,4},{7,6},{8,9},{9,11},{10,8... | collective-permute-start | bytes 172040 | tf_op jit(solution)/shard_map/ppermute | solution.py:503
  10.5 2.5 %collective-permute-start.3 = (bf16[112,256]{1,0:T(8,128)(2,1)S(1)}, bf16[112,256]{1,0:T(8,128)(2,1)S(1)}, u32[]{:S(2)}, u32[]{:S(2)}) collective-permute-start(bf16[112,256]{1,0:T(8,128)(2,1)S(1)} %get-tuple-element.32), channel_id=1, source_target_pairs={{0,3},{1,2},{2,1},{3,0},{4,7},{5,6},{6,5},{7,4},{8,11},{9,10},{10,... | collective-permute-start | bytes 172040 | tf_op jit(solution)/shard_map/ppermute | solution.py:503
  13.0 1.6 %collective-permute-start.4 = (bf16[112,256]{1,0:T(8,128)(2,1)S(1)}, bf16[112,256]{1,0:T(8,128)(2,1)S(1)}, u32[]{:S(2)}, u32[]{:S(2)}) collective-permute-start(bf16[112,256]{1,0:T(8,128)(2,1)S(1)} %get-tuple-element.33), channel_id=1, source_target_pairs={{0,2},{1,0},{2,3},{3,1},{4,6},{5,4},{6,7},{7,5},{8,10},{9,8},{10,1... | collective-permute-start | bytes 172040 | tf_op jit(solution)/shard_map/ppermute | solution.py:503
  14.5 0.0 copy-done
  14.5 0.0 copy-done.2
  14.5 0.0 copy-done.3
  14.5 0.0 copy-done.4
  14.5 0.0 copy-done.6
  14.5 0.0 copy-done.7
  14.6 0.0 copy-start.1
  14.6 2.1 %local.1 = (f32[256,4096]{1,0:T(8,128)S(1)}, bf16[384,256]{1,0:T(8,128)(2,1)S(1)}) custom-call(bf16[256,2048]{1,0:T(8,128)(2,1)S(1)} %get-tuple-element.23.refs_1_.refs_0_, bf16[256,2048]{1,0:T(8,128)(2,1)S(1)} %get-tuple-element.34.refs_1_, bf16[256,1024]{1,0:T(8,128)(2,1)S(1)} %get-tuple-element.35.refs_2_, ...), custom_call_target="tpu_custom_call" | custom-call | flops 1073741824 | bytes 8388608 | tf_op jit(solution)/shard_map/local/pallas_call | solution.py:438
  16.7 0.0 collective-permute-done.2.refs_1_
  16.7 0.0 collective-permute-done.3.refs_2_
  16.7 0.4 %collective-permute-done.4.refs_3_ = bf16[112,256]{1,0:T(8,128)(2,1)S(1)} collective-permute-done((bf16[112,256]{1,0:T(8,128)(2,1)S(1)}, bf16[112,256]{1,0:T(8,128)(2,1)S(1)}, u32[]{:S(2)}, u32[]{:S(2)}) %collective-permute-start.4) | collective-permute-done | bytes 57376 | tf_op jit(solution)/shard_map/ppermute | solution.py:503
  17.1 0.0 copy-done.1
  17.1 2.4 %last.1 = bf16[256,32,128]{2,1,0:T(8,128)(2,1)} custom-call(bf16[112,256]{1,0:T(8,128)(2,1)S(1)} %get-tuple-element.30.refs_0_, bf16[112,256]{1,0:T(8,128)(2,1)S(1)} %collective-permute-done.2.refs_1_, bf16[112,256]{1,0:T(8,128)(2,1)S(1)} %collective-permute-done.3.refs_2_, bf16[112,256]{1,0:T(8,128)(2,1)S(1)} %collective-permute-done.4.refs_3_, ...), custom_call_target="tpu_custom_call" | custom-call | tf_op jit(solution)/shard_map/last/pallas_call | solution.py:438
Async XLA Ops:
  1.9 5.3 %collective-permute-start = (bf16[128,256]{1,0:T(8,128)(2,1)S(1)}, bf16[128,256]{1,0:T(8,128)(2,1)S(1)}, u32[]{:S(2)}, u32[]{:S(2)}) collective-permute-start(bf16[128,256]{1,0:T(8,128)(2,1)S(1)} %get-tuple-element.28.refs_8_), channel_id=1, source_target_pairs={{0,28},{4,8},{8,4},{12,16},{16,12},{20,24},{24,20},{28,0},{1,29},{... | collective-permute-start | bytes 196616 | tf_op jit(solution)/shard_map/ppermute | solution.py:457
  5.3 2.0 %collective-permute-start.1 = (bf16[128,256]{1,0:T(8,128)(2,1)S(1)}, bf16[128,256]{1,0:T(8,128)(2,1)S(1)}, u32[]{:S(2)}, u32[]{:S(2)}) collective-permute-start(bf16[128,256]{1,0:T(8,128)(2,1)S(1)} %get-tuple-element.29.refs_7_), channel_id=1, source_target_pairs={{0,4},{4,0},{8,12},{12,8},{16,20},{20,16},{24,28},{28,24},{1,5},{5... | collective-permute-start | bytes 196616 | tf_op jit(solution)/shard_map/ppermute | solution.py:457
  5.3 2.0 %copy-start.5 = (bf16[144,256]{1,0:T(8,128)(2,1)S(1)}, bf16[144,256]{1,0:T(8,128)(2,1)}, u32[]{:S(2)}) copy-start(bf16[144,256]{1,0:T(8,128)(2,1)} %constant.12.clone.refs_3_) | copy-start | bytes 221188
  5.3 9.2 %copy-start = (bf16[4,256,256]{2,1,0:T(8,128)(2,1)S(1)}, bf16[4,256,256]{2,1,0:T(8,128)(2,1)}, u32[]{:S(2)}) copy-start(bf16[4,256,256]{2,1,0:T(8,128)(2,1)} %refs_4_.1) | copy-start | bytes 1572868
  5.3 9.2 %copy-start.2 = (bf16[256,512]{1,0:T(8,128)(2,1)S(1)}, bf16[256,512]{1,0:T(8,128)(2,1)}, u32[]{:S(2)}) copy-start(bf16[256,512]{1,0:T(8,128)(2,1)} %constant.15.clone.refs_13_) | copy-start | bytes 786436
  5.4 9.2 %copy-start.3 = (bf16[256,512]{1,0:T(8,128)(2,1)S(1)}, bf16[256,512]{1,0:T(8,128)(2,1)}, u32[]{:S(2)}) copy-start(bf16[256,512]{1,0:T(8,128)(2,1)} %constant.16.clone.refs_14_) | copy-start | bytes 786436
  5.4 9.2 %copy-start.4 = (bf16[256,256]{1,0:T(8,128)(2,1)S(1)}, bf16[256,256]{1,0:T(8,128)(2,1)}, u32[]{:S(2)}) copy-start(bf16[256,256]{1,0:T(8,128)(2,1)} %constant.14.clone.refs_12_) | copy-start | bytes 393220
  5.4 9.2 %copy-start.6 = (bf16[128,256]{1,0:T(8,128)(2,1)S(1)}, bf16[128,256]{1,0:T(8,128)(2,1)}, u32[]{:S(2)}) copy-start(bf16[128,256]{1,0:T(8,128)(2,1)} %constant.13.clone.refs_11_) | copy-start | bytes 196612
  5.4 9.2 %copy-start.7 = (bf16[64,64]{1,0:T(8,128)(2,1)S(1)}, bf16[64,64]{1,0:T(8,128)(2,1)}, u32[]{:S(2)}) copy-start(bf16[64,64]{1,0:T(8,128)(2,1)} %refs_6_.2) | copy-start | bytes 24580
  7.5 9.2 %collective-permute-start.2 = (bf16[112,256]{1,0:T(8,128)(2,1)S(1)}, bf16[112,256]{1,0:T(8,128)(2,1)S(1)}, u32[]{:S(2)}, u32[]{:S(2)}) collective-permute-start(bf16[112,256]{1,0:T(8,128)(2,1)S(1)} %get-tuple-element.31), channel_id=1, source_target_pairs={{0,1},{1,3},{2,0},{3,2},{4,5},{5,7},{6,4},{7,6},{8,9},{9,11},{10,8... | collective-permute-start | bytes 172040 | tf_op jit(solution)/shard_map/ppermute | solution.py:503
  10.5 6.2 %collective-permute-start.3 = (bf16[112,256]{1,0:T(8,128)(2,1)S(1)}, bf16[112,256]{1,0:T(8,128)(2,1)S(1)}, u32[]{:S(2)}, u32[]{:S(2)}) collective-permute-start(bf16[112,256]{1,0:T(8,128)(2,1)S(1)} %get-tuple-element.32), channel_id=1, source_target_pairs={{0,3},{1,2},{2,1},{3,0},{4,7},{5,6},{6,5},{7,4},{8,11},{9,10},{10,... | collective-permute-start | bytes 172040 | tf_op jit(solution)/shard_map/ppermute | solution.py:503
  13.0 4.2 %collective-permute-start.4 = (bf16[112,256]{1,0:T(8,128)(2,1)S(1)}, bf16[112,256]{1,0:T(8,128)(2,1)S(1)}, u32[]{:S(2)}, u32[]{:S(2)}) collective-permute-start(bf16[112,256]{1,0:T(8,128)(2,1)S(1)} %get-tuple-element.33), channel_id=1, source_target_pairs={{0,2},{1,0},{2,3},{3,1},{4,6},{5,4},{6,7},{7,5},{8,10},{9,8},{10,1... | collective-permute-start | bytes 172040 | tf_op jit(solution)/shard_map/ppermute | solution.py:503
  14.6 2.6 %copy-start.1 = (bf16[256,4096]{1,0:T(8,128)(2,1)S(1)}, bf16[256,4096]{1,0:T(8,128)(2,1)}, u32[]{:S(2)}) copy-start(bf16[256,4096]{1,0:T(8,128)(2,1)} %constant.17.clone.refs_6_) | copy-start | bytes 6291460

commit v5 on v4

--- a/solution.py
+++ b/solution.py
@@ -168,7 +168,7 @@
     return high, index - high * size
 
 
-def first_kernel(plan, x_ref, raw_ref, ends_ref, a_ref, b_ref, column_ref, t1_ref, t2_ref, nat, sem):
+def first_kernel(plan, x_ref, raw_ref, a_ref, b_ref, column_ref, t1_ref, t2_ref, nat, sums, table, sem):
     rows, cols = plan.rows, plan.cols
     width = x_ref.shape[0]
     last = rows // PART - 1
@@ -210,60 +210,47 @@
     for x in range(n1):
         t2_ref[pl.ds(x * c1, c1), :] = (ramp(2, i - x).astype(F32) * along).astype(BF16)
     shape = (plan.row_size, cols)
-    cells = [(k, 0, c) for k, c in plan.row_cells]
-    size, _, second = cell_tables(cells, shape)
+    level, _, second = cell_tables([(k, 0, c) for k, c in plan.row_cells], shape)
     y = lax.broadcasted_iota(jnp.int32, shape, 1)
-    inverse = jnp.where(size == 2, 0.25, jnp.where(size == 4, 0.0625, 0.015625))
-    along = ramp(size, y - size * second).astype(F32) * inverse
-    size = size.astype(F32)
-
-    def message(place, end):
-        total = None
-        for x in range(0, PART, 2):
-            table = [(ramp(size, size * 0 + (end - x - i)) * along).astype(BF16) for i in range(2)]
-            term = dot_nt(jnp.concatenate(table, axis=1), ends_ref[:, pl.ds((place * PART + x) * cols, 2 * cols)])
-            total = term if total is None else total + term
-        return total.astype(BF16)
-
+    for k in (1, 2, 3):
+        weight = ramp(2**k, y - 2**k * second).astype(F32) * 0.5**k
+        table[:, pl.ds((k - 1) * cols, cols)] = jnp.where(level == 2**k, weight, 0.0).astype(BF16)
     for c in range(CHUNKS):
         fields = pl.ds(c * chunk, chunk)
-        for place, h in enumerate((0, last)):
+        for place, (h, end) in enumerate(((0, 0), (last, PART))):
             copies[c][place].wait()
             nat[c, place] = raw_ref[h, fields].astype(F32).reshape(chunk * PART, cols)
+            found = [None] * 3
             for x in range(PART):
                 row = nat[c, place, pl.ds(x, chunk, stride=PART), :]
-                ends_ref[fields, pl.ds((place * PART + x) * cols, cols)] = row.astype(BF16)
-    low, up = message(0, 0), message(1, PART)
+                for k in range(3):
+                    weight = float(hat(k + 1, x, end / 2 ** (k + 1)))
+                    if weight:
+                        term = row * weight
+                        found[k] = term if found[k] is None else found[k] + term
+            for k in range(3):
+                sums[place, fields, pl.ds(k * cols, cols)] = found[k].astype(BF16)
+    low, up = [dot_nt(table[...], sums[place]).astype(BF16) for place in range(2)]
     a_ref[...] = jnp.where(even, up, low)
     b_ref[...] = jnp.where(even, low, up)
     for copy in copies[-1]:
         copy.wait()
 
 
-class Rows:
-    def __init__(self, plan, ends_ref, inner_ref):
-        self.plan, self.ends, self.inner = plan, ends_ref, inner_ref
-
-    def __call__(self, x, count):
-        rows, cols = self.plan.rows, self.plan.cols
-        if x < 8:
-            return self.ends[:, pl.ds(x * cols, count * cols)]
-        if x >= rows - 8:
-            return self.ends[:, pl.ds((x - rows + 16) * cols, count * cols)]
-        return self.inner[:, pl.ds((x - 8) * cols, count * cols)]
-
-
 def inner_kernel(
-    plan, raw_ref, ends_ref, column_ref, t1_ref, t2_ref, inner_ref, own_ref, level1, level2, nat
+    plan, raw_ref, column_ref, t1_ref, t2_ref, flat_ref, own_ref, level1, level2, nat
 ):
     rows, cols = plan.rows, plan.cols
-    width = ends_ref.shape[0]
-    for h in range(1, rows // PART - 1):
-        nat[h - 1] = raw_ref[h].astype(F32).reshape(width * PART, cols)
+    width = raw_ref.shape[1]
+    for h in range(rows // PART):
+        nat[h] = raw_ref[h].astype(F32).reshape(width * PART, cols)
         for x in range(PART):
-            row = nat[h - 1, pl.ds(x, width, stride=PART), :]
-            inner_ref[:, pl.ds(((h - 1) * PART + x) * cols, cols)] = row.astype(BF16)
-    fine = Rows(plan, ends_ref, inner_ref)
+            row = nat[h, pl.ds(x, width, stride=PART), :]
+            flat_ref[:, pl.ds((h * PART + x) * cols, cols)] = row.astype(BF16)
+
+    def fine(x, count):
+        return flat_ref[:, pl.ds(x * cols, count * cols)]
+
     total = None
     for x in range(0, rows, 2):
         term = dot_nt(column_ref[:, pl.ds(x * cols, 2 * cols)], fine(x, 2))
@@ -304,12 +291,11 @@
 
 
 def local_kernel(
-    plan, count, ends_ref, inner_ref, level1, level2, t2_ref, v_ref, k_ref, sa_ref, sb_ref, ra_ref, rb_ref, even_ref, odd_ref,
+    plan, count, flat_ref, level1, level2, t2_ref, v_ref, k_ref, sa_ref, sb_ref, ra_ref, rb_ref, even_ref, odd_ref,
     first_ref, last_ref, base_ref, spread_ref, carry1,
 ):
     rows, cols = plan.rows, plan.cols
     n1, c1 = plan.counts[1]
-    fine = Rows(plan, ends_ref, inner_ref)
     mixed2 = (dot(v_ref[2], level2[...]) * (1 / 1.5)).astype(BF16)
     step = 4 * c1
     for k in range(n1 * c1 // step):
@@ -332,7 +318,7 @@
     pairs = rows // 2
     for i in range(pairs):
         lanes = pl.ds(2 * i * cols, 2 * cols)
-        total = dot(v_ref[0], fine(2 * i, 2))
+        total = dot(v_ref[0], flat_ref[:, lanes])
         if i % 2 == 0:
             total = total + dot(carry1[:, pl.ds(i * c1, 2 * c1)], even_ref[...])
         elif i < pairs - 1:
@@ -465,15 +451,16 @@
         size = rows * cols
         row_message = ((plan.row_size, width), BF16)
         cells = plan.cells
-        raw, ends, send_a, send_b, column, to_level1, to_level2 = call(
+        raw, send_a, send_b, column, to_level1, to_level2 = call(
             lambda *refs: first_kernel(plan, *refs),
             [gradient],
             [
-                ((parts, width, PART, cols), BF16), ((width, 2 * PART * cols), BF16), row_message, row_message,
+                ((parts, width, PART, cols), BF16), row_message, row_message,
                 ((cells, size), BF16), ((9 * cols, 4 * c1), BF16), ((n1 * c1, n2 * c2), BF16),
             ],
             [
                 VMEM((CHUNKS, 2, width // CHUNKS * PART, cols), F32),
+                VMEM((2, width, 3 * cols), BF16), VMEM((plan.row_size, 3 * cols), BF16),
                 pltpu.SemaphoreType.DMA((2 * CHUNKS + parts - 2,)),
             ],
             hbm=(0,),
@@ -481,14 +468,14 @@
         )
         recv_b = swap(send_b, False)
         recv_a = swap(send_a, True)
-        inner, own, level1, level2 = call(
+        flat, own, level1, level2 = call(
             lambda *refs: inner_kernel(plan, *refs),
-            [raw, ends, column, to_level1, to_level2],
+            [raw, column, to_level1, to_level2],
             [
-                ((width, size - 2 * PART * cols), BF16), ((cells, width), F32), ((width, n1 * c1), BF16),
+                ((width, size), BF16), ((cells, width), F32), ((width, n1 * c1), BF16),
                 ((width, n2 * c2), BF16),
             ],
-            [VMEM((parts - 2, width * PART, cols), F32)],
+            [VMEM((parts, width * PART, cols), F32)],
             name="inner",
             cost=pl.CostEstimate(flops=3 * cells * width * size, bytes_accessed=4 * 1024 * 1024, transcendentals=0),
         )
@@ -504,7 +491,7 @@
         base, spread = call(
             lambda *refs: local_kernel(plan, along, *refs),
             [
-                ends, inner, level1, level2, to_level2, vertical, kernel, send_a, send_b, recv_a, recv_b, const(plan.even),
+                flat, level1, level2, to_level2, vertical, kernel, send_a, send_b, recv_a, recv_b, const(plan.even),
                 const(plan.odd), const(plan.from_first), const(plan.from_last),
             ],
             [((width, size), F32), ((along * plan.cells3, 2 * plan.block), BF16)],

time: 19.7 us -> 19.6 us (level)
  transfers between devices with their start and end apart: 5 -> 5, of which waited for: 2 -> 1; matrix products, arithmetic and copies ran while one was open for 0% -> 0% of each run, Pallas kernels for 20% -> 21%
where the time goes in v5:
time: 19.6 us; the launch traced here: 19.4 us
  starting transfers between devices  10.4 us (53%)
  Pallas kernels  8.39 us (43%)
  waiting for transfers between devices  0.43 us (2%)
    pallas_call x5, Pallas kernels, call(): pl.pallas_call(kernel, in_specs=specs, out_specs=out_specs, out_shape=out...  8.39 us
    ppermute x3, starting transfers between devices, on_device(): lax.ppermute(x, 'gy', list(enumerate(step)))  7 us
    ppermute x2, starting transfers between devices, swap(): return lax.ppermute(x, 'gx', [(i, partner(i)) for i in range(across)])  3.4 us
    ppermute x3, waiting for transfers between devices, on_device(): lax.ppermute(x, 'gy', list(enumerate(step)))  0.43 us
  transfers between devices with their start and end apart: 5, of which 1 were waited for; matrix products, arithmetic and copies ran while one was open for 0% of the time, Pallas kernels for 21%

profile of v5, /device:TPU:0, one launch (start us, length us, event | category | flops | bytes accessed | tf_op | source)
XLA Modules:
  0.0 19.4 jit_solution(6444915512793788768)
XLA Ops:
  0.0 1.8 %first.1 = (bf16[4,256,8,128]{3,2,1,0:T(8,128)(2,1)S(1)}, bf16[128,256]{1,0:T(8,128)(2,1)S(1)}, bf16[128,256]{1,0:T(8,128)(2,1)S(1)}, bf16[144,4096]{1,0:T(8,128...) custom-call(bf16[256,32,128]{2,1,0:T(8,128)(2,1)} %refs_0_.1), custom_call_target="tpu_custom_call" | custom-call | tf_op jit(solution)/shard_map/first/pallas_call | solution.py:424
  1.8 3.4 %collective-permute-start = (bf16[128,256]{1,0:T(8,128)(2,1)S(1)}, bf16[128,256]{1,0:T(8,128)(2,1)S(1)}, u32[]{:S(2)}, u32[]{:S(2)}) collective-permute-start(bf16[128,256]{1,0:T(8,128)(2,1)S(1)} %get-tuple-element.26.refs_7_), channel_id=1, source_target_pairs={{0,28},{4,8},{8,4},{12,16},{16,12},{20,24},{24,20},{28,0},{1,29},{... | collective-permute-start | bytes 196616 | tf_op jit(solution)/shard_map/ppermute | solution.py:443
  5.2 0.0 collective-permute-start.1
  5.2 0.0 copy-start.5
  5.2 0.0 copy-start
  5.2 0.0 copy-start.2
  5.2 0.0 copy-start.3
  5.2 0.0 copy-start.4
  5.3 0.0 copy-start.6
  5.3 0.0 copy-start.7
  5.3 1.9 %inner.1 = (bf16[256,4096]{1,0:T(8,128)(2,1)S(1)}, f32[144,256]{1,0:T(8,128)S(1)}, bf16[256,1024]{1,0:T(8,128)(2,1)S(1)}, bf16[256,256]{1,0:T(8,128)(2,1)S(1)}) custom-call(bf16[4,256,8,128]{3,2,1,0:T(8,128)(2,1)S(1)} %get-tuple-element.21.refs_0_, bf16[144,4096]{1,0:T(8,128)(2,1)S(1)} %get-tuple-element.22.refs_1_, ...), custom_call_target="tpu_custom_call" | custom-call | flops 452984832 | bytes 4194304 | tf_op jit(solution)/shard_map/inner/pallas_call | solution.py:424
  7.2 0.0 collective-permute-done.refs_1_.refs_9_
  7.2 0.0 collective-permute-done.1.refs_2_.refs_8_
  7.2 0.0 copy-done.5
  7.2 0.2 %merge.1 = (bf16[112,256]{1,0:T(8,128)(2,1)S(1)}, bf16[112,256]{1,0:T(8,128)(2,1)S(1)}, bf16[112,256]{1,0:T(8,128)(2,1)S(1)}, bf16[112,256]{1,0:T(8,128)(2,1)S(1)}) custom-call(f32[144,256]{1,0:T(8,128)S(1)} %get-tuple-element.25.refs_0_, bf16[128,256]{1,0:T(8,128)(2,1)S(1)} %collective-permute-done.refs_1_.refs_9_, ...), custom_call_target="tpu_custom_call" | custom-call | tf_op jit(solution)/shard_map/merge/pallas_call | solution.py:424
  7.4 2.9 %collective-permute-start.2 = (bf16[112,256]{1,0:T(8,128)(2,1)S(1)}, bf16[112,256]{1,0:T(8,128)(2,1)S(1)}, u32[]{:S(2)}, u32[]{:S(2)}) collective-permute-start(bf16[112,256]{1,0:T(8,128)(2,1)S(1)} %get-tuple-element.29), channel_id=1, source_target_pairs={{0,1},{1,3},{2,0},{3,2},{4,5},{5,7},{6,4},{7,6},{8,9},{9,11},{10,8... | collective-permute-start | bytes 172040 | tf_op jit(solution)/shard_map/ppermute | solution.py:490
  10.3 2.5 %collective-permute-start.3 = (bf16[112,256]{1,0:T(8,128)(2,1)S(1)}, bf16[112,256]{1,0:T(8,128)(2,1)S(1)}, u32[]{:S(2)}, u32[]{:S(2)}) collective-permute-start(bf16[112,256]{1,0:T(8,128)(2,1)S(1)} %get-tuple-element.30), channel_id=1, source_target_pairs={{0,3},{1,2},{2,1},{3,0},{4,7},{5,6},{6,5},{7,4},{8,11},{9,10},{10,... | collective-permute-start | bytes 172040 | tf_op jit(solution)/shard_map/ppermute | solution.py:490
  12.8 1.6 %collective-permute-start.4 = (bf16[112,256]{1,0:T(8,128)(2,1)S(1)}, bf16[112,256]{1,0:T(8,128)(2,1)S(1)}, u32[]{:S(2)}, u32[]{:S(2)}) collective-permute-start(bf16[112,256]{1,0:T(8,128)(2,1)S(1)} %get-tuple-element.31), channel_id=1, source_target_pairs={{0,2},{1,0},{2,3},{3,1},{4,6},{5,4},{6,7},{7,5},{8,10},{9,8},{10,1... | collective-permute-start | bytes 172040 | tf_op jit(solution)/shard_map/ppermute | solution.py:490
  14.4 0.0 copy-done
  14.4 0.0 copy-done.2
  14.4 0.0 copy-done.3
  14.4 0.0 copy-done.4
  14.4 0.0 copy-done.6
  14.4 0.0 copy-done.7
  14.4 0.0 copy-start.1
  14.4 2.1 %local.1 = (f32[256,4096]{1,0:T(8,128)S(1)}, bf16[384,256]{1,0:T(8,128)(2,1)S(1)}) custom-call(bf16[256,4096]{1,0:T(8,128)(2,1)S(1)} %get-tuple-element.32.refs_0_, bf16[256,1024]{1,0:T(8,128)(2,1)S(1)} %get-tuple-element.33.refs_1_, bf16[256,256]{1,0:T(8,128)(2,1)S(1)} %get-tuple-element.34.refs_2_, bf16[1024,256]{1,0:T(8,128)(2,1)S(1)} %get-tuple-element.24.refs_3_, ...), custom_call_target="tpu_custom_call" | custom-call | flops 1073741824 | bytes 8388608 | tf_op jit(solution)/shard_map/local/pallas_call | solution.py:424
  16.6 0.0 collective-permute-done.2.refs_1_
  16.6 0.0 collective-permute-done.3.refs_2_
  16.6 0.4 %collective-permute-done.4.refs_3_ = bf16[112,256]{1,0:T(8,128)(2,1)S(1)} collective-permute-done((bf16[112,256]{1,0:T(8,128)(2,1)S(1)}, bf16[112,256]{1,0:T(8,128)(2,1)S(1)}, u32[]{:S(2)}, u32[]{:S(2)}) %collective-permute-start.4) | collective-permute-done | bytes 57376 | tf_op jit(solution)/shard_map/ppermute | solution.py:490
  17.0 0.0 copy-done.1
  17.0 2.4 %last.1 = bf16[256,32,128]{2,1,0:T(8,128)(2,1)} custom-call(bf16[112,256]{1,0:T(8,128)(2,1)S(1)} %get-tuple-element.28.refs_0_, bf16[112,256]{1,0:T(8,128)(2,1)S(1)} %collective-permute-done.2.refs_1_, bf16[112,256]{1,0:T(8,128)(2,1)S(1)} %collective-permute-done.3.refs_2_, bf16[112,256]{1,0:T(8,128)(2,1)S(1)} %collective-permute-done.4.refs_3_, ...), custom_call_target="tpu_custom_call" | custom-call | tf_op jit(solution)/shard_map/last/pallas_call | solution.py:424
Async XLA Ops:
  1.8 5.4 %collective-permute-start = (bf16[128,256]{1,0:T(8,128)(2,1)S(1)}, bf16[128,256]{1,0:T(8,128)(2,1)S(1)}, u32[]{:S(2)}, u32[]{:S(2)}) collective-permute-start(bf16[128,256]{1,0:T(8,128)(2,1)S(1)} %get-tuple-element.26.refs_7_), channel_id=1, source_target_pairs={{0,28},{4,8},{8,4},{12,16},{16,12},{20,24},{24,20},{28,0},{1,29},{... | collective-permute-start | bytes 196616 | tf_op jit(solution)/shard_map/ppermute | solution.py:443
  5.2 2.0 %collective-permute-start.1 = (bf16[128,256]{1,0:T(8,128)(2,1)S(1)}, bf16[128,256]{1,0:T(8,128)(2,1)S(1)}, u32[]{:S(2)}, u32[]{:S(2)}) collective-permute-start(bf16[128,256]{1,0:T(8,128)(2,1)S(1)} %get-tuple-element.27.refs_6_), channel_id=1, source_target_pairs={{0,4},{4,0},{8,12},{12,8},{16,20},{20,16},{24,28},{28,24},{1,5},{5... | collective-permute-start | bytes 196616 | tf_op jit(solution)/shard_map/ppermute | solution.py:443
  5.2 2.0 %copy-start.5 = (bf16[144,256]{1,0:T(8,128)(2,1)S(1)}, bf16[144,256]{1,0:T(8,128)(2,1)}, u32[]{:S(2)}) copy-start(bf16[144,256]{1,0:T(8,128)(2,1)} %constant.12.clone.refs_3_) | copy-start | bytes 221188
  5.2 9.2 %copy-start = (bf16[4,256,256]{2,1,0:T(8,128)(2,1)S(1)}, bf16[4,256,256]{2,1,0:T(8,128)(2,1)}, u32[]{:S(2)}) copy-start(bf16[4,256,256]{2,1,0:T(8,128)(2,1)} %refs_4_.3) | copy-start | bytes 1572868
  5.2 9.2 %copy-start.2 = (bf16[256,512]{1,0:T(8,128)(2,1)S(1)}, bf16[256,512]{1,0:T(8,128)(2,1)}, u32[]{:S(2)}) copy-start(bf16[256,512]{1,0:T(8,128)(2,1)} %constant.15.clone.refs_12_) | copy-start | bytes 786436
  5.2 9.2 %copy-start.3 = (bf16[256,512]{1,0:T(8,128)(2,1)S(1)}, bf16[256,512]{1,0:T(8,128)(2,1)}, u32[]{:S(2)}) copy-start(bf16[256,512]{1,0:T(8,128)(2,1)} %constant.16.clone.refs_13_) | copy-start | bytes 786436
  5.2 9.2 %copy-start.4 = (bf16[256,256]{1,0:T(8,128)(2,1)S(1)}, bf16[256,256]{1,0:T(8,128)(2,1)}, u32[]{:S(2)}) copy-start(bf16[256,256]{1,0:T(8,128)(2,1)} %constant.14.clone.refs_11_) | copy-start | bytes 393220
  5.3 9.2 %copy-start.6 = (bf16[128,256]{1,0:T(8,128)(2,1)S(1)}, bf16[128,256]{1,0:T(8,128)(2,1)}, u32[]{:S(2)}) copy-start(bf16[128,256]{1,0:T(8,128)(2,1)} %constant.13.clone.refs_10_) | copy-start | bytes 196612
  5.3 9.2 %copy-start.7 = (bf16[64,64]{1,0:T(8,128)(2,1)S(1)}, bf16[64,64]{1,0:T(8,128)(2,1)}, u32[]{:S(2)}) copy-start(bf16[64,64]{1,0:T(8,128)(2,1)} %refs_5_.1) | copy-start | bytes 24580
  7.4 9.2 %collective-permute-start.2 = (bf16[112,256]{1,0:T(8,128)(2,1)S(1)}, bf16[112,256]{1,0:T(8,128)(2,1)S(1)}, u32[]{:S(2)}, u32[]{:S(2)}) collective-permute-start(bf16[112,256]{1,0:T(8,128)(2,1)S(1)} %get-tuple-element.29), channel_id=1, source_target_pairs={{0,1},{1,3},{2,0},{3,2},{4,5},{5,7},{6,4},{7,6},{8,9},{9,11},{10,8... | collective-permute-start | bytes 172040 | tf_op jit(solution)/shard_map/ppermute | solution.py:490
  10.3 6.2 %collective-permute-start.3 = (bf16[112,256]{1,0:T(8,128)(2,1)S(1)}, bf16[112,256]{1,0:T(8,128)(2,1)S(1)}, u32[]{:S(2)}, u32[]{:S(2)}) collective-permute-start(bf16[112,256]{1,0:T(8,128)(2,1)S(1)} %get-tuple-element.30), channel_id=1, source_target_pairs={{0,3},{1,2},{2,1},{3,0},{4,7},{5,6},{6,5},{7,4},{8,11},{9,10},{10,... | collective-permute-start | bytes 172040 | tf_op jit(solution)/shard_map/ppermute | solution.py:490
  12.8 4.2 %collective-permute-start.4 = (bf16[112,256]{1,0:T(8,128)(2,1)S(1)}, bf16[112,256]{1,0:T(8,128)(2,1)S(1)}, u32[]{:S(2)}, u32[]{:S(2)}) collective-permute-start(bf16[112,256]{1,0:T(8,128)(2,1)S(1)} %get-tuple-element.31), channel_id=1, source_target_pairs={{0,2},{1,0},{2,3},{3,1},{4,6},{5,4},{6,7},{7,5},{8,10},{9,8},{10,1... | collective-permute-start | bytes 172040 | tf_op jit(solution)/shard_map/ppermute | solution.py:490
  14.4 2.6 %copy-start.1 = (bf16[256,4096]{1,0:T(8,128)(2,1)S(1)}, bf16[256,4096]{1,0:T(8,128)(2,1)}, u32[]{:S(2)}) copy-start(bf16[256,4096]{1,0:T(8,128)(2,1)} %constant.17.clone.refs_6_) | copy-start | bytes 6291460

commit v6 on v5

--- a/solution.py
+++ b/solution.py
@@ -27,7 +27,7 @@
 
 def routes(count):
     if count == 4:
-        return [(1, 3, 0, 2), (3, 2, 1, 0), (2, 0, 3, 1)]
+        return [(2, 3, 1, 0), (3, 2, 0, 1), (1, 0, 3, 2)]
     return [[(i + d) % count for i in range(count)] for d in range(1, count)]
 
 
@@ -270,10 +270,9 @@
 
 def merge_kernel(plan, count, own_ref, b_ref, a_ref, merge_ref, right_ref, *out_refs):
     even = lax.rem(lax.axis_index("gx"), 2) == 0
-    size = plan.row_size
     a, b = a_ref[...], b_ref[...]
     before, after = jnp.where(even, b, a), jnp.where(even, a, b)
-    total32 = own_ref[...] + dot(merge_ref[:, :size], before) + dot(merge_ref[:, size:], after)
+    total32 = own_ref[...] + dot(merge_ref[...], jnp.concatenate([before, after], axis=0))
     total = total32.astype(BF16)
     right_ref[...] = total[: plan.message]
     row = lax.broadcasted_iota(jnp.int32, (plan.edge_size, total.shape[1]), 0)
@@ -363,39 +362,40 @@
         spread_ref[pl.ds(d * cells3, cells3), block:] = keep
 
 
-def last_kernel(plan, count, *refs):
-    steps = routes(count)
-    own_ref, *in_refs = refs[: 1 + len(steps)]
-    v_ref, spread_ref, final_ref, base_ref, out_ref, nat, buf, sem = refs[1 + len(steps) :]
+def column_parts(plan, count, messages, first, v_ref, spread_ref):
+    width = v_ref.shape[1]
+    block, cells3 = plan.block, plan.cells3
+    z = lax.axis_index("gy")
+    level3 = jnp.concatenate([message[:cells3] for message in messages], axis=0)
+    mixed = (dot_nt(v_ref[3], level3) * (1 / 1.5**3)).astype(BF16)
+    carry = dot(mixed, spread_ref[pl.ds(first * cells3, len(messages) * cells3), :])
+    carry = (carry[:, :block] + carry[:, block:]) * (1 / 1.5**3)
+    left = jnp.zeros((plan.edge_size, width), F32)
+    right = jnp.zeros((plan.edge_size, width), F32)
+    for d, message in enumerate(messages, first):
+        source, edge = source_of(z, count, d), message[plan.edge :].astype(F32)
+        if d == 0:
+            right = right + edge
+        else:
+            left = left + jnp.where((source == z - 1) & (z > 0), edge, 0.0)
+            right = right + jnp.where(source == z + 1, edge, 0.0)
+    right = jnp.where(z < count - 1, right, 0.0)
+    edges = jnp.concatenate([left, right], axis=0).astype(BF16)
+    one = dot_nt(v_ref[1], edges) * (1 / 1.5**2)
+    two = dot_nt(v_ref[2], edges) * (1 / 1.5**4)
+    return jnp.concatenate([carry, one, two], axis=1)
+
+
+def gather_kernel(plan, count, *refs):
+    *message_refs, v_ref, spread_ref, parts_ref = refs
+    parts_ref[...] = column_parts(plan, count, [ref[...] for ref in message_refs], 0, v_ref, spread_ref)
+
+
+def last_kernel(plan, count, in_ref, parts_ref, v_ref, spread_ref, final_ref, base_ref, out_ref, nat, buf, sem):
     rows, cols = plan.rows, plan.cols
     width = v_ref.shape[1]
-    block = plan.block
-    z = lax.axis_index("gy")
-    messages = [own_ref[...]]
-    for d in range(1, count):
-        step_of = [got[d - 1][0] for got in arrivals(count)]
-        message = None
-        for step in sorted(set(step_of)):
-            value = in_refs[step][...]
-            mine = chosen(z, [int(s == step) for s in step_of]) == 1
-            message = value if message is None else jnp.where(mine, value, message)
-        messages.append(message)
-    level3 = jnp.concatenate([message[: plan.cells3] for message in messages], axis=0)
-    mixed = (dot_nt(v_ref[3], level3) * (1 / 1.5**3)).astype(BF16)
-    carry = dot(mixed, spread_ref[...])
-    carry = (carry[:, :block] + carry[:, block:]) * (1 / 1.5**3)
-    left = jnp.zeros((plan.edge_size, width), F32)
-    right = own_ref[plan.edge :].astype(F32)
-    for d in range(1, count):
-        source, edge = source_of(z, count, d), messages[d][plan.edge :].astype(F32)
-        left = left + jnp.where((source == z - 1) & (z > 0), edge, 0.0)
-        right = right + jnp.where((source == z + 1) & (z < count - 1), edge, 0.0)
-    left = left.astype(BF16)
-    right = jnp.where(z < count - 1, right, 0.0).astype(BF16)
-    edges = jnp.concatenate([left, right], axis=0)
-    one = dot_nt(v_ref[1], edges) * (1 / 1.5**2)
-    two = dot_nt(v_ref[2], edges) * (1 / 1.5**4)
-    parts = jnp.concatenate([carry, one, two], axis=1).astype(BF16)
+    parts = column_parts(plan, count, [in_ref[...]], count - 1, v_ref, spread_ref)
+    parts = (parts + parts_ref[...]).astype(BF16)
     copies = []
     for h in range(rows // PART):
         for x in range(0, PART, 2):
@@ -403,10 +403,17 @@
             total = base_ref[:, lanes] + dot(parts, final_ref[:, lanes])
             nat[h, pl.ds(x, width, stride=PART), :] = total[:, :cols]
             nat[h, pl.ds(x + 1, width, stride=PART), :] = total[:, cols:]
-        buf[h] = nat[h].reshape(width, PART, cols).astype(BF16)
-        copy = pltpu.make_async_copy(buf.at[h], out_ref.at[:, pl.ds(h * PART, PART), :], sem.at[h])
-        copy.start()
-        copies.append(copy)
+        pieces = CHUNKS if h == rows // PART - 1 else 1
+        part = width // pieces
+        for i in range(pieces):
+            fields = pl.ds(i * part, part)
+            found = nat[h, pl.ds(i * part * PART, part * PART), :]
+            buf[h, fields] = found.reshape(part, PART, cols).astype(BF16)
+            copy = pltpu.make_async_copy(
+                buf.at[h, fields], out_ref.at[fields, pl.ds(h * PART, PART), :], sem.at[h + i]
+            )
+            copy.start()
+            copies.append(copy)
     for copy in copies:
         copy.wait()
 
@@ -499,14 +506,20 @@
             name="local",
             cost=pl.CostEstimate(flops=4 * width * width * size, bytes_accessed=8 * 1024 * 1024, transcendentals=0),
         )
+        (partial,) = call(
+            lambda *refs: gather_kernel(plan, along, *refs),
+            [right, *arrived[:-1], vertical, spread],
+            [((width, plan.final_size), F32)],
+            name="gather",
+        )
         (out,) = call(
             lambda *refs: last_kernel(plan, along, *refs),
-            [right, *arrived, vertical, spread, const(plan.final), base],
+            [arrived[-1], partial, vertical, spread, const(plan.final), base],
             [((width, rows, cols), BF16)],
             [
                 VMEM((parts, width * PART, cols), F32),
                 VMEM((parts, width, PART, cols), BF16),
-                pltpu.SemaphoreType.DMA((parts,)),
+                pltpu.SemaphoreType.DMA((parts + CHUNKS - 1,)),
             ],
             any_out=(0,),
             name="last",

time: 19.6 us -> 19.5 us (level)
  starting transfers between devices: 10.4 us -> 8.94 us
  waiting for transfers between devices: 0.43 us -> 1.47 us
  Pallas kernels: 8.39 us -> 8.77 us
    ppermute x3, starting transfers between devices: 7 us -> 5.54 us  [on_device(): lax.ppermute(x, 'gy', list(enumerate(step)))]
    ppermute x3, waiting for transfers between devices: 0.43 us -> 1.47 us  [on_device(): lax.ppermute(x, 'gy', list(enumerate(step)))]
    pallas_call x5 -> x6, Pallas kernels: 8.39 us -> 8.77 us  [call(): pl.pallas_call(kernel, in_specs=specs, out_specs=out_specs, out_shape=out...]
  transfers between devices with their start and end apart: 5 -> 5, of which waited for: 1 -> 2; matrix products, arithmetic and copies ran while one was open for 0% -> 0% of each run, Pallas kernels for 21% -> 23%
where the time goes in v6:
time: 19.5 us; the launch traced here: 19.4 us
  starting transfers between devices  8.94 us (46%)
  Pallas kernels  8.77 us (45%)
  waiting for transfers between devices  1.47 us (8%)
    pallas_call x6, Pallas kernels, call(): pl.pallas_call(kernel, in_specs=specs, out_specs=out_specs, out_shape=out...  8.77 us
    ppermute x3, starting transfers between devices, on_device(): lax.ppermute(x, 'gy', list(enumerate(step)))  5.54 us
    ppermute x2, starting transfers between devices, swap(): return lax.ppermute(x, 'gx', [(i, partner(i)) for i in range(across)])  3.4 us
    ppermute x3, waiting for transfers between devices, on_device(): lax.ppermute(x, 'gy', list(enumerate(step)))  1.47 us
  transfers between devices with their start and end apart: 5, of which 2 were waited for; matrix products, arithmetic and copies ran while one was open for 0% of the time, Pallas kernels for 23%

profile of v6, /device:TPU:0, one launch (start us, length us, event | category | flops | bytes accessed | tf_op | source)
XLA Modules:
  0.0 19.4 jit_solution(16543614390941674125)
XLA Ops:
  0.0 1.8 %first.1 = (bf16[4,256,8,128]{3,2,1,0:T(8,128)(2,1)S(1)}, bf16[128,256]{1,0:T(8,128)(2,1)S(1)}, bf16[128,256]{1,0:T(8,128)(2,1)S(1)}, bf16[144,4096]{1,0:T(8,128...) custom-call(bf16[256,32,128]{2,1,0:T(8,128)(2,1)} %refs_0_.1), custom_call_target="tpu_custom_call" | custom-call | tf_op jit(solution)/shard_map/first/pallas_call | solution.py:431
  1.8 3.4 %collective-permute-start = (bf16[128,256]{1,0:T(8,128)(2,1)S(1)}, bf16[128,256]{1,0:T(8,128)(2,1)S(1)}, u32[]{:S(2)}, u32[]{:S(2)}) collective-permute-start(bf16[128,256]{1,0:T(8,128)(2,1)S(1)} %get-tuple-element.26.refs_7_), channel_id=1, source_target_pairs={{0,28},{4,8},{8,4},{12,16},{16,12},{20,24},{24,20},{28,0},{1,29},{... | collective-permute-start | bytes 196616 | tf_op jit(solution)/shard_map/ppermute | solution.py:450
  5.2 0.0 collective-permute-start.1
  5.2 0.0 copy-start.5
  5.2 0.0 copy-start
  5.2 0.0 copy-start.2
  5.2 0.0 copy-start.3
  5.2 0.0 copy-start.4
  5.3 0.0 copy-start.6
  5.3 0.0 copy-start.7
  5.3 1.9 %inner.1 = (bf16[256,4096]{1,0:T(8,128)(2,1)S(1)}, f32[144,256]{1,0:T(8,128)S(1)}, bf16[256,1024]{1,0:T(8,128)(2,1)S(1)}, bf16[256,256]{1,0:T(8,128)(2,1)S(1)}) custom-call(bf16[4,256,8,128]{3,2,1,0:T(8,128)(2,1)S(1)} %get-tuple-element.21.refs_0_, bf16[144,4096]{1,0:T(8,128)(2,1)S(1)} %get-tuple-element.22.refs_1_, ...), custom_call_target="tpu_custom_call" | custom-call | flops 452984832 | bytes 4194304 | tf_op jit(solution)/shard_map/inner/pallas_call | solution.py:431
  7.2 0.0 collective-permute-done.refs_1_.refs_9_
  7.2 0.0 collective-permute-done.1.refs_2_.refs_8_
  7.2 0.0 copy-done.5
  7.2 0.2 %merge.1 = (bf16[112,256]{1,0:T(8,128)(2,1)S(1)}, bf16[112,256]{1,0:T(8,128)(2,1)S(1)}, bf16[112,256]{1,0:T(8,128)(2,1)S(1)}, bf16[112,256]{1,0:T(8,128)(2,1)S(1)}) custom-call(f32[144,256]{1,0:T(8,128)S(1)} %get-tuple-element.25.refs_0_, bf16[128,256]{1,0:T(8,128)(2,1)S(1)} %collective-permute-done.refs_1_.refs_9_, ...), custom_call_target="tpu_custom_call" | custom-call | tf_op jit(solution)/shard_map/merge/pallas_call | solution.py:431
  7.4 4.0 %collective-permute-start.3 = (bf16[112,256]{1,0:T(8,128)(2,1)S(1)}, bf16[112,256]{1,0:T(8,128)(2,1)S(1)}, u32[]{:S(2)}, u32[]{:S(2)}) collective-permute-start(bf16[112,256]{1,0:T(8,128)(2,1)S(1)} %get-tuple-element.30), channel_id=1, source_target_pairs={{0,2},{1,3},{2,1},{3,0},{4,6},{5,7},{6,5},{7,4},{8,10},{9,11},{10,... | collective-permute-start | bytes 172040 | tf_op jit(solution)/shard_map/ppermute | solution.py:497
  11.3 1.1 %collective-permute-start.4 = (bf16[112,256]{1,0:T(8,128)(2,1)S(1)}, bf16[112,256]{1,0:T(8,128)(2,1)S(1)}, u32[]{:S(2)}, u32[]{:S(2)}) collective-permute-start(bf16[112,256]{1,0:T(8,128)(2,1)S(1)} %get-tuple-element.31), channel_id=1, source_target_pairs={{0,3},{1,2},{2,0},{3,1},{4,7},{5,6},{6,4},{7,5},{8,11},{9,10},{10,... | collective-permute-start | bytes 172040 | tf_op jit(solution)/shard_map/ppermute | solution.py:497
  12.4 0.5 %collective-permute-start.2 = (bf16[112,256]{1,0:T(8,128)(2,1)S(1)}, bf16[112,256]{1,0:T(8,128)(2,1)S(1)}, u32[]{:S(2)}, u32[]{:S(2)}) collective-permute-start(bf16[112,256]{1,0:T(8,128)(2,1)S(1)} %get-tuple-element.28), channel_id=1, source_target_pairs={{0,1},{1,0},{2,3},{3,2},{4,5},{5,4},{6,7},{7,6},{8,9},{9,8},{10,11... | collective-permute-start | bytes 172040 | tf_op jit(solution)/shard_map/ppermute | solution.py:497
  12.9 0.0 copy-done
  12.9 0.0 copy-done.2
  12.9 0.0 copy-done.3
  12.9 0.0 copy-done.4
  12.9 0.0 copy-done.6
  12.9 0.0 copy-done.7
  13.0 0.0 copy-start.1
  13.0 2.1 %local.1 = (f32[256,4096]{1,0:T(8,128)S(1)}, bf16[384,256]{1,0:T(8,128)(2,1)S(1)}) custom-call(bf16[256,4096]{1,0:T(8,128)(2,1)S(1)} %get-tuple-element.32.refs_0_, bf16[256,1024]{1,0:T(8,128)(2,1)S(1)} %get-tuple-element.33.refs_1_, bf16[256,256]{1,0:T(8,128)(2,1)S(1)} %get-tuple-element.34.refs_2_, bf16[1024,256]{1,0:T(8,128)(2,1)S(1)} %get-tuple-element.24.refs_3_, ...), custom_call_target="tpu_custom_call" | custom-call | flops 1073741824 | bytes 8388608 | tf_op jit(solution)/shard_map/local/pallas_call | solution.py:431
  15.1 0.0 collective-permute-done.3.refs_1_
  15.1 1.4 %collective-permute-done.4.refs_2_ = bf16[112,256]{1,0:T(8,128)(2,1)S(1)} collective-permute-done((bf16[112,256]{1,0:T(8,128)(2,1)S(1)}, bf16[112,256]{1,0:T(8,128)(2,1)S(1)}, u32[]{:S(2)}, u32[]{:S(2)}) %collective-permute-start.4) | collective-permute-done | bytes 57376 | tf_op jit(solution)/shard_map/ppermute | solution.py:497
  16.5 0.5 %gather.1.refs_1_ = f32[256,256]{1,0:T(8,128)S(1)} custom-call(bf16[112,256]{1,0:T(8,128)(2,1)S(1)} %get-tuple-element.29.refs_0_, bf16[112,256]{1,0:T(8,128)(2,1)S(1)} %collective-permute-done.3.refs_1_, bf16[112,256]{1,0:T(8,128)(2,1)S(1)} %collective-permute-done.4.refs_2_, bf16[4,256,256]{2,1,0:T(8,128)(2,1)S(1)} %copy-done, ...), custom_call_target="tpu_custom_call" | custom-call | tf_op jit(solution)/shard_map/gather/pallas_call | solution.py:431
  16.9 0.1 collective-permute-done.2.refs_0_
  17.0 0.0 copy-done.1
  17.0 2.3 %last.1 = bf16[256,32,128]{2,1,0:T(8,128)(2,1)} custom-call(bf16[112,256]{1,0:T(8,128)(2,1)S(1)} %collective-permute-done.2.refs_0_, f32[256,256]{1,0:T(8,128)S(1)} %gather.1.refs_1_, bf16[4,256,256]{2,1,0:T(8,128)(2,1)S(1)} %copy-done, bf16[384,256]{1,0:T(8,128)(2,1)S(1)} %get-tuple-element.35.refs_4_.refs_3_, bf16[256,4096]{1,0:T(8,128)(2,1)S(1)} %copy-done.1, ...), custom_call_target="tpu_custom_call" | custom-call | tf_op jit(solution)/shard_map/last/pallas_call | solution.py:431
Async XLA Ops:
  1.8 5.4 %collective-permute-start = (bf16[128,256]{1,0:T(8,128)(2,1)S(1)}, bf16[128,256]{1,0:T(8,128)(2,1)S(1)}, u32[]{:S(2)}, u32[]{:S(2)}) collective-permute-start(bf16[128,256]{1,0:T(8,128)(2,1)S(1)} %get-tuple-element.26.refs_7_), channel_id=1, source_target_pairs={{0,28},{4,8},{8,4},{12,16},{16,12},{20,24},{24,20},{28,0},{1,29},{... | collective-permute-start | bytes 196616 | tf_op jit(solution)/shard_map/ppermute | solution.py:450
  5.2 2.0 %collective-permute-start.1 = (bf16[128,256]{1,0:T(8,128)(2,1)S(1)}, bf16[128,256]{1,0:T(8,128)(2,1)S(1)}, u32[]{:S(2)}, u32[]{:S(2)}) collective-permute-start(bf16[128,256]{1,0:T(8,128)(2,1)S(1)} %get-tuple-element.27.refs_6_), channel_id=1, source_target_pairs={{0,4},{4,0},{8,12},{12,8},{16,20},{20,16},{24,28},{28,24},{1,5},{5... | collective-permute-start | bytes 196616 | tf_op jit(solution)/shard_map/ppermute | solution.py:450
  5.2 2.0 %copy-start.5 = (bf16[144,256]{1,0:T(8,128)(2,1)S(1)}, bf16[144,256]{1,0:T(8,128)(2,1)}, u32[]{:S(2)}) copy-start(bf16[144,256]{1,0:T(8,128)(2,1)} %constant.12.clone.refs_3_) | copy-start | bytes 221188
  5.2 7.7 %copy-start = (bf16[4,256,256]{2,1,0:T(8,128)(2,1)S(1)}, bf16[4,256,256]{2,1,0:T(8,128)(2,1)}, u32[]{:S(2)}) copy-start(bf16[4,256,256]{2,1,0:T(8,128)(2,1)} %refs_2_.1) | copy-start | bytes 1572868
  5.2 7.7 %copy-start.2 = (bf16[256,512]{1,0:T(8,128)(2,1)S(1)}, bf16[256,512]{1,0:T(8,128)(2,1)}, u32[]{:S(2)}) copy-start(bf16[256,512]{1,0:T(8,128)(2,1)} %constant.15.clone.refs_12_) | copy-start | bytes 786436
  5.2 7.7 %copy-start.3 = (bf16[256,512]{1,0:T(8,128)(2,1)S(1)}, bf16[256,512]{1,0:T(8,128)(2,1)}, u32[]{:S(2)}) copy-start(bf16[256,512]{1,0:T(8,128)(2,1)} %constant.16.clone.refs_13_) | copy-start | bytes 786436
  5.2 7.7 %copy-start.4 = (bf16[256,256]{1,0:T(8,128)(2,1)S(1)}, bf16[256,256]{1,0:T(8,128)(2,1)}, u32[]{:S(2)}) copy-start(bf16[256,256]{1,0:T(8,128)(2,1)} %constant.14.clone.refs_11_) | copy-start | bytes 393220
  5.3 7.7 %copy-start.6 = (bf16[128,256]{1,0:T(8,128)(2,1)S(1)}, bf16[128,256]{1,0:T(8,128)(2,1)}, u32[]{:S(2)}) copy-start(bf16[128,256]{1,0:T(8,128)(2,1)} %constant.13.clone.refs_10_) | copy-start | bytes 196612
  5.3 7.7 %copy-start.7 = (bf16[64,64]{1,0:T(8,128)(2,1)S(1)}, bf16[64,64]{1,0:T(8,128)(2,1)}, u32[]{:S(2)}) copy-start(bf16[64,64]{1,0:T(8,128)(2,1)} %refs_5_.1) | copy-start | bytes 24580
  7.4 7.7 %collective-permute-start.3 = (bf16[112,256]{1,0:T(8,128)(2,1)S(1)}, bf16[112,256]{1,0:T(8,128)(2,1)S(1)}, u32[]{:S(2)}, u32[]{:S(2)}) collective-permute-start(bf16[112,256]{1,0:T(8,128)(2,1)S(1)} %get-tuple-element.30), channel_id=1, source_target_pairs={{0,2},{1,3},{2,1},{3,0},{4,6},{5,7},{6,5},{7,4},{8,10},{9,11},{10,... | collective-permute-start | bytes 172040 | tf_op jit(solution)/shard_map/ppermute | solution.py:497
  11.3 5.1 %collective-permute-start.4 = (bf16[112,256]{1,0:T(8,128)(2,1)S(1)}, bf16[112,256]{1,0:T(8,128)(2,1)S(1)}, u32[]{:S(2)}, u32[]{:S(2)}) collective-permute-start(bf16[112,256]{1,0:T(8,128)(2,1)S(1)} %get-tuple-element.31), channel_id=1, source_target_pairs={{0,3},{1,2},{2,0},{3,1},{4,7},{5,6},{6,4},{7,5},{8,11},{9,10},{10,... | collective-permute-start | bytes 172040 | tf_op jit(solution)/shard_map/ppermute | solution.py:497
  12.4 4.6 %collective-permute-start.2 = (bf16[112,256]{1,0:T(8,128)(2,1)S(1)}, bf16[112,256]{1,0:T(8,128)(2,1)S(1)}, u32[]{:S(2)}, u32[]{:S(2)}) collective-permute-start(bf16[112,256]{1,0:T(8,128)(2,1)S(1)} %get-tuple-element.28), channel_id=1, source_target_pairs={{0,1},{1,0},{2,3},{3,2},{4,5},{5,4},{6,7},{7,6},{8,9},{9,8},{10,11... | collective-permute-start | bytes 172040 | tf_op jit(solution)/shard_map/ppermute | solution.py:497
  13.0 4.1 %copy-start.1 = (bf16[256,4096]{1,0:T(8,128)(2,1)S(1)}, bf16[256,4096]{1,0:T(8,128)(2,1)}, u32[]{:S(2)}) copy-start(bf16[256,4096]{1,0:T(8,128)(2,1)} %constant.17.clone.refs_4_) | copy-start | bytes 6291460

commit v7 on v6

--- a/solution.py
+++ b/solution.py
@@ -268,7 +268,7 @@
     level2[...] = (dot(level1[...], t2_ref[...]) * (1 / 1.5)).astype(BF16)
 
 
-def merge_kernel(plan, count, own_ref, b_ref, a_ref, merge_ref, right_ref, *out_refs):
+def merge_kernel(plan, count, own_ref, a_ref, b_ref, merge_ref, right_ref, *out_refs):
     even = lax.rem(lax.axis_index("gx"), 2) == 0
     a, b = a_ref[...], b_ref[...]
     before, after = jnp.where(even, b, a), jnp.where(even, a, b)
@@ -398,11 +398,10 @@
     parts = (parts + parts_ref[...]).astype(BF16)
     copies = []
     for h in range(rows // PART):
-        for x in range(0, PART, 2):
-            lanes = pl.ds((h * PART + x) * cols, 2 * cols)
-            total = base_ref[:, lanes] + dot(parts, final_ref[:, lanes])
-            nat[h, pl.ds(x, width, stride=PART), :] = total[:, :cols]
-            nat[h, pl.ds(x + 1, width, stride=PART), :] = total[:, cols:]
+        lanes = pl.ds(h * PART * cols, PART * cols)
+        total = base_ref[:, lanes] + dot(parts, final_ref[:, lanes])
+        for x in range(PART):
+            nat[h, pl.ds(x, width, stride=PART), :] = total[:, x * cols : (x + 1) * cols]
         pieces = CHUNKS if h == rows // PART - 1 else 1
         part = width // pieces
         for i in range(pieces):
@@ -490,7 +489,7 @@
         message = ((plan.message, width), BF16)
         right, *messages = call(
             lambda *refs: merge_kernel(plan, along, *refs),
-            [own, recv_b, recv_a, const(plan.merge)],
+            [own, recv_a, recv_b, const(plan.merge)],
             [message] * (1 + len(steps)),
             name="merge",
         )

time: 19.5 us -> 19.7 us (1.010)
  waiting for transfers between devices: 1.47 us -> 2.04 us
  starting transfers between devices: 8.94 us -> 8.51 us
    ppermute x3, starting transfers between devices: 5.54 us -> 4.44 us  [on_device(): lax.ppermute(x, 'gy', list(enumerate(step)))]
    ppermute x2, starting transfers between devices: 3.4 us -> 4.08 us  [swap(): return lax.ppermute(x, 'gx', [(i, partner(i)) for i in range(across)])]
    ppermute x3, waiting for transfers between devices: 1.47 us -> 2.03 us  [on_device(): lax.ppermute(x, 'gy', list(enumerate(step)))]
  transfers between devices with their start and end apart: 5 -> 5, of which waited for: 2 -> 1; matrix products, arithmetic and copies ran while one was open for 0% -> 0% of each run, Pallas kernels for 23% -> 23%
where the time goes in v7:
time: 19.7 us; the launch traced here: 19.5 us
  Pallas kernels  8.78 us (45%)
  starting transfers between devices  8.51 us (43%)
  waiting for transfers between devices  2.04 us (10%)
    pallas_call x6, Pallas kernels, call(): pl.pallas_call(kernel, in_specs=specs, out_specs=out_specs, out_shape=out...  8.78 us
    ppermute x3, starting transfers between devices, on_device(): lax.ppermute(x, 'gy', list(enumerate(step)))  4.44 us
    ppermute x2, starting transfers between devices, swap(): return lax.ppermute(x, 'gx', [(i, partner(i)) for i in range(across)])  4.08 us
    ppermute x3, waiting for transfers between devices, on_device(): lax.ppermute(x, 'gy', list(enumerate(step)))  2.03 us
  transfers between devices with their start and end apart: 5, of which 1 were waited for; matrix products, arithmetic and copies ran while one was open for 0% of the time, Pallas kernels for 23%

profile of v7, /device:TPU:0, one launch (start us, length us, event | category | flops | bytes accessed | tf_op | source)
XLA Modules:
  0.0 19.5 jit_solution(7916490257252791847)
XLA Ops:
  0.0 1.8 %first.1 = (bf16[4,256,8,128]{3,2,1,0:T(8,128)(2,1)S(1)}, bf16[128,256]{1,0:T(8,128)(2,1)S(1)}, bf16[128,256]{1,0:T(8,128)(2,1)S(1)}, bf16[144,4096]{1,0:T(8,128...) custom-call(bf16[256,32,128]{2,1,0:T(8,128)(2,1)} %refs_0_.1), custom_call_target="tpu_custom_call" | custom-call | tf_op jit(solution)/shard_map/first/pallas_call | solution.py:430
  1.8 0.5 %collective-permute-start = (bf16[128,256]{1,0:T(8,128)(2,1)S(1)}, bf16[128,256]{1,0:T(8,128)(2,1)S(1)}, u32[]{:S(2)}, u32[]{:S(2)}) collective-permute-start(bf16[128,256]{1,0:T(8,128)(2,1)S(1)} %get-tuple-element.26.refs_6_), channel_id=1, source_target_pairs={{0,4},{4,0},{8,12},{12,8},{16,20},{20,16},{24,28},{28,24},{1,5},{5... | collective-permute-start | bytes 196616 | tf_op jit(solution)/shard_map/ppermute | solution.py:449
  2.3 3.6 %collective-permute-start.1 = (bf16[128,256]{1,0:T(8,128)(2,1)S(1)}, bf16[128,256]{1,0:T(8,128)(2,1)S(1)}, u32[]{:S(2)}, u32[]{:S(2)}) collective-permute-start(bf16[128,256]{1,0:T(8,128)(2,1)S(1)} %get-tuple-element.27.refs_7_), channel_id=1, source_target_pairs={{0,28},{4,8},{8,4},{12,16},{16,12},{20,24},{24,20},{28,0},{1,29},{... | collective-permute-start | bytes 196616 | tf_op jit(solution)/shard_map/ppermute | solution.py:449
  5.9 0.0 copy-start.5
  5.9 0.0 copy-start
  5.9 0.0 copy-start.2
  5.9 0.0 copy-start.3
  5.9 0.0 copy-start.4
  5.9 0.0 copy-start.6
  5.9 0.0 copy-start.7
  5.9 1.9 %inner.1 = (bf16[256,4096]{1,0:T(8,128)(2,1)S(1)}, f32[144,256]{1,0:T(8,128)S(1)}, bf16[256,1024]{1,0:T(8,128)(2,1)S(1)}, bf16[256,256]{1,0:T(8,128)(2,1)S(1)}) custom-call(bf16[4,256,8,128]{3,2,1,0:T(8,128)(2,1)S(1)} %get-tuple-element.21.refs_0_, bf16[144,4096]{1,0:T(8,128)(2,1)S(1)} %get-tuple-element.22.refs_1_, ...), custom_call_target="tpu_custom_call" | custom-call | flops 452984832 | bytes 4194304 | tf_op jit(solution)/shard_map/inner/pallas_call | solution.py:430
  7.8 0.0 collective-permute-done.refs_1_.refs_8_
  7.8 0.0 collective-permute-done.1.refs_2_.refs_9_
  7.8 0.0 copy-done.5
  7.9 0.2 merge.1
  8.0 2.9 %collective-permute-start.3 = (bf16[112,256]{1,0:T(8,128)(2,1)S(1)}, bf16[112,256]{1,0:T(8,128)(2,1)S(1)}, u32[]{:S(2)}, u32[]{:S(2)}) collective-permute-start(bf16[112,256]{1,0:T(8,128)(2,1)S(1)} %get-tuple-element.30), channel_id=1, source_target_pairs={{0,2},{1,3},{2,1},{3,0},{4,6},{5,7},{6,5},{7,4},{8,10},{9,11},{10,... | collective-permute-start | bytes 172040 | tf_op jit(solution)/shard_map/ppermute | solution.py:496
  10.9 1.1 %collective-permute-start.4 = (bf16[112,256]{1,0:T(8,128)(2,1)S(1)}, bf16[112,256]{1,0:T(8,128)(2,1)S(1)}, u32[]{:S(2)}, u32[]{:S(2)}) collective-permute-start(bf16[112,256]{1,0:T(8,128)(2,1)S(1)} %get-tuple-element.31), channel_id=1, source_target_pairs={{0,3},{1,2},{2,0},{3,1},{4,7},{5,6},{6,4},{7,5},{8,11},{9,10},{10,... | collective-permute-start | bytes 172040 | tf_op jit(solution)/shard_map/ppermute | solution.py:496
  12.0 0.5 %collective-permute-start.2 = (bf16[112,256]{1,0:T(8,128)(2,1)S(1)}, bf16[112,256]{1,0:T(8,128)(2,1)S(1)}, u32[]{:S(2)}, u32[]{:S(2)}) collective-permute-start(bf16[112,256]{1,0:T(8,128)(2,1)S(1)} %get-tuple-element.28), channel_id=1, source_target_pairs={{0,1},{1,0},{2,3},{3,2},{4,5},{5,4},{6,7},{7,6},{8,9},{9,8},{10,11... | collective-permute-start | bytes 172040 | tf_op jit(solution)/shard_map/ppermute | solution.py:496
  12.5 0.0 copy-done
  12.5 0.0 copy-done.2
  12.5 0.0 copy-done.3
  12.5 0.0 copy-done.4
  12.5 0.0 copy-done.6
  12.5 0.0 copy-done.7
  12.5 0.0 copy-start.1
  12.5 2.1 %local.1 = (f32[256,4096]{1,0:T(8,128)S(1)}, bf16[384,256]{1,0:T(8,128)(2,1)S(1)}) custom-call(bf16[256,4096]{1,0:T(8,128)(2,1)S(1)} %get-tuple-element.32.refs_0_, bf16[256,1024]{1,0:T(8,128)(2,1)S(1)} %get-tuple-element.33.refs_1_, bf16[256,256]{1,0:T(8,128)(2,1)S(1)} %get-tuple-element.34.refs_2_, bf16[1024,256]{1,0:T(8,128)(2,1)S(1)} %get-tuple-element.24.refs_3_, ...), custom_call_target="tpu_custom_call" | custom-call | flops 1073741824 | bytes 8388608 | tf_op jit(solution)/shard_map/local/pallas_call | solution.py:430
  14.6 0.0 collective-permute-done.3.refs_1_
  14.6 2.0 %collective-permute-done.4.refs_2_ = bf16[112,256]{1,0:T(8,128)(2,1)S(1)} collective-permute-done((bf16[112,256]{1,0:T(8,128)(2,1)S(1)}, bf16[112,256]{1,0:T(8,128)(2,1)S(1)}, u32[]{:S(2)}, u32[]{:S(2)}) %collective-permute-start.4) | collective-permute-done | bytes 57376 | tf_op jit(solution)/shard_map/ppermute | solution.py:496
  16.7 0.5 %gather.1.refs_1_ = f32[256,256]{1,0:T(8,128)S(1)} custom-call(bf16[112,256]{1,0:T(8,128)(2,1)S(1)} %get-tuple-element.29.refs_0_, bf16[112,256]{1,0:T(8,128)(2,1)S(1)} %collective-permute-done.3.refs_1_, bf16[112,256]{1,0:T(8,128)(2,1)S(1)} %collective-permute-done.4.refs_2_, bf16[4,256,256]{2,1,0:T(8,128)(2,1)S(1)} %copy-done, ...), custom_call_target="tpu_custom_call" | custom-call | tf_op jit(solution)/shard_map/gather/pallas_call | solution.py:430
  17.2 0.0 collective-permute-done.2.refs_0_
  17.2 0.0 copy-done.1
  17.2 2.3 %last.1 = bf16[256,32,128]{2,1,0:T(8,128)(2,1)} custom-call(bf16[112,256]{1,0:T(8,128)(2,1)S(1)} %collective-permute-done.2.refs_0_, f32[256,256]{1,0:T(8,128)S(1)} %gather.1.refs_1_, bf16[4,256,256]{2,1,0:T(8,128)(2,1)S(1)} %copy-done, bf16[384,256]{1,0:T(8,128)(2,1)S(1)} %get-tuple-element.35.refs_4_.refs_3_, bf16[256,4096]{1,0:T(8,128)(2,1)S(1)} %copy-done.1, ...), custom_call_target="tpu_custom_call" | custom-call | tf_op jit(solution)/shard_map/last/pallas_call | solution.py:430
Async XLA Ops:
  1.8 6.0 %collective-permute-start = (bf16[128,256]{1,0:T(8,128)(2,1)S(1)}, bf16[128,256]{1,0:T(8,128)(2,1)S(1)}, u32[]{:S(2)}, u32[]{:S(2)}) collective-permute-start(bf16[128,256]{1,0:T(8,128)(2,1)S(1)} %get-tuple-element.26.refs_6_), channel_id=1, source_target_pairs={{0,4},{4,0},{8,12},{12,8},{16,20},{20,16},{24,28},{28,24},{1,5},{5... | collective-permute-start | bytes 196616 | tf_op jit(solution)/shard_map/ppermute | solution.py:449
  2.3 5.5 %collective-permute-start.1 = (bf16[128,256]{1,0:T(8,128)(2,1)S(1)}, bf16[128,256]{1,0:T(8,128)(2,1)S(1)}, u32[]{:S(2)}, u32[]{:S(2)}) collective-permute-start(bf16[128,256]{1,0:T(8,128)(2,1)S(1)} %get-tuple-element.27.refs_7_), channel_id=1, source_target_pairs={{0,28},{4,8},{8,4},{12,16},{16,12},{20,24},{24,20},{28,0},{1,29},{... | collective-permute-start | bytes 196616 | tf_op jit(solution)/shard_map/ppermute | solution.py:449
  5.9 2.0 %copy-start.5 = (bf16[144,256]{1,0:T(8,128)(2,1)S(1)}, bf16[144,256]{1,0:T(8,128)(2,1)}, u32[]{:S(2)}) copy-start(bf16[144,256]{1,0:T(8,128)(2,1)} %constant.12.clone.refs_3_) | copy-start | bytes 221188
  5.9 6.6 %copy-start = (bf16[4,256,256]{2,1,0:T(8,128)(2,1)S(1)}, bf16[4,256,256]{2,1,0:T(8,128)(2,1)}, u32[]{:S(2)}) copy-start(bf16[4,256,256]{2,1,0:T(8,128)(2,1)} %refs_2_.1) | copy-start | bytes 1572868
  5.9 6.6 %copy-start.2 = (bf16[256,512]{1,0:T(8,128)(2,1)S(1)}, bf16[256,512]{1,0:T(8,128)(2,1)}, u32[]{:S(2)}) copy-start(bf16[256,512]{1,0:T(8,128)(2,1)} %constant.15.clone.refs_12_) | copy-start | bytes 786436
  5.9 6.6 %copy-start.3 = (bf16[256,512]{1,0:T(8,128)(2,1)S(1)}, bf16[256,512]{1,0:T(8,128)(2,1)}, u32[]{:S(2)}) copy-start(bf16[256,512]{1,0:T(8,128)(2,1)} %constant.16.clone.refs_13_) | copy-start | bytes 786436
  5.9 6.6 %copy-start.4 = (bf16[256,256]{1,0:T(8,128)(2,1)S(1)}, bf16[256,256]{1,0:T(8,128)(2,1)}, u32[]{:S(2)}) copy-start(bf16[256,256]{1,0:T(8,128)(2,1)} %constant.14.clone.refs_11_) | copy-start | bytes 393220
  5.9 6.6 %copy-start.6 = (bf16[128,256]{1,0:T(8,128)(2,1)S(1)}, bf16[128,256]{1,0:T(8,128)(2,1)}, u32[]{:S(2)}) copy-start(bf16[128,256]{1,0:T(8,128)(2,1)} %constant.13.clone.refs_10_) | copy-start | bytes 196612
  5.9 6.6 %copy-start.7 = (bf16[64,64]{1,0:T(8,128)(2,1)S(1)}, bf16[64,64]{1,0:T(8,128)(2,1)}, u32[]{:S(2)}) copy-start(bf16[64,64]{1,0:T(8,128)(2,1)} %refs_5_.1) | copy-start | bytes 24580
  8.0 6.6 %collective-permute-start.3 = (bf16[112,256]{1,0:T(8,128)(2,1)S(1)}, bf16[112,256]{1,0:T(8,128)(2,1)S(1)}, u32[]{:S(2)}, u32[]{:S(2)}) collective-permute-start(bf16[112,256]{1,0:T(8,128)(2,1)S(1)} %get-tuple-element.30), channel_id=1, source_target_pairs={{0,2},{1,3},{2,1},{3,0},{4,6},{5,7},{6,5},{7,4},{8,10},{9,11},{10,... | collective-permute-start | bytes 172040 | tf_op jit(solution)/shard_map/ppermute | solution.py:496
  10.9 5.8 %collective-permute-start.4 = (bf16[112,256]{1,0:T(8,128)(2,1)S(1)}, bf16[112,256]{1,0:T(8,128)(2,1)S(1)}, u32[]{:S(2)}, u32[]{:S(2)}) collective-permute-start(bf16[112,256]{1,0:T(8,128)(2,1)S(1)} %get-tuple-element.31), channel_id=1, source_target_pairs={{0,3},{1,2},{2,0},{3,1},{4,7},{5,6},{6,4},{7,5},{8,11},{9,10},{10,... | collective-permute-start | bytes 172040 | tf_op jit(solution)/shard_map/ppermute | solution.py:496
  12.0 5.2 %collective-permute-start.2 = (bf16[112,256]{1,0:T(8,128)(2,1)S(1)}, bf16[112,256]{1,0:T(8,128)(2,1)S(1)}, u32[]{:S(2)}, u32[]{:S(2)}) collective-permute-start(bf16[112,256]{1,0:T(8,128)(2,1)S(1)} %get-tuple-element.28), channel_id=1, source_target_pairs={{0,1},{1,0},{2,3},{3,2},{4,5},{5,4},{6,7},{7,6},{8,9},{9,8},{10,11... | collective-permute-start | bytes 172040 | tf_op jit(solution)/shard_map/ppermute | solution.py:496
  12.5 4.7 %copy-start.1 = (bf16[256,4096]{1,0:T(8,128)(2,1)S(1)}, bf16[256,4096]{1,0:T(8,128)(2,1)}, u32[]{:S(2)}) copy-start(bf16[256,4096]{1,0:T(8,128)(2,1)} %constant.17.clone.refs_4_) | copy-start | bytes 6291460

commit v8 on v7

--- a/solution.py
+++ b/solution.py
@@ -268,7 +268,7 @@
     level2[...] = (dot(level1[...], t2_ref[...]) * (1 / 1.5)).astype(BF16)
 
 
-def merge_kernel(plan, count, own_ref, a_ref, b_ref, merge_ref, right_ref, *out_refs):
+def merge_kernel(plan, count, own_ref, b_ref, a_ref, merge_ref, right_ref, *out_refs):
     even = lax.rem(lax.axis_index("gx"), 2) == 0
     a, b = a_ref[...], b_ref[...]
     before, after = jnp.where(even, b, a), jnp.where(even, a, b)
@@ -489,7 +489,7 @@
         message = ((plan.message, width), BF16)
         right, *messages = call(
             lambda *refs: merge_kernel(plan, along, *refs),
-            [own, recv_a, recv_b, const(plan.merge)],
+            [own, recv_b, recv_a, const(plan.merge)],
             [message] * (1 + len(steps)),
             name="merge",
         )

time: 19.7 us -> 19.5 us (0.990)
  waiting for transfers between devices: 2.04 us -> 1.47 us
  starting transfers between devices: 8.51 us -> 8.94 us
    ppermute x3, starting transfers between devices: 4.44 us -> 5.54 us  [on_device(): lax.ppermute(x, 'gy', list(enumerate(step)))]
    ppermute x2, starting transfers between devices: 4.08 us -> 3.4 us  [swap(): return lax.ppermute(x, 'gx', [(i, partner(i)) for i in range(across)])]
    ppermute x3, waiting for transfers between devices: 2.03 us -> 1.47 us  [on_device(): lax.ppermute(x, 'gy', list(enumerate(step)))]
  transfers between devices with their start and end apart: 5 -> 5, of which waited for: 1 -> 2; matrix products, arithmetic and copies ran while one was open for 0% -> 0% of each run, Pallas kernels for 23% -> 23%
where the time goes in v8:
time: 19.5 us; the launch traced here: 19.4 us
  starting transfers between devices  8.94 us (46%)
  Pallas kernels  8.77 us (45%)
  waiting for transfers between devices  1.47 us (8%)
    pallas_call x6, Pallas kernels, call(): pl.pallas_call(kernel, in_specs=specs, out_specs=out_specs, out_shape=out...  8.77 us
    ppermute x3, starting transfers between devices, on_device(): lax.ppermute(x, 'gy', list(enumerate(step)))  5.54 us
    ppermute x2, starting transfers between devices, swap(): return lax.ppermute(x, 'gx', [(i, partner(i)) for i in range(across)])  3.4 us
    ppermute x3, waiting for transfers between devices, on_device(): lax.ppermute(x, 'gy', list(enumerate(step)))  1.47 us
  transfers between devices with their start and end apart: 5, of which 2 were waited for; matrix products, arithmetic and copies ran while one was open for 0% of the time, Pallas kernels for 23%

profile of v8, /device:TPU:0, one launch (start us, length us, event | category | flops | bytes accessed | tf_op | source)
XLA Modules:
  0.0 19.4 jit_solution(16543614390941674125)
XLA Ops:
  0.0 1.8 %first.1 = (bf16[4,256,8,128]{3,2,1,0:T(8,128)(2,1)S(1)}, bf16[128,256]{1,0:T(8,128)(2,1)S(1)}, bf16[128,256]{1,0:T(8,128)(2,1)S(1)}, bf16[144,4096]{1,0:T(8,128...) custom-call(bf16[256,32,128]{2,1,0:T(8,128)(2,1)} %refs_0_.1), custom_call_target="tpu_custom_call" | custom-call | tf_op jit(solution)/shard_map/first/pallas_call | solution.py:430
  1.8 3.4 %collective-permute-start = (bf16[128,256]{1,0:T(8,128)(2,1)S(1)}, bf16[128,256]{1,0:T(8,128)(2,1)S(1)}, u32[]{:S(2)}, u32[]{:S(2)}) collective-permute-start(bf16[128,256]{1,0:T(8,128)(2,1)S(1)} %get-tuple-element.26.refs_7_), channel_id=1, source_target_pairs={{0,28},{4,8},{8,4},{12,16},{16,12},{20,24},{24,20},{28,0},{1,29},{... | collective-permute-start | bytes 196616 | tf_op jit(solution)/shard_map/ppermute | solution.py:449
  5.2 0.0 collective-permute-start.1
  5.2 0.0 copy-start.5
  5.2 0.0 copy-start
  5.2 0.0 copy-start.2
  5.2 0.0 copy-start.3
  5.2 0.0 copy-start.4
  5.3 0.0 copy-start.6
  5.3 0.0 copy-start.7
  5.3 1.9 %inner.1 = (bf16[256,4096]{1,0:T(8,128)(2,1)S(1)}, f32[144,256]{1,0:T(8,128)S(1)}, bf16[256,1024]{1,0:T(8,128)(2,1)S(1)}, bf16[256,256]{1,0:T(8,128)(2,1)S(1)}) custom-call(bf16[4,256,8,128]{3,2,1,0:T(8,128)(2,1)S(1)} %get-tuple-element.21.refs_0_, bf16[144,4096]{1,0:T(8,128)(2,1)S(1)} %get-tuple-element.22.refs_1_, ...), custom_call_target="tpu_custom_call" | custom-call | flops 452984832 | bytes 4194304 | tf_op jit(solution)/shard_map/inner/pallas_call | solution.py:430
  7.2 0.0 collective-permute-done.refs_1_.refs_9_
  7.2 0.0 collective-permute-done.1.refs_2_.refs_8_
  7.2 0.0 copy-done.5
  7.2 0.2 %merge.1 = (bf16[112,256]{1,0:T(8,128)(2,1)S(1)}, bf16[112,256]{1,0:T(8,128)(2,1)S(1)}, bf16[112,256]{1,0:T(8,128)(2,1)S(1)}, bf16[112,256]{1,0:T(8,128)(2,1)S(1)}) custom-call(f32[144,256]{1,0:T(8,128)S(1)} %get-tuple-element.25.refs_0_, bf16[128,256]{1,0:T(8,128)(2,1)S(1)} %collective-permute-done.refs_1_.refs_9_, ...), custom_call_target="tpu_custom_call" | custom-call | tf_op jit(solution)/shard_map/merge/pallas_call | solution.py:430
  7.4 4.0 %collective-permute-start.3 = (bf16[112,256]{1,0:T(8,128)(2,1)S(1)}, bf16[112,256]{1,0:T(8,128)(2,1)S(1)}, u32[]{:S(2)}, u32[]{:S(2)}) collective-permute-start(bf16[112,256]{1,0:T(8,128)(2,1)S(1)} %get-tuple-element.30), channel_id=1, source_target_pairs={{0,2},{1,3},{2,1},{3,0},{4,6},{5,7},{6,5},{7,4},{8,10},{9,11},{10,... | collective-permute-start | bytes 172040 | tf_op jit(solution)/shard_map/ppermute | solution.py:496
  11.3 1.1 %collective-permute-start.4 = (bf16[112,256]{1,0:T(8,128)(2,1)S(1)}, bf16[112,256]{1,0:T(8,128)(2,1)S(1)}, u32[]{:S(2)}, u32[]{:S(2)}) collective-permute-start(bf16[112,256]{1,0:T(8,128)(2,1)S(1)} %get-tuple-element.31), channel_id=1, source_target_pairs={{0,3},{1,2},{2,0},{3,1},{4,7},{5,6},{6,4},{7,5},{8,11},{9,10},{10,... | collective-permute-start | bytes 172040 | tf_op jit(solution)/shard_map/ppermute | solution.py:496
  12.4 0.5 %collective-permute-start.2 = (bf16[112,256]{1,0:T(8,128)(2,1)S(1)}, bf16[112,256]{1,0:T(8,128)(2,1)S(1)}, u32[]{:S(2)}, u32[]{:S(2)}) collective-permute-start(bf16[112,256]{1,0:T(8,128)(2,1)S(1)} %get-tuple-element.28), channel_id=1, source_target_pairs={{0,1},{1,0},{2,3},{3,2},{4,5},{5,4},{6,7},{7,6},{8,9},{9,8},{10,11... | collective-permute-start | bytes 172040 | tf_op jit(solution)/shard_map/ppermute | solution.py:496
  12.9 0.0 copy-done
  12.9 0.0 copy-done.2
  12.9 0.0 copy-done.3
  12.9 0.0 copy-done.4
  12.9 0.0 copy-done.6
  12.9 0.0 copy-done.7
  13.0 0.0 copy-start.1
  13.0 2.1 %local.1 = (f32[256,4096]{1,0:T(8,128)S(1)}, bf16[384,256]{1,0:T(8,128)(2,1)S(1)}) custom-call(bf16[256,4096]{1,0:T(8,128)(2,1)S(1)} %get-tuple-element.32.refs_0_, bf16[256,1024]{1,0:T(8,128)(2,1)S(1)} %get-tuple-element.33.refs_1_, bf16[256,256]{1,0:T(8,128)(2,1)S(1)} %get-tuple-element.34.refs_2_, bf16[1024,256]{1,0:T(8,128)(2,1)S(1)} %get-tuple-element.24.refs_3_, ...), custom_call_target="tpu_custom_call" | custom-call | flops 1073741824 | bytes 8388608 | tf_op jit(solution)/shard_map/local/pallas_call | solution.py:430
  15.1 0.0 collective-permute-done.3.refs_1_
  15.1 1.4 %collective-permute-done.4.refs_2_ = bf16[112,256]{1,0:T(8,128)(2,1)S(1)} collective-permute-done((bf16[112,256]{1,0:T(8,128)(2,1)S(1)}, bf16[112,256]{1,0:T(8,128)(2,1)S(1)}, u32[]{:S(2)}, u32[]{:S(2)}) %collective-permute-start.4) | collective-permute-done | bytes 57376 | tf_op jit(solution)/shard_map/ppermute | solution.py:496
  16.5 0.5 %gather.1.refs_1_ = f32[256,256]{1,0:T(8,128)S(1)} custom-call(bf16[112,256]{1,0:T(8,128)(2,1)S(1)} %get-tuple-element.29.refs_0_, bf16[112,256]{1,0:T(8,128)(2,1)S(1)} %collective-permute-done.3.refs_1_, bf16[112,256]{1,0:T(8,128)(2,1)S(1)} %collective-permute-done.4.refs_2_, bf16[4,256,256]{2,1,0:T(8,128)(2,1)S(1)} %copy-done, ...), custom_call_target="tpu_custom_call" | custom-call | tf_op jit(solution)/shard_map/gather/pallas_call | solution.py:430
  16.9 0.1 collective-permute-done.2.refs_0_
  17.0 0.0 copy-done.1
  17.0 2.3 %last.1 = bf16[256,32,128]{2,1,0:T(8,128)(2,1)} custom-call(bf16[112,256]{1,0:T(8,128)(2,1)S(1)} %collective-permute-done.2.refs_0_, f32[256,256]{1,0:T(8,128)S(1)} %gather.1.refs_1_, bf16[4,256,256]{2,1,0:T(8,128)(2,1)S(1)} %copy-done, bf16[384,256]{1,0:T(8,128)(2,1)S(1)} %get-tuple-element.35.refs_4_.refs_3_, bf16[256,4096]{1,0:T(8,128)(2,1)S(1)} %copy-done.1, ...), custom_call_target="tpu_custom_call" | custom-call | tf_op jit(solution)/shard_map/last/pallas_call | solution.py:430
Async XLA Ops:
  1.8 5.4 %collective-permute-start = (bf16[128,256]{1,0:T(8,128)(2,1)S(1)}, bf16[128,256]{1,0:T(8,128)(2,1)S(1)}, u32[]{:S(2)}, u32[]{:S(2)}) collective-permute-start(bf16[128,256]{1,0:T(8,128)(2,1)S(1)} %get-tuple-element.26.refs_7_), channel_id=1, source_target_pairs={{0,28},{4,8},{8,4},{12,16},{16,12},{20,24},{24,20},{28,0},{1,29},{... | collective-permute-start | bytes 196616 | tf_op jit(solution)/shard_map/ppermute | solution.py:449
  5.2 2.0 %collective-permute-start.1 = (bf16[128,256]{1,0:T(8,128)(2,1)S(1)}, bf16[128,256]{1,0:T(8,128)(2,1)S(1)}, u32[]{:S(2)}, u32[]{:S(2)}) collective-permute-start(bf16[128,256]{1,0:T(8,128)(2,1)S(1)} %get-tuple-element.27.refs_6_), channel_id=1, source_target_pairs={{0,4},{4,0},{8,12},{12,8},{16,20},{20,16},{24,28},{28,24},{1,5},{5... | collective-permute-start | bytes 196616 | tf_op jit(solution)/shard_map/ppermute | solution.py:449
  5.2 2.0 %copy-start.5 = (bf16[144,256]{1,0:T(8,128)(2,1)S(1)}, bf16[144,256]{1,0:T(8,128)(2,1)}, u32[]{:S(2)}) copy-start(bf16[144,256]{1,0:T(8,128)(2,1)} %constant.12.clone.refs_3_) | copy-start | bytes 221188
  5.2 7.7 %copy-start = (bf16[4,256,256]{2,1,0:T(8,128)(2,1)S(1)}, bf16[4,256,256]{2,1,0:T(8,128)(2,1)}, u32[]{:S(2)}) copy-start(bf16[4,256,256]{2,1,0:T(8,128)(2,1)} %refs_2_.1) | copy-start | bytes 1572868
  5.2 7.7 %copy-start.2 = (bf16[256,512]{1,0:T(8,128)(2,1)S(1)}, bf16[256,512]{1,0:T(8,128)(2,1)}, u32[]{:S(2)}) copy-start(bf16[256,512]{1,0:T(8,128)(2,1)} %constant.15.clone.refs_12_) | copy-start | bytes 786436
  5.2 7.7 %copy-start.3 = (bf16[256,512]{1,0:T(8,128)(2,1)S(1)}, bf16[256,512]{1,0:T(8,128)(2,1)}, u32[]{:S(2)}) copy-start(bf16[256,512]{1,0:T(8,128)(2,1)} %constant.16.clone.refs_13_) | copy-start | bytes 786436
  5.2 7.7 %copy-start.4 = (bf16[256,256]{1,0:T(8,128)(2,1)S(1)}, bf16[256,256]{1,0:T(8,128)(2,1)}, u32[]{:S(2)}) copy-start(bf16[256,256]{1,0:T(8,128)(2,1)} %constant.14.clone.refs_11_) | copy-start | bytes 393220
  5.3 7.7 %copy-start.6 = (bf16[128,256]{1,0:T(8,128)(2,1)S(1)}, bf16[128,256]{1,0:T(8,128)(2,1)}, u32[]{:S(2)}) copy-start(bf16[128,256]{1,0:T(8,128)(2,1)} %constant.13.clone.refs_10_) | copy-start | bytes 196612
  5.3 7.7 %copy-start.7 = (bf16[64,64]{1,0:T(8,128)(2,1)S(1)}, bf16[64,64]{1,0:T(8,128)(2,1)}, u32[]{:S(2)}) copy-start(bf16[64,64]{1,0:T(8,128)(2,1)} %refs_5_.1) | copy-start | bytes 24580
  7.4 7.7 %collective-permute-start.3 = (bf16[112,256]{1,0:T(8,128)(2,1)S(1)}, bf16[112,256]{1,0:T(8,128)(2,1)S(1)}, u32[]{:S(2)}, u32[]{:S(2)}) collective-permute-start(bf16[112,256]{1,0:T(8,128)(2,1)S(1)} %get-tuple-element.30), channel_id=1, source_target_pairs={{0,2},{1,3},{2,1},{3,0},{4,6},{5,7},{6,5},{7,4},{8,10},{9,11},{10,... | collective-permute-start | bytes 172040 | tf_op jit(solution)/shard_map/ppermute | solution.py:496
  11.3 5.1 %collective-permute-start.4 = (bf16[112,256]{1,0:T(8,128)(2,1)S(1)}, bf16[112,256]{1,0:T(8,128)(2,1)S(1)}, u32[]{:S(2)}, u32[]{:S(2)}) collective-permute-start(bf16[112,256]{1,0:T(8,128)(2,1)S(1)} %get-tuple-element.31), channel_id=1, source_target_pairs={{0,3},{1,2},{2,0},{3,1},{4,7},{5,6},{6,4},{7,5},{8,11},{9,10},{10,... | collective-permute-start | bytes 172040 | tf_op jit(solution)/shard_map/ppermute | solution.py:496
  12.4 4.6 %collective-permute-start.2 = (bf16[112,256]{1,0:T(8,128)(2,1)S(1)}, bf16[112,256]{1,0:T(8,128)(2,1)S(1)}, u32[]{:S(2)}, u32[]{:S(2)}) collective-permute-start(bf16[112,256]{1,0:T(8,128)(2,1)S(1)} %get-tuple-element.28), channel_id=1, source_target_pairs={{0,1},{1,0},{2,3},{3,2},{4,5},{5,4},{6,7},{7,6},{8,9},{9,8},{10,11... | collective-permute-start | bytes 172040 | tf_op jit(solution)/shard_map/ppermute | solution.py:496
  13.0 4.1 %copy-start.1 = (bf16[256,4096]{1,0:T(8,128)(2,1)S(1)}, bf16[256,4096]{1,0:T(8,128)(2,1)}, u32[]{:S(2)}) copy-start(bf16[256,4096]{1,0:T(8,128)(2,1)} %constant.17.clone.refs_4_) | copy-start | bytes 6291460
